TPU v7x, 32 devices: a whole 2x2x4 slice. The times are simulated.
32 devices in a mesh: groups: 1, expert: 16 (over z, y, x), sub: 2 (over core).
Axes of the slice: x: 2, y: 2, z: 4, core: 2. Of those that a mesh axis runs over, the one named last changes fastest.
Arguments:
- tokens: bfloat16 [1024, 3584], P(('groups', 'expert', 'sub')), may hold values from -6 to 6
- gate_weight: bfloat16 [16, 3584, 1024], P('expert', None, 'sub'), may hold values from -0.09375 to 0.09375
- up_weight: bfloat16 [16, 3584, 1024], P('expert', None, 'sub'), may hold values from -0.09375 to 0.09375
- down_weight: bfloat16 [16, 1024, 3584], P('expert', 'sub'), may hold values from -0.1875 to 0.1875
- expert_ids: int32 [1024, 8], P(('groups', 'expert', 'sub')), may hold values from 0 to 15, all different within a row; in each aligned block of 32 rows (0 to 31, 32 to 63, ...) at most 32 rows name the same one
- gate_fixed: int32 [1024, 8], P(('groups', 'expert', 'sub')), may hold values from 1 to 65535
Outputs:
- mixed_out: bfloat16 [1024, 3584], P(('groups', 'expert', 'sub'))
Inputs may be any that keep to these rules, and one draw needn't show every extreme that they name: `expert_ids`: each row names 8 different experts; among the 32 rows of one device no expert is named more than 32 times, a bound that some block reaches.
All inputs are finite; a program needn't handle non-finite values.
Results may differ from a plain program's by a relative error of at most 0.0058.
Values may be sent and summed in bfloat16 or wider, within the bound.
No kernel may reach another device: no remote copies, remote signals or barrier semaphores. Data moves between devices by JAX's collectives and lax.ppermute only.
A program may use at most 128 MiB of HBM per device.

v0:
```python
import jax
import jax.numpy as jnp
from jax import lax
from jax.sharding import PartitionSpec as P


def slot_numbers(expert_ids, experts, capacity):
    flat_ids = expert_ids.reshape(-1)
    onehot = (flat_ids[:, None] == jnp.arange(experts, dtype=jnp.int32)[None, :]).astype(jnp.int32)
    ordinal = jnp.sum(jnp.cumsum(onehot, axis=0) * onehot, axis=1) - 1
    return (flat_ids * capacity + ordinal).reshape(expert_ids.shape)


def whole_expert(arrived, full_gate, full_up, full_down):
    feature_count = arrived.shape[-1]
    row_block = arrived.reshape(-1, feature_count)
    gate_proj = jnp.dot(row_block, full_gate[0], preferred_element_type=jnp.float32)
    up_proj = jnp.dot(row_block, full_up[0], preferred_element_type=jnp.float32)
    hidden = (jax.nn.silu(gate_proj) * up_proj).astype(jnp.bfloat16)
    result = jnp.dot(hidden, full_down[0], preferred_element_type=jnp.float32)
    return result.reshape(arrived.shape).astype(jnp.bfloat16)


def per_device(tokens, gate_weight, up_weight, down_weight, expert_ids, gate_fixed):
    experts = lax.axis_size("expert")
    tok_rows, top_count = expert_ids.shape
    capacity = min(tok_rows, max(2, 2 * tok_rows * top_count // experts))
    feature_count = tokens.shape[1]
    full_gate, full_up, full_down = (
        lax.all_gather(gate_weight, "sub", axis=2, tiled=True),
        lax.all_gather(up_weight, "sub", axis=2, tiled=True),
        lax.all_gather(down_weight, "sub", axis=1, tiled=True),
    )
    slot_ids = slot_numbers(expert_ids, experts, capacity)
    slot_axis = jnp.arange(experts * capacity, dtype=jnp.int32)
    slot_match = slot_axis[:, None, None] == slot_ids[None, :, :]
    placing = jnp.any(slot_match, axis=2).astype(jnp.bfloat16)
    outgoing = jnp.dot(placing, tokens, preferred_element_type=jnp.float32).astype(jnp.bfloat16)
    outgoing = outgoing.reshape(experts, capacity, feature_count)
    returned_rows = lax.all_to_all(
        whole_expert(
            lax.all_to_all(outgoing, "expert", split_axis=0, concat_axis=0, tiled=True),
            full_gate,
            full_up,
            full_down,
        ),
        "expert",
        split_axis=0,
        concat_axis=0,
        tiled=True,
    )
    fixed_point = gate_fixed.astype(jnp.float32)
    route_share = fixed_point / jnp.sum(fixed_point, axis=1, keepdims=True)
    combine = jnp.sum(jnp.where(slot_match, route_share[None, :, :], 0.0), axis=2).T
    mixed_out = jnp.dot(
        combine,
        returned_rows.reshape(-1, feature_count).astype(jnp.float32),
        precision=lax.Precision.HIGHEST,
    )
    return mixed_out.astype(jnp.bfloat16)


def solution(mesh):
    in_specs = (
        P(("groups", "expert", "sub"), None),
        P("expert", None, "sub"),
        P("expert", None, "sub"),
        P("expert", "sub", None),
        P(("groups", "expert", "sub"), None),
        P(("groups", "expert", "sub"), None),
    )
    out_specs = P(("groups", "expert", "sub"), None)
    return jax.shard_map(
        per_device, mesh=mesh, in_specs=in_specs, out_specs=out_specs, check_vma=False
    )
```

profile of v0, /device:TPU:14, one launch (start us, length us, event | category | flops | bytes accessed | tf_op | source)
XLA Modules:
  0.0 224.0 jit_solution(17169228251221409762)
XLA Ops:
  6.5 0.0 copy-start
  6.5 0.0 copy-start.2
  6.5 0.0 all-gather.6.cloned.1.call-start
  6.5 0.7 all-gather.6.cloned.1.call-update
  7.3 0.0 all-gather.4.cloned.1.call-start
  7.3 0.7 all-gather.4.cloned.1.call-update
  8.0 0.0 copy-done.2
  8.0 0.1 copy.14
  8.1 0.1 eq.43
  8.2 0.1 eq.39
  8.3 0.6 reduce-window.6
  8.9 0.2 slice_reduce_fusion
  9.1 0.1 fusion.13
  9.2 0.1 sub.7
  9.3 0.2 fusion.11
  9.6 0.0 copy-done
  9.6 2.9 %convolution_convert_fusion = bf16[512,3584]{1,0:T(8,128)(2,1)} fusion(pred[512,32]{0,1:T(8,128)(4,1)S(1)} %fusion.11, bf16[32,3584]{1,0:T(8,128)(2,1)S(1)} %copy-done), kind=kOutput, calls=%fused_computation.7 | convolution fusion | flops 119275520 | bytes 3915776 | tf_op jit(solution)/shard_map/dot_general | solution.py:38
  12.5 7.1 %all-to-all-start = ((bf16[16,32,3584]{2,1,0:T(8,128)(2,1)}), bf16[16,32,3584]{2,1,0:T(8,128)(2,1)}, u32[]{:S(2)}, u32[]{:S(2)}) async-start(bf16[16,32,3584]{2,1,0:T(8,128)(2,1)} %bitcast.40), calls=%async_computation | async-start | bytes 7340032 | tf_op jit(solution)/shard_map/all_to_all | solution.py:42
  19.6 0.0 all-gather.8.cloned.1.call-start
  19.7 0.7 all-gather.8.cloned.1.call-update
  20.4 81.9 %all-to-all-done = bf16[16,32,3584]{2,1,0:T(8,128)(2,1)} async-done(((bf16[16,32,3584]{2,1,0:T(8,128)(2,1)}), bf16[16,32,3584]{2,1,0:T(8,128)(2,1)}, u32[]{:S(2)}, u32[]{:S(2)}) %all-to-all-start) | async-done | bytes 3670048 | tf_op jit(solution)/shard_map/all_to_all | solution.py:42
  102.2 0.0 all-gather.6.cloned.1.call-done
  102.2 7.3 %fusion.2 = f32[512,1024]{1,0:T(8,128)S(1)} fusion(bf16[512,3584]{1,0:T(8,128)(2,1)} %bitcast.2, bf16[1,3584,1024]{2,1,0:T(8,128)(2,1)} %all-gather.6.cloned.1.call-done), kind=kOutput, calls=%fused_computation.2 | convolution fusion | flops 3758096384 | bytes 13107200 | tf_op jit(solution)/shard_map/dot_general | solution.py:18
  109.5 0.0 all-gather.4.cloned.1.call-done
  109.6 8.4 %multiply_convert_fusion = bf16[512,1024]{1,0:T(8,128)(2,1)S(1)} fusion(f32[512,1024]{1,0:T(8,128)S(1)} %fusion.2, bf16[512,3584]{1,0:T(8,128)(2,1)} %bitcast.2, bf16[1,3584,1024]{2,1,0:T(8,128)(2,1)} %all-gather.4.cloned.1.call-done), kind=kOutput, calls=%fused_computation.9 | convolution fusion | flops 3761242112 | bytes 14155776 | tf_op jit(solution)/shard_map/dot_general | solution.py:17
  118.0 0.0 all-gather.8.cloned.1.call-done
  118.0 8.5 %fusion.6 = bf16[16,32,3584]{2,1,0:T(8,128)(2,1)} fusion(bf16[16,32,1024]{2,1,0:T(8,128)(2,1)S(1)} %bitcast.41, bf16[1,1024,3584]{2,1,0:T(8,128)(2,1)} %all-gather.8.cloned.1.call-done), kind=kOutput, calls=%fused_computation.6 | convolution fusion | flops 3759931392 | bytes 12058624 | tf_op jit(solution)/shard_map/dot_general | solution.py:20
  126.5 0.0 copy-start.1
  126.5 5.2 %all-to-all-start.1 = ((bf16[16,32,3584]{2,1,0:T(8,128)(2,1)}), bf16[16,32,3584]{2,1,0:T(8,128)(2,1)}, u32[]{:S(2)}, u32[]{:S(2)}) async-start(bf16[16,32,3584]{2,1,0:T(8,128)(2,1)} %fusion.6), calls=%async_computation.1 | async-start | bytes 7340032 | tf_op jit(solution)/shard_map/all_to_all | solution.py:40
  131.8 0.0 copy-done.1
  131.8 0.1 copy.18
  131.9 0.2 select_reduce_fusion
  132.1 80.8 %all-to-all-done.1 = bf16[16,32,3584]{2,1,0:T(8,128)(2,1)} async-done(((bf16[16,32,3584]{2,1,0:T(8,128)(2,1)}), bf16[16,32,3584]{2,1,0:T(8,128)(2,1)}, u32[]{:S(2)}, u32[]{:S(2)}) %all-to-all-start.1) | async-done | bytes 3670048 | tf_op jit(solution)/shard_map/all_to_all | solution.py:40
  212.9 4.6 %convolution_convert_fusion.1 = bf16[32,3584]{1,0:T(8,128)(2,1)} fusion(f32[512,32]{0,1:T(8,128)S(1)} %select_reduce_fusion, bf16[512,3584]{1,0:T(8,128)(2,1)} %bitcast.8), kind=kOutput, calls=%fused_computation.8 | convolution fusion | flops 704757760 | bytes 3964928 | tf_op jit(solution)/shard_map/dot_general | solution.py:55
  (7 shorter events, 0.1 us)
Async XLA Ops:
  6.5 3.0 %copy-start = (bf16[32,3584]{1,0:T(8,128)(2,1)S(1)}, bf16[32,3584]{1,0:T(8,128)(2,1)}, u32[]{:S(2)}) copy-start(bf16[32,3584]{1,0:T(8,128)(2,1)} %param.6) | copy-start | bytes 688132
  6.5 1.5 copy-start.2
  6.5 95.7 %all-gather.6.cloned.1.call-start = ((), (), s32[]{:S(2)}) async-start(), calls=%async_computation.3 | async-start | bytes 11010048 | tf_op jit(solution)/shard_map/all_gather | solution.py:31
  7.3 102.3 %all-gather.4.cloned.1.call-start = ((), (), s32[]{:S(2)}) async-start(), calls=%async_computation.2 | async-start | bytes 11010048 | tf_op jit(solution)/shard_map/all_gather | solution.py:30
  12.5 89.7 %all-to-all-start = ((bf16[16,32,3584]{2,1,0:T(8,128)(2,1)}), bf16[16,32,3584]{2,1,0:T(8,128)(2,1)}, u32[]{:S(2)}, u32[]{:S(2)}) async-start(bf16[16,32,3584]{2,1,0:T(8,128)(2,1)} %bitcast.40), calls=%async_computation | async-start | bytes 7340032 | tf_op jit(solution)/shard_map/all_to_all | solution.py:42
  19.6 98.4 %all-gather.8.cloned.1.call-start = ((), (), s32[]{:S(2)}) async-start(), calls=%async_computation.4 | async-start | bytes 11010048 | tf_op jit(solution)/shard_map/all_gather | solution.py:32
  126.5 5.3 %copy-start.1 = (s32[32,8]{0,1:T(8,128)S(1)}, s32[32,8]{0,1:T(8,128)}, u32[]{:S(2)}) copy-start(s32[32,8]{0,1:T(8,128)} %param.11) | copy-start | bytes 3076
  126.5 86.3 %all-to-all-start.1 = ((bf16[16,32,3584]{2,1,0:T(8,128)(2,1)}), bf16[16,32,3584]{2,1,0:T(8,128)(2,1)}, u32[]{:S(2)}, u32[]{:S(2)}) async-start(bf16[16,32,3584]{2,1,0:T(8,128)(2,1)} %fusion.6), calls=%async_computation.1 | async-start | bytes 7340032 | tf_op jit(solution)/shard_map/all_to_all | solution.py:40
Sparse Core Ops, SparseCore 0:
  8.9 19.6 all-gather.5
  30.2 19.4 all-gather.3
  51.2 19.4 all-gather.7
where the time goes:
time: 224 us
  waiting for transfers between devices  165 us (74%)
  matrix products  31.8 us (14%)
  between operations  13.2 us (6%)
  starting transfers between devices  12.5 us (6%)
    all_to_all x1, waiting for transfers between devices, per_device(): lax.all_to_all(outgoing, 'expert', split_axis=0, concat_axis=0, tiled=True)  81.9 us
    all_to_all x1, waiting for transfers between devices, per_device(): lax.all_to_all(whole_expert(lax.all_to_all(outgoing, 'expert', split_axis...  80.8 us
    dot_general x1, matrix products, whole_expert(): result = jnp.dot(hidden, full_down[0], preferred_element_type=jnp.float32)  8.5 us
    dot_general x1, matrix products, whole_expert(): jnp.dot(row_block, full_gate[0], preferred_element_type=jnp.float32)  8.4 us
    dot_general x1, matrix products, whole_expert(): up_proj = jnp.dot(row_block, full_up[0], preferred_element_type=jnp.float32)  7.3 us
    all_to_all x1, starting transfers between devices, per_device(): lax.all_to_all(outgoing, 'expert', split_axis=0, concat_axis=0, tiled=True)  7.14 us
    all_to_all x1, starting transfers between devices, per_device(): lax.all_to_all(whole_expert(lax.all_to_all(outgoing, 'expert', split_axis...  5.25 us
    dot_general x1, matrix products, per_device(): jnp.dot(combine, returned_rows.reshape(-1, feature_count).astype(jnp.floa...  4.61 us
  transfers between devices with their start and end apart: 5, of which 2 were waited for; matrix products, arithmetic and copies ran while one was open for 9% of the time, Pallas kernels for 0%

commit v1 on v0

v1 whole, which is shorter than its diff:
```python
import jax
import jax.numpy as jnp
from jax import lax
from jax.sharding import PartitionSpec as P

LANES = 128
DEPTH_TILE = 256


def plan(experts, feature_count):
    bits = experts.bit_length() - 1
    if experts == 16:
        orders = ((3, 2, 0, 1), (0, 3, 2, 1), (3, 2, 1, 0), (1, 3, 2, 0))
        mirror = (1, 0, 2, 3)
    else:
        orders = tuple(tuple((turn + step) % bits for step in range(bits)) for turn in range(0, bits, max(1, bits // 4)))[:4]
        half = bits // 2
        mirror = tuple((bit + half) % bits if bits % 2 == 0 else bit for bit in range(bits))
    tiles = feature_count // DEPTH_TILE
    count = len(orders)
    widths = [DEPTH_TILE * (tiles // count + (1 if i < tiles % count else 0)) for i in range(count)]
    widths[-1] += feature_count - sum(widths)
    return orders, mirror, widths


def cross(block, bit, experts, mirror):
    pairs = []
    for chip in range(experts):
        for core, flipped in ((0, bit), (1, mirror[bit])):
            pairs.append((chip * 2 + core, (chip ^ (1 << flipped)) * 2 + core))
    return lax.ppermute(block, ("expert", "sub"), pairs)


def other_core(block):
    return lax.ppermute(block, "sub", [(0, 1), (1, 0)])


def per_device(tokens, gate_weight, up_weight, down_weight, expert_ids, gate_fixed):
    experts = lax.axis_size("expert")
    bits = experts.bit_length() - 1
    tok_rows, top_count = expert_ids.shape
    feature_count = tokens.shape[1]
    orders, mirror, widths = plan(experts, feature_count)
    starts = [sum(widths[:i]) for i in range(len(widths))]
    rows = experts * tok_rows

    fixed_point = gate_fixed.astype(jnp.float32)
    route_share = fixed_point / jnp.sum(fixed_point, axis=1, keepdims=True)
    chosen = expert_ids[:, :, None] == jnp.arange(experts, dtype=jnp.int32)[None, None, :]
    dense_share = jnp.sum(jnp.where(chosen, route_share[:, :, None], 0.0), axis=1)
    high = lax.reduce_precision(dense_share, 8, 7)
    low = dense_share - high
    shares = jnp.concatenate([high, low], axis=1)
    shares = jnp.pad(shares, ((0, 0), (0, -2 * experts % LANES))).astype(jnp.bfloat16)

    own = [w[0] for w in (gate_weight, up_weight, down_weight)]
    far = [other_core(w) for w in own]

    held = []
    for start, width in zip(starts, widths):
        piece = tokens[:, start : start + width]
        if start == 0:
            piece = jnp.concatenate([piece, shares], axis=1)
        held.append(piece.reshape((1,) * bits + piece.shape))
    for step in range(bits):
        for i, order in enumerate(orders):
            held[i] = jnp.concatenate([held[i], cross(held[i], order[step], experts, mirror)], axis=order[step])
    held = [piece.reshape(rows, -1) for piece in held]

    mine = lax.axis_index("expert")
    lane = jnp.arange(shares.shape[1], dtype=jnp.int32)
    picked = (lane == mine) | (lane == mine + experts)
    weight = jnp.sum(jnp.where(picked[None, :], held[0][:, widths[0] :].astype(jnp.float32), 0.0), axis=1, keepdims=True)
    held[0] = held[0][:, : widths[0]]
    x = jnp.concatenate(held, axis=1)

    hidden = []
    for w in (own, far):
        gate_proj = jnp.dot(x, w[0], preferred_element_type=jnp.float32)
        up_proj = jnp.dot(x, w[1], preferred_element_type=jnp.float32)
        hidden.append((jax.nn.silu(gate_proj) * up_proj).astype(jnp.bfloat16))

    sums = []
    for start, width in zip(starts, widths):
        part = sum(jnp.dot(h, w[2][:, start : start + width], preferred_element_type=jnp.float32) for h, w in zip(hidden, (own, far)))
        sums.append((part * weight).astype(jnp.bfloat16).reshape((2,) * bits + (tok_rows, width)))
    for step in reversed(range(bits)):
        for i, order in enumerate(orders):
            axis = order[step]
            keep = lax.slice_in_dim(sums[i], 0, 1, axis=axis)
            arrived = cross(lax.slice_in_dim(sums[i], 1, 2, axis=axis), axis, experts, mirror)
            sums[i] = (keep.astype(jnp.float32) + arrived.astype(jnp.float32)).astype(jnp.bfloat16)
    return jnp.concatenate([part.reshape(tok_rows, -1) for part in sums], axis=1)


def solution(mesh):
    in_specs = (
        P(("groups", "expert", "sub"), None),
        P("expert", None, "sub"),
        P("expert", None, "sub"),
        P("expert", "sub", None),
        P(("groups", "expert", "sub"), None),
        P(("groups", "expert", "sub"), None),
    )
    out_specs = P(("groups", "expert", "sub"), None)
    return jax.shard_map(
        per_device, mesh=mesh, in_specs=in_specs, out_specs=out_specs, check_vma=False
    )
```

time: 224 us -> 132 us (0.59)
  the two profiles are of different devices: /device:TPU:14 before, /device:TPU:0 now
where the time goes in v1:
time: 132 us; the launch traced here: 131 us
  waiting for transfers between devices  56.7 us (43%)
  starting transfers between devices  44.3 us (34%)
  matrix products  18.3 us (14%)
  other arithmetic  9.35 us (7%)
  local copies, waits for them, and re-layouts  2.25 us (2%)
    ppermute x32, waiting for transfers between devices, cross(): return lax.ppermute(block, ('expert', 'sub'), pairs)  56.7 us
    ppermute x32, starting transfers between devices, cross(): return lax.ppermute(block, ('expert', 'sub'), pairs)  43.8 us
    dot_general x2, matrix products, per_device(): gate_proj = jnp.dot(x, w[0], preferred_element_type=jnp.float32)  8.34 us
    concatenate x16, other arithmetic, per_device(): jnp.concatenate([held[i], cross(held[i], order[step], experts, mirror)],...  5.39 us
    dot_general x8, matrix products, per_device(): jnp.dot(h, w[2][:, start:start + width], preferred_element_type=jnp.float32)  5.19 us
    dot_general x2, matrix products, per_device(): up_proj = jnp.dot(x, w[1], preferred_element_type=jnp.float32)  4.74 us
  transfers between devices with their start and end apart: 35, of which 17 were waited for; matrix products, arithmetic and copies ran while one was open for 21% of the time, Pallas kernels for 0%

profile of v1, /device:TPU:0, one launch (start us, length us, event | category | flops | bytes accessed | tf_op | source)
XLA Modules:
  0.0 131.4 jit_solution(16469177946695532680)
XLA Ops:
  0.0 0.8 slice_bitcast_fusion.2
  0.8 4.1 %collective-permute-start.8 = (bf16[1,1,1,1,32,768]{5,4,3,2,1,0:T(8,128)(2,1)S(1)}, bf16[1,1,1,1,32,768]{5,4,3,2,1,0:T(8,128)(2,1)S(1)}, u32[]{:S(2)}, u32[]{:S(2)}) collective-permute-start(bf16[1,1,1,1,32,768]{5,4,3,2,1,0:T(8,128)(2,1)S(1)} %get-tuple-element.11), channel_id=1, source_target_pairs={{0,16},{1,17},{2,18},{3,19},{4,20},{5,21},{6,22},{7,23},{8,24},{9,... | collective-permute-start | bytes 147464 | tf_op jit(solution)/shard_map/ppermute | solution.py:31
  4.9 0.9 fusion.30
  5.8 0.7 convert_reduce_fusion
  6.5 0.7 convert_divide_fusion
  7.2 0.7 select_reduce_fusion.1
  8.1 1.8 %collective-permute-start.4 = (bf16[1,1,1,1,32,1024]{5,4,3,2,1,0:T(8,128)(2,1)S(1)}, bf16[1,1,1,1,32,1024]{5,4,3,2,1,0:T(8,128)(2,1)S(1)}, u32[]{:S(2)}, u32[]{:S(2)}) collective-permute-start(bf16[1,1,1,1,32,1024]{5,4,3,2,1,0:T(8,128)(2,1)S(1)} %get-tuple-element.10), channel_id=1, source_target_pairs={{0,2},{1,5},{2,0},{3,7},{4,6},{5,1},{6,4},{7,3},{8,10},{9,13},{10,... | collective-permute-start | bytes 196616 | tf_op jit(solution)/shard_map/ppermute | solution.py:31
  9.9 1.5 %collective-permute-start.12 = (bf16[1,1,1,1,32,768]{5,4,3,2,1,0:T(8,128)(2,1)S(1)}, bf16[1,1,1,1,32,768]{5,4,3,2,1,0:T(8,128)(2,1)S(1)}, u32[]{:S(2)}, u32[]{:S(2)}) collective-permute-start(bf16[1,1,1,1,32,768]{5,4,3,2,1,0:T(8,128)(2,1)S(1)} %get-tuple-element.12), channel_id=1, source_target_pairs={{0,4},{1,3},{2,6},{3,1},{4,0},{5,7},{6,2},{7,5},{8,12},{9,11},{10,... | collective-permute-start | bytes 147464 | tf_op jit(solution)/shard_map/ppermute | solution.py:31
  11.5 1.6 %collective-permute-start.9 = (bf16[1,1,1,2,32,768]{5,4,3,2,1,0:T(8,128)(2,1)S(1)}, bf16[1,1,1,2,32,768]{5,4,3,2,1,0:T(8,128)(2,1)S(1)}, u32[]{:S(2)}, u32[]{:S(2)}) collective-permute-start(bf16[1,1,1,2,32,768]{5,4,3,2,1,0:T(8,128)(2,1)S(1)} %pad_maximum_fusion.16), channel_id=1, source_target_pairs={{0,8},{1,9},{2,10},{3,11},{4,12},{5,13},{6,14},{7,15},{8,0},{9,1},... | collective-permute-start | bytes 294920 | tf_op jit(solution)/shard_map/ppermute | solution.py:31
  13.1 0.9 collective-permute-done.12
  14.0 2.7 %collective-permute-start.13 = (bf16[1,2,1,1,32,768]{5,4,3,2,1,0:T(8,128)(2,1)S(1)}, bf16[1,2,1,1,32,768]{5,4,3,2,1,0:T(8,128)(2,1)S(1)}, u32[]{:S(2)}, u32[]{:S(2)}) collective-permute-start(bf16[1,2,1,1,32,768]{5,4,3,2,1,0:T(8,128)(2,1)S(1)} %pad_maximum_fusion.17), channel_id=1, source_target_pairs={{0,16},{1,17},{2,18},{3,19},{4,20},{5,21},{6,22},{7,23},{8,24},{9,... | collective-permute-start | bytes 294920 | tf_op jit(solution)/shard_map/ppermute | solution.py:31
  17.1 1.6 %collective-permute-start.1 = (bf16[1,1,1,2,32,1152]{5,4,3,2,1,0:T(8,128)(2,1)S(1)}, bf16[1,1,1,2,32,1152]{5,4,3,2,1,0:T(8,128)(2,1)S(1)}, u32[]{:S(2)}, u32[]{:S(2)}) collective-permute-start(bf16[1,1,1,2,32,1152]{5,4,3,2,1,0:T(8,128)(2,1)S(1)} %pad_maximum_fusion.14), channel_id=1, source_target_pairs={{0,8},{1,9},{2,10},{3,11},{4,12},{5,13},{6,14},{7,15},{8,0},{9,1},... | collective-permute-start | bytes 442376 | tf_op jit(solution)/shard_map/ppermute | solution.py:31
  18.8 1.6 %collective-permute-start.10 = (bf16[1,1,2,2,32,768]{5,4,3,2,1,0:T(8,128)(2,1)S(1)}, bf16[1,1,2,2,32,768]{5,4,3,2,1,0:T(8,128)(2,1)S(1)}, u32[]{:S(2)}, u32[]{:S(2)}) collective-permute-start(bf16[1,1,2,2,32,768]{5,4,3,2,1,0:T(8,128)(2,1)S(1)} %pad_maximum_fusion.12), channel_id=1, source_target_pairs={{0,4},{1,3},{2,6},{3,1},{4,0},{5,7},{6,2},{7,5},{8,12},{9,11},{10,... | collective-permute-start | bytes 589832 | tf_op jit(solution)/shard_map/ppermute | solution.py:31
  20.4 3.9 %collective-permute-done.13 = bf16[1,2,1,1,32,768]{5,4,3,2,1,0:T(8,128)(2,1)S(1)} collective-permute-done((bf16[1,2,1,1,32,768]{5,4,3,2,1,0:T(8,128)(2,1)S(1)}, bf16[1,2,1,1,32,768]{5,4,3,2,1,0:T(8,128)(2,1)S(1)}, u32[]{:S(2)}, u32[]{:S(2)}) %collective-permute-start.13) | collective-permute-done | bytes 98336 | tf_op jit(solution)/shard_map/ppermute | solution.py:31
  24.4 2.0 %collective-permute-done.5 = bf16[2,1,1,1,32,1024]{5,4,3,2,1,0:T(8,128)(2,1)S(1)} collective-permute-done((bf16[2,1,1,1,32,1024]{5,4,3,2,1,0:T(8,128)(2,1)S(1)}, bf16[2,1,1,1,32,1024]{5,4,3,2,1,0:T(8,128)(2,1)S(1)}, u32[]{:S(2)}, u32[]{:S(2)}) %collective-permute-start.5) | collective-permute-done | bytes 131104 | tf_op jit(solution)/shard_map/ppermute | solution.py:31
  26.6 1.5 %collective-permute-start.2 = (bf16[1,1,2,2,32,1152]{5,4,3,2,1,0:T(8,128)(2,1)S(1)}, bf16[1,1,2,2,32,1152]{5,4,3,2,1,0:T(8,128)(2,1)S(1)}, u32[]{:S(2)}, u32[]{:S(2)}) collective-permute-start(bf16[1,1,2,2,32,1152]{5,4,3,2,1,0:T(8,128)(2,1)S(1)} %pad_maximum_fusion.9), channel_id=1, source_target_pairs={{0,2},{1,5},{2,0},{3,7},{4,6},{5,1},{6,4},{7,3},{8,10},{9,13},{10,... | collective-permute-start | bytes 884744 | tf_op jit(solution)/shard_map/ppermute | solution.py:31
  28.2 0.8 pad_maximum_fusion.7
  29.0 0.6 collective-permute-start.11
  29.5 2.6 %collective-permute-done.14 = bf16[1,2,1,2,32,768]{5,4,3,2,1,0:T(8,128)(2,1)S(1)} collective-permute-done((bf16[1,2,1,2,32,768]{5,4,3,2,1,0:T(8,128)(2,1)S(1)}, bf16[1,2,1,2,32,768]{5,4,3,2,1,0:T(8,128)(2,1)S(1)}, u32[]{:S(2)}, u32[]{:S(2)}) %collective-permute-start.14) | collective-permute-done | bytes 196640 | tf_op jit(solution)/shard_map/ppermute | solution.py:31
  32.2 1.3 collective-permute-start.15
  33.5 2.2 %collective-permute-done.6 = bf16[2,1,1,2,32,1024]{5,4,3,2,1,0:T(8,128)(2,1)S(1)} collective-permute-done((bf16[2,1,1,2,32,1024]{5,4,3,2,1,0:T(8,128)(2,1)S(1)}, bf16[2,1,1,2,32,1024]{5,4,3,2,1,0:T(8,128)(2,1)S(1)}, u32[]{:S(2)}, u32[]{:S(2)}) %collective-permute-start.6) | collective-permute-done | bytes 262176 | tf_op jit(solution)/shard_map/ppermute | solution.py:31
  35.7 0.8 pad_maximum_fusion.6
  36.6 2.1 %collective-permute-start.3 = (bf16[2,1,2,2,32,1152]{5,4,3,2,1,0:T(8,128)(2,1)S(1)}, bf16[2,1,2,2,32,1152]{5,4,3,2,1,0:T(8,128)(2,1)S(1)}, u32[]{:S(2)}, u32[]{:S(2)}) collective-permute-start(bf16[2,1,2,2,32,1152]{5,4,3,2,1,0:T(8,128)(2,1)S(1)} %pad_maximum_fusion.5), channel_id=1, source_target_pairs={{0,4},{1,3},{2,6},{3,1},{4,0},{5,7},{6,2},{7,5},{8,12},{9,11},{10,... | collective-permute-start | bytes 1769480 | tf_op jit(solution)/shard_map/ppermute | solution.py:31
  38.7 0.6 collective-permute-start.17
  39.3 1.1 pad_maximum_fusion.3
  40.4 5.8 %collective-permute-done.15 = bf16[1,2,2,2,32,768]{5,4,3,2,1,0:T(8,128)(2,1)} collective-permute-done((bf16[1,2,2,2,32,768]{5,4,3,2,1,0:T(8,128)(2,1)S(1)}, bf16[1,2,2,2,32,768]{5,4,3,2,1,0:T(8,128)(2,1)}, u32[]{:S(2)}, u32[]{:S(2)}) %collective-permute-start.15) | collective-permute-done | bytes 393248 | tf_op jit(solution)/shard_map/ppermute | solution.py:31
  46.1 1.1 pad_maximum_fusion.4
  47.2 1.2 pad_maximum_fusion.2
  48.4 4.1 %collective-permute-done.3 = bf16[2,1,2,2,32,1152]{5,4,3,2,1,0:T(8,128)(2,1)S(1)} collective-permute-done((bf16[2,1,2,2,32,1152]{5,4,3,2,1,0:T(8,128)(2,1)S(1)}, bf16[2,1,2,2,32,1152]{5,4,3,2,1,0:T(8,128)(2,1)S(1)}, u32[]{:S(2)}, u32[]{:S(2)}) %collective-permute-start.3) | collective-permute-done | bytes 589856 | tf_op jit(solution)/shard_map/ppermute | solution.py:31
  52.8 4.2 %fusion.24 = f32[512,512]{1,0:T(8,128)S(1)} fusion(bf16[1,3584,512]{2,1,0:T(8,128)(2,1)} %param.7, bf16[512,768]{1,0:T(8,128)(2,1)S(1)} %bitcast.66, bf16[512,768]{1,0:T(8,128)(2,1)S(1)} %bitcast.62, bf16[512,1024]{1,0:T(8,128)(2,1)S(1)} %bitcast.58, bf16[512,1024]{1,0:T(8,128)(2,1)S(1)} %slice.194), kind=kOutput, calls=%fused_computation.77 | convolution fusion | flops 1893728256 | bytes 8388608 | tf_op jit(solution)/shard_map/dot_general | solution.py:79
  57.1 2.5 %fusion = bf16[512,512]{1,0:T(8,128)(2,1)S(1)} fusion(f32[512,512]{1,0:T(8,128)S(1)} %fusion.24, bf16[1,3584,512]{2,1,0:T(8,128)(2,1)S(1)} %copy-done.1, bf16[512,768]{1,0:T(8,128)(2,1)S(1)} %bitcast.67, bf16[512,768]{1,0:T(8,128)(2,1)S(1)} %bitcast.63, bf16[512,1024]{1,0:T(8,128)(2,1)S(1)} %bitcast.59, bf16[512,1024]{1,0:T(8,128)(2,1)S(1)} %slice.194), kind=kOutput, calls=%fused_computation.6 | convolution fusion | flops 1895301120 | bytes 8912896 | tf_op jit(solution)/shard_map/dot_general | solution.py:80
  59.6 0.6 fusion.11
  60.2 0.6 fusion.8
  60.7 0.7 fusion.5
  61.5 0.7 fusion.2
  62.2 4.1 %fusion.27 = f32[512,512]{1,0:T(8,128)S(1)} fusion(bf16[3584,512]{1,0:T(8,128)(2,1)} %collective-permute-done.16, bf16[512,768]{1,0:T(8,128)(2,1)S(1)} %bitcast.68, bf16[512,768]{1,0:T(8,128)(2,1)S(1)} %bitcast.64, bf16[512,1024]{1,0:T(8,128)(2,1)S(1)} %bitcast.60, bf16[512,1024]{1,0:T(8,128)(2,1)S(1)} %slice.194), kind=kOutput, calls=%fused_computation.80 | convolution fusion | flops 1893728256 | bytes 8388608 | tf_op jit(solution)/shard_map/dot_general | solution.py:79
  66.3 2.3 %multiply_convert_fusion.4 = bf16[512,512]{1,0:T(8,128)(2,1)S(1)} fusion(f32[512,512]{1,0:T(8,128)S(1)} %fusion.27, bf16[3584,512]{1,0:T(8,128)(2,1)S(1)} %collective-permute-done.17, bf16[512,768]{1,0:T(8,128)(2,1)S(1)} %bitcast.69, bf16[512,768]{1,0:T(8,128)(2,1)S(1)} %bitcast.65, bf16[512,1024]{1,0:T(8,128)(2,1)S(1)} %bitcast.61, ...), kind=kOutput, calls=%fused_computation.17 | convolution fusion | flops 1895301120 | bytes 8912896 | tf_op jit(solution)/shard_map/dot_general | solution.py:80
  68.6 0.7 multiply_convert_fusion.1
  69.7 0.6 multiply_convert_fusion.3
  70.4 1.6 %collective-permute-start.27 = (bf16[1,2,2,2,32,768]{5,4,3,2,1,0:T(8,128)(2,1)S(1)}, bf16[1,2,2,2,32,768]{5,4,3,2,1,0:T(8,128)(2,1)S(1)}, u32[]{:S(2)}, u32[]{:S(2)}) collective-permute-start(bf16[1,2,2,2,32,768]{5,4,3,2,1,0:T(8,128)(2,1)S(1)} %bitcast.71), channel_id=1, source_target_pairs={{0,2},{1,5},{2,0},{3,7},{4,6},{5,1},{6,4},{7,3},{8,10},{9,13},{10,... | collective-permute-start | bytes 1179656 | tf_op jit(solution)/shard_map/ppermute | solution.py:31
  72.0 0.6 multiply_convert_fusion.2
  73.2 0.7 multiply_convert_fusion
  74.0 1.8 %collective-permute-start.23 = (bf16[2,1,2,2,32,1024]{5,4,3,2,1,0:T(8,128)(2,1)S(1)}, bf16[2,1,2,2,32,1024]{5,4,3,2,1,0:T(8,128)(2,1)S(1)}, u32[]{:S(2)}, u32[]{:S(2)}) collective-permute-start(bf16[2,1,2,2,32,1024]{5,4,3,2,1,0:T(8,128)(2,1)S(1)} %slice.209), channel_id=1, source_target_pairs={{0,4},{1,3},{2,6},{3,1},{4,0},{5,7},{6,2},{7,5},{8,12},{9,11},{10,... | collective-permute-start | bytes 1572872 | tf_op jit(solution)/shard_map/ppermute | solution.py:31
  75.8 6.6 %collective-permute-done.27 = bf16[1,2,2,2,32,768]{5,4,3,2,1,0:T(8,128)(2,1)S(1)} collective-permute-done((bf16[1,2,2,2,32,768]{5,4,3,2,1,0:T(8,128)(2,1)S(1)}, bf16[1,2,2,2,32,768]{5,4,3,2,1,0:T(8,128)(2,1)S(1)}, u32[]{:S(2)}, u32[]{:S(2)}) %collective-permute-start.27) | collective-permute-done | bytes 393248 | tf_op jit(solution)/shard_map/ppermute | solution.py:31
  82.5 1.9 %collective-permute-start.28 = (bf16[1,1,2,2,32,768]{5,4,3,2,1,0:T(8,128)(2,1)S(1)}, bf16[1,1,2,2,32,768]{5,4,3,2,1,0:T(8,128)(2,1)S(1)}, u32[]{:S(2)}, u32[]{:S(2)}) collective-permute-start(bf16[1,1,2,2,32,768]{5,4,3,2,1,0:T(8,128)(2,1)S(1)} %slice.221), channel_id=1, source_target_pairs={{0,4},{1,3},{2,6},{3,1},{4,0},{5,7},{6,2},{7,5},{8,12},{9,11},{10,... | collective-permute-start | bytes 589832 | tf_op jit(solution)/shard_map/ppermute | solution.py:31
  84.4 6.4 %collective-permute-done.31 = bf16[1,2,2,2,32,768]{5,4,3,2,1,0:T(8,128)(2,1)S(1)} collective-permute-done((bf16[1,2,2,2,32,768]{5,4,3,2,1,0:T(8,128)(2,1)S(1)}, bf16[1,2,2,2,32,768]{5,4,3,2,1,0:T(8,128)(2,1)S(1)}, u32[]{:S(2)}, u32[]{:S(2)}) %collective-permute-start.31) | collective-permute-done | bytes 393248 | tf_op jit(solution)/shard_map/ppermute | solution.py:31
  90.9 0.8 collective-permute-start.32
  92.0 1.5 %collective-permute-start.20 = (bf16[1,1,2,2,32,1024]{5,4,3,2,1,0:T(8,128)(2,1)S(1)}, bf16[1,1,2,2,32,1024]{5,4,3,2,1,0:T(8,128)(2,1)S(1)}, u32[]{:S(2)}, u32[]{:S(2)}) collective-permute-start(bf16[1,1,2,2,32,1024]{5,4,3,2,1,0:T(8,128)(2,1)S(1)} %slice.201), channel_id=1, source_target_pairs={{0,2},{1,5},{2,0},{3,7},{4,6},{5,1},{6,4},{7,3},{8,10},{9,13},{10,... | collective-permute-start | bytes 786440 | tf_op jit(solution)/shard_map/ppermute | solution.py:31
  93.8 1.4 %collective-permute-start.24 = (bf16[2,1,1,2,32,1024]{5,4,3,2,1,0:T(8,128)(2,1)S(1)}, bf16[2,1,1,2,32,1024]{5,4,3,2,1,0:T(8,128)(2,1)S(1)}, u32[]{:S(2)}, u32[]{:S(2)}) collective-permute-start(bf16[2,1,1,2,32,1024]{5,4,3,2,1,0:T(8,128)(2,1)S(1)} %slice.211), channel_id=1, source_target_pairs={{0,8},{1,9},{2,10},{3,11},{4,12},{5,13},{6,14},{7,15},{8,0},{9,1},... | collective-permute-start | bytes 786440 | tf_op jit(solution)/shard_map/ppermute | solution.py:31
  95.3 0.7 collective-permute-start.29
  96.0 2.4 %collective-permute-done.32 = bf16[1,2,1,2,32,768]{5,4,3,2,1,0:T(8,128)(2,1)S(1)} collective-permute-done((bf16[1,2,1,2,32,768]{5,4,3,2,1,0:T(8,128)(2,1)S(1)}, bf16[1,2,1,2,32,768]{5,4,3,2,1,0:T(8,128)(2,1)S(1)}, u32[]{:S(2)}, u32[]{:S(2)}) %collective-permute-start.32) | collective-permute-done | bytes 196640 | tf_op jit(solution)/shard_map/ppermute | solution.py:31
  98.5 3.5 %collective-permute-start.33 = (bf16[1,2,1,1,32,768]{5,4,3,2,1,0:T(8,128)(2,1)S(1)}, bf16[1,2,1,1,32,768]{5,4,3,2,1,0:T(8,128)(2,1)S(1)}, u32[]{:S(2)}, u32[]{:S(2)}) collective-permute-start(bf16[1,2,1,1,32,768]{5,4,3,2,1,0:T(8,128)(2,1)S(1)} %slice.233), channel_id=1, source_target_pairs={{0,16},{1,17},{2,18},{3,19},{4,20},{5,21},{6,22},{7,23},{8,24},{9,... | collective-permute-start | bytes 294920 | tf_op jit(solution)/shard_map/ppermute | solution.py:31
  102.0 6.3 %collective-permute-done.29 = bf16[1,1,1,2,32,768]{5,4,3,2,1,0:T(8,128)(2,1)S(1)} collective-permute-done((bf16[1,1,1,2,32,768]{5,4,3,2,1,0:T(8,128)(2,1)S(1)}, bf16[1,1,1,2,32,768]{5,4,3,2,1,0:T(8,128)(2,1)S(1)}, u32[]{:S(2)}, u32[]{:S(2)}) %collective-permute-start.29) | collective-permute-done | bytes 98336 | tf_op jit(solution)/shard_map/ppermute | solution.py:31
  108.3 2.0 %collective-permute-start.30 = (bf16[1,1,1,1,32,768]{5,4,3,2,1,0:T(8,128)(2,1)S(1)}, bf16[1,1,1,1,32,768]{5,4,3,2,1,0:T(8,128)(2,1)S(1)}, u32[]{:S(2)}, u32[]{:S(2)}) collective-permute-start(bf16[1,1,1,1,32,768]{5,4,3,2,1,0:T(8,128)(2,1)S(1)} %slice.225), channel_id=1, source_target_pairs={{0,16},{1,17},{2,18},{3,19},{4,20},{5,21},{6,22},{7,23},{8,24},{9,... | collective-permute-start | bytes 147464 | tf_op jit(solution)/shard_map/ppermute | solution.py:31
  110.4 1.5 %collective-permute-start.34 = (bf16[1,1,1,1,32,768]{5,4,3,2,1,0:T(8,128)(2,1)S(1)}, bf16[1,1,1,1,32,768]{5,4,3,2,1,0:T(8,128)(2,1)S(1)}, u32[]{:S(2)}, u32[]{:S(2)}) collective-permute-start(bf16[1,1,1,1,32,768]{5,4,3,2,1,0:T(8,128)(2,1)S(1)} %slice.235), channel_id=1, source_target_pairs={{0,4},{1,3},{2,6},{3,1},{4,0},{5,7},{6,2},{7,5},{8,12},{9,11},{10,... | collective-permute-start | bytes 147464 | tf_op jit(solution)/shard_map/ppermute | solution.py:31
  111.9 2.5 %collective-permute-done.30 = bf16[1,1,1,1,32,768]{5,4,3,2,1,0:T(8,128)(2,1)S(1)} collective-permute-done((bf16[1,1,1,1,32,768]{5,4,3,2,1,0:T(8,128)(2,1)S(1)}, bf16[1,1,1,1,32,768]{5,4,3,2,1,0:T(8,128)(2,1)S(1)}, u32[]{:S(2)}, u32[]{:S(2)}) %collective-permute-start.30) | collective-permute-done | bytes 49184 | tf_op jit(solution)/shard_map/ppermute | solution.py:31
  114.7 2.5 %collective-permute-start.21 = (bf16[1,1,1,2,32,1024]{5,4,3,2,1,0:T(8,128)(2,1)S(1)}, bf16[1,1,1,2,32,1024]{5,4,3,2,1,0:T(8,128)(2,1)S(1)}, u32[]{:S(2)}, u32[]{:S(2)}) collective-permute-start(bf16[1,1,1,2,32,1024]{5,4,3,2,1,0:T(8,128)(2,1)S(1)} %slice.203), channel_id=1, source_target_pairs={{0,8},{1,9},{2,10},{3,11},{4,12},{5,13},{6,14},{7,15},{8,0},{9,1},... | collective-permute-start | bytes 393224 | tf_op jit(solution)/shard_map/ppermute | solution.py:31
  117.3 1.0 collective-permute-start.25
  118.2 3.3 %collective-permute-done.21 = bf16[1,1,1,2,32,1024]{5,4,3,2,1,0:T(8,128)(2,1)S(1)} collective-permute-done((bf16[1,1,1,2,32,1024]{5,4,3,2,1,0:T(8,128)(2,1)S(1)}, bf16[1,1,1,2,32,1024]{5,4,3,2,1,0:T(8,128)(2,1)S(1)}, u32[]{:S(2)}, u32[]{:S(2)}) %collective-permute-start.21) | collective-permute-done | bytes 131104 | tf_op jit(solution)/shard_map/ppermute | solution.py:31
  121.6 1.3 collective-permute-start.22
  122.9 3.4 %collective-permute-done.25 = bf16[2,1,1,1,32,1024]{5,4,3,2,1,0:T(8,128)(2,1)S(1)} collective-permute-done((bf16[2,1,1,1,32,1024]{5,4,3,2,1,0:T(8,128)(2,1)S(1)}, bf16[2,1,1,1,32,1024]{5,4,3,2,1,0:T(8,128)(2,1)S(1)}, u32[]{:S(2)}, u32[]{:S(2)}) %collective-permute-start.25) | collective-permute-done | bytes 131104 | tf_op jit(solution)/shard_map/ppermute | solution.py:31
  126.5 0.6 collective-permute-done.22
  127.1 3.7 %collective-permute-done.26 = bf16[1,1,1,1,32,1024]{5,4,3,2,1,0:T(8,128)(2,1)S(1)} collective-permute-done((bf16[1,1,1,1,32,1024]{5,4,3,2,1,0:T(8,128)(2,1)S(1)}, bf16[1,1,1,1,32,1024]{5,4,3,2,1,0:T(8,128)(2,1)S(1)}, u32[]{:S(2)}, u32[]{:S(2)}) %collective-permute-start.26) | collective-permute-done | bytes 65568 | tf_op jit(solution)/shard_map/ppermute | solution.py:31
  130.7 0.7 pad_maximum_fusion.11
  (83 shorter events, 3.9 us)
Async XLA Ops:
  0.8 10.6 %collective-permute-start.8 = (bf16[1,1,1,1,32,768]{5,4,3,2,1,0:T(8,128)(2,1)S(1)}, bf16[1,1,1,1,32,768]{5,4,3,2,1,0:T(8,128)(2,1)S(1)}, u32[]{:S(2)}, u32[]{:S(2)}) collective-permute-start(bf16[1,1,1,1,32,768]{5,4,3,2,1,0:T(8,128)(2,1)S(1)} %get-tuple-element.11), channel_id=1, source_target_pairs={{0,16},{1,17},{2,18},{3,19},{4,20},{5,21},{6,22},{7,23},{8,24},{9,... | collective-permute-start | bytes 147464 | tf_op jit(solution)/shard_map/ppermute | solution.py:31
  8.0 9.1 %collective-permute-start = (bf16[1,1,1,1,32,1152]{5,4,3,2,1,0:T(8,128)(2,1)S(1)}, bf16[1,1,1,1,32,1152]{5,4,3,2,1,0:T(8,128)(2,1)S(1)}, u32[]{:S(2)}, u32[]{:S(2)}) collective-permute-start(bf16[1,1,1,1,32,1152]{5,4,3,2,1,0:T(8,128)(2,1)S(1)} %fusion.17), channel_id=1, source_target_pairs={{0,16},{1,17},{2,18},{3,19},{4,20},{5,21},{6,22},{7,23},{8,24},{9,... | collective-permute-start | bytes 221192 | tf_op jit(solution)/shard_map/ppermute | solution.py:31
  8.1 8.6 %collective-permute-start.4 = (bf16[1,1,1,1,32,1024]{5,4,3,2,1,0:T(8,128)(2,1)S(1)}, bf16[1,1,1,1,32,1024]{5,4,3,2,1,0:T(8,128)(2,1)S(1)}, u32[]{:S(2)}, u32[]{:S(2)}) collective-permute-start(bf16[1,1,1,1,32,1024]{5,4,3,2,1,0:T(8,128)(2,1)S(1)} %get-tuple-element.10), channel_id=1, source_target_pairs={{0,2},{1,5},{2,0},{3,7},{4,6},{5,1},{6,4},{7,3},{8,10},{9,13},{10,... | collective-permute-start | bytes 196616 | tf_op jit(solution)/shard_map/ppermute | solution.py:31
  9.9 4.1 %collective-permute-start.12 = (bf16[1,1,1,1,32,768]{5,4,3,2,1,0:T(8,128)(2,1)S(1)}, bf16[1,1,1,1,32,768]{5,4,3,2,1,0:T(8,128)(2,1)S(1)}, u32[]{:S(2)}, u32[]{:S(2)}) collective-permute-start(bf16[1,1,1,1,32,768]{5,4,3,2,1,0:T(8,128)(2,1)S(1)} %get-tuple-element.12), channel_id=1, source_target_pairs={{0,4},{1,3},{2,6},{3,1},{4,0},{5,7},{6,2},{7,5},{8,12},{9,11},{10,... | collective-permute-start | bytes 147464 | tf_op jit(solution)/shard_map/ppermute | solution.py:31
  11.5 7.3 %collective-permute-start.9 = (bf16[1,1,1,2,32,768]{5,4,3,2,1,0:T(8,128)(2,1)S(1)}, bf16[1,1,1,2,32,768]{5,4,3,2,1,0:T(8,128)(2,1)S(1)}, u32[]{:S(2)}, u32[]{:S(2)}) collective-permute-start(bf16[1,1,1,2,32,768]{5,4,3,2,1,0:T(8,128)(2,1)S(1)} %pad_maximum_fusion.16), channel_id=1, source_target_pairs={{0,8},{1,9},{2,10},{3,11},{4,12},{5,13},{6,14},{7,15},{8,0},{9,1},... | collective-permute-start | bytes 294920 | tf_op jit(solution)/shard_map/ppermute | solution.py:31
  14.0 10.3 %collective-permute-start.13 = (bf16[1,2,1,1,32,768]{5,4,3,2,1,0:T(8,128)(2,1)S(1)}, bf16[1,2,1,1,32,768]{5,4,3,2,1,0:T(8,128)(2,1)S(1)}, u32[]{:S(2)}, u32[]{:S(2)}) collective-permute-start(bf16[1,2,1,1,32,768]{5,4,3,2,1,0:T(8,128)(2,1)S(1)} %pad_maximum_fusion.17), channel_id=1, source_target_pairs={{0,16},{1,17},{2,18},{3,19},{4,20},{5,21},{6,22},{7,23},{8,24},{9,... | collective-permute-start | bytes 294920 | tf_op jit(solution)/shard_map/ppermute | solution.py:31
  16.7 9.7 %collective-permute-start.5 = (bf16[2,1,1,1,32,1024]{5,4,3,2,1,0:T(8,128)(2,1)S(1)}, bf16[2,1,1,1,32,1024]{5,4,3,2,1,0:T(8,128)(2,1)S(1)}, u32[]{:S(2)}, u32[]{:S(2)}) collective-permute-start(bf16[2,1,1,1,32,1024]{5,4,3,2,1,0:T(8,128)(2,1)S(1)} %pad_maximum_fusion.15), channel_id=1, source_target_pairs={{0,16},{1,17},{2,18},{3,19},{4,20},{5,21},{6,22},{7,23},{8,24},{9,... | collective-permute-start | bytes 393224 | tf_op jit(solution)/shard_map/ppermute | solution.py:31
  17.1 9.5 %collective-permute-start.1 = (bf16[1,1,1,2,32,1152]{5,4,3,2,1,0:T(8,128)(2,1)S(1)}, bf16[1,1,1,2,32,1152]{5,4,3,2,1,0:T(8,128)(2,1)S(1)}, u32[]{:S(2)}, u32[]{:S(2)}) collective-permute-start(bf16[1,1,1,2,32,1152]{5,4,3,2,1,0:T(8,128)(2,1)S(1)} %pad_maximum_fusion.14), channel_id=1, source_target_pairs={{0,8},{1,9},{2,10},{3,11},{4,12},{5,13},{6,14},{7,15},{8,0},{9,1},... | collective-permute-start | bytes 442376 | tf_op jit(solution)/shard_map/ppermute | solution.py:31
  18.8 9.3 %collective-permute-start.10 = (bf16[1,1,2,2,32,768]{5,4,3,2,1,0:T(8,128)(2,1)S(1)}, bf16[1,1,2,2,32,768]{5,4,3,2,1,0:T(8,128)(2,1)S(1)}, u32[]{:S(2)}, u32[]{:S(2)}) collective-permute-start(bf16[1,1,2,2,32,768]{5,4,3,2,1,0:T(8,128)(2,1)S(1)} %pad_maximum_fusion.12), channel_id=1, source_target_pairs={{0,4},{1,3},{2,6},{3,1},{4,0},{5,7},{6,2},{7,5},{8,12},{9,11},{10,... | collective-permute-start | bytes 589832 | tf_op jit(solution)/shard_map/ppermute | solution.py:31
  24.3 7.8 %collective-permute-start.14 = (bf16[1,2,1,2,32,768]{5,4,3,2,1,0:T(8,128)(2,1)S(1)}, bf16[1,2,1,2,32,768]{5,4,3,2,1,0:T(8,128)(2,1)S(1)}, u32[]{:S(2)}, u32[]{:S(2)}) collective-permute-start(bf16[1,2,1,2,32,768]{5,4,3,2,1,0:T(8,128)(2,1)S(1)} %pad_maximum_fusion.13), channel_id=1, source_target_pairs={{0,8},{1,9},{2,10},{3,11},{4,12},{5,13},{6,14},{7,15},{8,0},{9,1},... | collective-permute-start | bytes 589832 | tf_op jit(solution)/shard_map/ppermute | solution.py:31
  26.4 9.2 %collective-permute-start.6 = (bf16[2,1,1,2,32,1024]{5,4,3,2,1,0:T(8,128)(2,1)S(1)}, bf16[2,1,1,2,32,1024]{5,4,3,2,1,0:T(8,128)(2,1)S(1)}, u32[]{:S(2)}, u32[]{:S(2)}) collective-permute-start(bf16[2,1,1,2,32,1024]{5,4,3,2,1,0:T(8,128)(2,1)S(1)} %pad_maximum_fusion.10), channel_id=1, source_target_pairs={{0,8},{1,9},{2,10},{3,11},{4,12},{5,13},{6,14},{7,15},{8,0},{9,1},... | collective-permute-start | bytes 786440 | tf_op jit(solution)/shard_map/ppermute | solution.py:31
  26.6 9.9 %collective-permute-start.2 = (bf16[1,1,2,2,32,1152]{5,4,3,2,1,0:T(8,128)(2,1)S(1)}, bf16[1,1,2,2,32,1152]{5,4,3,2,1,0:T(8,128)(2,1)S(1)}, u32[]{:S(2)}, u32[]{:S(2)}) collective-permute-start(bf16[1,1,2,2,32,1152]{5,4,3,2,1,0:T(8,128)(2,1)S(1)} %pad_maximum_fusion.9), channel_id=1, source_target_pairs={{0,2},{1,5},{2,0},{3,7},{4,6},{5,1},{6,4},{7,3},{8,10},{9,13},{10,... | collective-permute-start | bytes 884744 | tf_op jit(solution)/shard_map/ppermute | solution.py:31
  29.0 9.7 %collective-permute-start.11 = (bf16[1,2,2,2,32,768]{5,4,3,2,1,0:T(8,128)(2,1)}, bf16[1,2,2,2,32,768]{5,4,3,2,1,0:T(8,128)(2,1)}, u32[]{:S(2)}, u32[]{:S(2)}) collective-permute-start(bf16[1,2,2,2,32,768]{5,4,3,2,1,0:T(8,128)(2,1)} %pad_maximum_fusion.7), channel_id=1, source_target_pairs={{0,2},{1,5},{2,0},{3,7},{4,6},{5,1},{6,4},{7,3},{8,10},{9,13},{10,... | collective-permute-start | bytes 1179656 | tf_op jit(solution)/shard_map/ppermute | solution.py:31
  32.2 14.0 %collective-permute-start.15 = (bf16[1,2,2,2,32,768]{5,4,3,2,1,0:T(8,128)(2,1)S(1)}, bf16[1,2,2,2,32,768]{5,4,3,2,1,0:T(8,128)(2,1)}, u32[]{:S(2)}, u32[]{:S(2)}) collective-permute-start(bf16[1,2,2,2,32,768]{5,4,3,2,1,0:T(8,128)(2,1)S(1)} %pad_maximum_fusion.8), channel_id=1, source_target_pairs={{0,2},{1,5},{2,0},{3,7},{4,6},{5,1},{6,4},{7,3},{8,10},{9,13},{10,... | collective-permute-start | bytes 1179656 | tf_op jit(solution)/shard_map/ppermute | solution.py:31
  36.5 10.7 %collective-permute-start.7 = (bf16[2,1,2,2,32,1024]{5,4,3,2,1,0:T(8,128)(2,1)}, bf16[2,1,2,2,32,1024]{5,4,3,2,1,0:T(8,128)(2,1)}, u32[]{:S(2)}, u32[]{:S(2)}) collective-permute-start(bf16[2,1,2,2,32,1024]{5,4,3,2,1,0:T(8,128)(2,1)} %pad_maximum_fusion.6), channel_id=1, source_target_pairs={{0,4},{1,3},{2,6},{3,1},{4,0},{5,7},{6,2},{7,5},{8,12},{9,11},{10,... | collective-permute-start | bytes 1572872 | tf_op jit(solution)/shard_map/ppermute | solution.py:31
  36.6 15.8 %collective-permute-start.3 = (bf16[2,1,2,2,32,1152]{5,4,3,2,1,0:T(8,128)(2,1)S(1)}, bf16[2,1,2,2,32,1152]{5,4,3,2,1,0:T(8,128)(2,1)S(1)}, u32[]{:S(2)}, u32[]{:S(2)}) collective-permute-start(bf16[2,1,2,2,32,1152]{5,4,3,2,1,0:T(8,128)(2,1)S(1)} %pad_maximum_fusion.5), channel_id=1, source_target_pairs={{0,4},{1,3},{2,6},{3,1},{4,0},{5,7},{6,2},{7,5},{8,12},{9,11},{10,... | collective-permute-start | bytes 1769480 | tf_op jit(solution)/shard_map/ppermute | solution.py:31
  38.7 23.5 %collective-permute-start.16 = (bf16[3584,512]{1,0:T(8,128)(2,1)}, bf16[3584,512]{1,0:T(8,128)(2,1)}, u32[]{:S(2)}, u32[]{:S(2)}) collective-permute-start(bf16[3584,512]{1,0:T(8,128)(2,1)} %bitcast.8), channel_id=1, source_target_pairs={{0,1},{1,0},{2,3},{3,2},{4,5},{5,4},{6,7},{7,6},{8,9},{9,8},{10,11... | collective-permute-start | bytes 11010056 | tf_op jit(solution)/shard_map/ppermute | solution.py:35
  38.7 27.6 %collective-permute-start.17 = (bf16[3584,512]{1,0:T(8,128)(2,1)}, bf16[3584,512]{1,0:T(8,128)(2,1)S(1)}, u32[]{:S(2)}, u32[]{:S(2)}) collective-permute-start(bf16[3584,512]{1,0:T(8,128)(2,1)} %bitcast.72), channel_id=1, source_target_pairs={{0,1},{1,0},{2,3},{3,2},{4,5},{5,4},{6,7},{7,6},{8,9},{9,8},{10,11... | collective-permute-start | bytes 11010056 | tf_op jit(solution)/shard_map/ppermute | solution.py:35
  46.1 22.4 %collective-permute-start.18 = (bf16[512,3584]{1,0:T(8,128)(2,1)}, bf16[512,3584]{1,0:T(8,128)(2,1)S(1)}, u32[]{:S(2)}, u32[]{:S(2)}) collective-permute-start(bf16[512,3584]{1,0:T(8,128)(2,1)} %bitcast.51), channel_id=1, source_target_pairs={{0,1},{1,0},{2,3},{3,2},{4,5},{5,4},{6,7},{7,6},{8,9},{9,8},{10,11... | collective-permute-start | bytes 11010056 | tf_op jit(solution)/shard_map/ppermute | solution.py:35
  52.8 4.3 %copy-start.1 = (bf16[1,3584,512]{2,1,0:T(8,128)(2,1)S(1)}, bf16[1,3584,512]{2,1,0:T(8,128)(2,1)}, u32[]{:S(2)}) copy-start(bf16[1,3584,512]{2,1,0:T(8,128)(2,1)} %param.8) | copy-start | bytes 11010052
  57.1 2.5 %copy-start = (bf16[1,512,3584]{2,1,0:T(8,128)(2,1)S(1)}, bf16[1,512,3584]{2,1,0:T(8,128)(2,1)}, u32[]{:S(2)}) copy-start(bf16[1,512,3584]{2,1,0:T(8,128)(2,1)} %param.9) | copy-start | bytes 11010052
  69.4 22.4 %collective-permute-start.19 = (bf16[2,1,2,2,32,1024]{5,4,3,2,1,0:T(8,128)(2,1)S(1)}, bf16[2,1,2,2,32,1024]{5,4,3,2,1,0:T(8,128)(2,1)S(1)}, u32[]{:S(2)}, u32[]{:S(2)}) collective-permute-start(bf16[2,1,2,2,32,1024]{5,4,3,2,1,0:T(8,128)(2,1)S(1)} %slice.199), channel_id=1, source_target_pairs={{0,4},{1,3},{2,6},{3,1},{4,0},{5,7},{6,2},{7,5},{8,12},{9,11},{10,... | collective-permute-start | bytes 1572872 | tf_op jit(solution)/shard_map/ppermute | solution.py:31
  70.4 12.0 %collective-permute-start.27 = (bf16[1,2,2,2,32,768]{5,4,3,2,1,0:T(8,128)(2,1)S(1)}, bf16[1,2,2,2,32,768]{5,4,3,2,1,0:T(8,128)(2,1)S(1)}, u32[]{:S(2)}, u32[]{:S(2)}) collective-permute-start(bf16[1,2,2,2,32,768]{5,4,3,2,1,0:T(8,128)(2,1)S(1)} %bitcast.71), channel_id=1, source_target_pairs={{0,2},{1,5},{2,0},{3,7},{4,6},{5,1},{6,4},{7,3},{8,10},{9,13},{10,... | collective-permute-start | bytes 1179656 | tf_op jit(solution)/shard_map/ppermute | solution.py:31
  72.7 18.1 %collective-permute-start.31 = (bf16[1,2,2,2,32,768]{5,4,3,2,1,0:T(8,128)(2,1)S(1)}, bf16[1,2,2,2,32,768]{5,4,3,2,1,0:T(8,128)(2,1)S(1)}, u32[]{:S(2)}, u32[]{:S(2)}) collective-permute-start(bf16[1,2,2,2,32,768]{5,4,3,2,1,0:T(8,128)(2,1)S(1)} %bitcast.70), channel_id=1, source_target_pairs={{0,2},{1,5},{2,0},{3,7},{4,6},{5,1},{6,4},{7,3},{8,10},{9,13},{10,... | collective-permute-start | bytes 1179656 | tf_op jit(solution)/shard_map/ppermute | solution.py:31
  74.0 19.6 %collective-permute-start.23 = (bf16[2,1,2,2,32,1024]{5,4,3,2,1,0:T(8,128)(2,1)S(1)}, bf16[2,1,2,2,32,1024]{5,4,3,2,1,0:T(8,128)(2,1)S(1)}, u32[]{:S(2)}, u32[]{:S(2)}) collective-permute-start(bf16[2,1,2,2,32,1024]{5,4,3,2,1,0:T(8,128)(2,1)S(1)} %slice.209), channel_id=1, source_target_pairs={{0,4},{1,3},{2,6},{3,1},{4,0},{5,7},{6,2},{7,5},{8,12},{9,11},{10,... | collective-permute-start | bytes 1572872 | tf_op jit(solution)/shard_map/ppermute | solution.py:31
  82.5 12.7 %collective-permute-start.28 = (bf16[1,1,2,2,32,768]{5,4,3,2,1,0:T(8,128)(2,1)S(1)}, bf16[1,1,2,2,32,768]{5,4,3,2,1,0:T(8,128)(2,1)S(1)}, u32[]{:S(2)}, u32[]{:S(2)}) collective-permute-start(bf16[1,1,2,2,32,768]{5,4,3,2,1,0:T(8,128)(2,1)S(1)} %slice.221), channel_id=1, source_target_pairs={{0,4},{1,3},{2,6},{3,1},{4,0},{5,7},{6,2},{7,5},{8,12},{9,11},{10,... | collective-permute-start | bytes 589832 | tf_op jit(solution)/shard_map/ppermute | solution.py:31
  90.9 7.5 %collective-permute-start.32 = (bf16[1,2,1,2,32,768]{5,4,3,2,1,0:T(8,128)(2,1)S(1)}, bf16[1,2,1,2,32,768]{5,4,3,2,1,0:T(8,128)(2,1)S(1)}, u32[]{:S(2)}, u32[]{:S(2)}) collective-permute-start(bf16[1,2,1,2,32,768]{5,4,3,2,1,0:T(8,128)(2,1)S(1)} %slice.231), channel_id=1, source_target_pairs={{0,8},{1,9},{2,10},{3,11},{4,12},{5,13},{6,14},{7,15},{8,0},{9,1},... | collective-permute-start | bytes 589832 | tf_op jit(solution)/shard_map/ppermute | solution.py:31
  92.0 22.5 %collective-permute-start.20 = (bf16[1,1,2,2,32,1024]{5,4,3,2,1,0:T(8,128)(2,1)S(1)}, bf16[1,1,2,2,32,1024]{5,4,3,2,1,0:T(8,128)(2,1)S(1)}, u32[]{:S(2)}, u32[]{:S(2)}) collective-permute-start(bf16[1,1,2,2,32,1024]{5,4,3,2,1,0:T(8,128)(2,1)S(1)} %slice.201), channel_id=1, source_target_pairs={{0,2},{1,5},{2,0},{3,7},{4,6},{5,1},{6,4},{7,3},{8,10},{9,13},{10,... | collective-permute-start | bytes 786440 | tf_op jit(solution)/shard_map/ppermute | solution.py:31
  93.8 23.4 %collective-permute-start.24 = (bf16[2,1,1,2,32,1024]{5,4,3,2,1,0:T(8,128)(2,1)S(1)}, bf16[2,1,1,2,32,1024]{5,4,3,2,1,0:T(8,128)(2,1)S(1)}, u32[]{:S(2)}, u32[]{:S(2)}) collective-permute-start(bf16[2,1,1,2,32,1024]{5,4,3,2,1,0:T(8,128)(2,1)S(1)} %slice.211), channel_id=1, source_target_pairs={{0,8},{1,9},{2,10},{3,11},{4,12},{5,13},{6,14},{7,15},{8,0},{9,1},... | collective-permute-start | bytes 786440 | tf_op jit(solution)/shard_map/ppermute | solution.py:31
  95.3 13.0 %collective-permute-start.29 = (bf16[1,1,1,2,32,768]{5,4,3,2,1,0:T(8,128)(2,1)S(1)}, bf16[1,1,1,2,32,768]{5,4,3,2,1,0:T(8,128)(2,1)S(1)}, u32[]{:S(2)}, u32[]{:S(2)}) collective-permute-start(bf16[1,1,1,2,32,768]{5,4,3,2,1,0:T(8,128)(2,1)S(1)} %slice.223), channel_id=1, source_target_pairs={{0,8},{1,9},{2,10},{3,11},{4,12},{5,13},{6,14},{7,15},{8,0},{9,1},... | collective-permute-start | bytes 294920 | tf_op jit(solution)/shard_map/ppermute | solution.py:31
  98.5 11.8 %collective-permute-start.33 = (bf16[1,2,1,1,32,768]{5,4,3,2,1,0:T(8,128)(2,1)S(1)}, bf16[1,2,1,1,32,768]{5,4,3,2,1,0:T(8,128)(2,1)S(1)}, u32[]{:S(2)}, u32[]{:S(2)}) collective-permute-start(bf16[1,2,1,1,32,768]{5,4,3,2,1,0:T(8,128)(2,1)S(1)} %slice.233), channel_id=1, source_target_pairs={{0,16},{1,17},{2,18},{3,19},{4,20},{5,21},{6,22},{7,23},{8,24},{9,... | collective-permute-start | bytes 294920 | tf_op jit(solution)/shard_map/ppermute | solution.py:31
  108.3 6.1 %collective-permute-start.30 = (bf16[1,1,1,1,32,768]{5,4,3,2,1,0:T(8,128)(2,1)S(1)}, bf16[1,1,1,1,32,768]{5,4,3,2,1,0:T(8,128)(2,1)S(1)}, u32[]{:S(2)}, u32[]{:S(2)}) collective-permute-start(bf16[1,1,1,1,32,768]{5,4,3,2,1,0:T(8,128)(2,1)S(1)} %slice.225), channel_id=1, source_target_pairs={{0,16},{1,17},{2,18},{3,19},{4,20},{5,21},{6,22},{7,23},{8,24},{9,... | collective-permute-start | bytes 147464 | tf_op jit(solution)/shard_map/ppermute | solution.py:31
  110.4 4.2 %collective-permute-start.34 = (bf16[1,1,1,1,32,768]{5,4,3,2,1,0:T(8,128)(2,1)S(1)}, bf16[1,1,1,1,32,768]{5,4,3,2,1,0:T(8,128)(2,1)S(1)}, u32[]{:S(2)}, u32[]{:S(2)}) collective-permute-start(bf16[1,1,1,1,32,768]{5,4,3,2,1,0:T(8,128)(2,1)S(1)} %slice.235), channel_id=1, source_target_pairs={{0,4},{1,3},{2,6},{3,1},{4,0},{5,7},{6,2},{7,5},{8,12},{9,11},{10,... | collective-permute-start | bytes 147464 | tf_op jit(solution)/shard_map/ppermute | solution.py:31
  114.7 6.9 %collective-permute-start.21 = (bf16[1,1,1,2,32,1024]{5,4,3,2,1,0:T(8,128)(2,1)S(1)}, bf16[1,1,1,2,32,1024]{5,4,3,2,1,0:T(8,128)(2,1)S(1)}, u32[]{:S(2)}, u32[]{:S(2)}) collective-permute-start(bf16[1,1,1,2,32,1024]{5,4,3,2,1,0:T(8,128)(2,1)S(1)} %slice.203), channel_id=1, source_target_pairs={{0,8},{1,9},{2,10},{3,11},{4,12},{5,13},{6,14},{7,15},{8,0},{9,1},... | collective-permute-start | bytes 393224 | tf_op jit(solution)/shard_map/ppermute | solution.py:31
  117.3 9.1 %collective-permute-start.25 = (bf16[2,1,1,1,32,1024]{5,4,3,2,1,0:T(8,128)(2,1)S(1)}, bf16[2,1,1,1,32,1024]{5,4,3,2,1,0:T(8,128)(2,1)S(1)}, u32[]{:S(2)}, u32[]{:S(2)}) collective-permute-start(bf16[2,1,1,1,32,1024]{5,4,3,2,1,0:T(8,128)(2,1)S(1)} %slice.213), channel_id=1, source_target_pairs={{0,16},{1,17},{2,18},{3,19},{4,20},{5,21},{6,22},{7,23},{8,24},{9,... | collective-permute-start | bytes 393224 | tf_op jit(solution)/shard_map/ppermute | solution.py:31
  121.6 5.4 %collective-permute-start.22 = (bf16[1,1,1,1,32,1024]{5,4,3,2,1,0:T(8,128)(2,1)S(1)}, bf16[1,1,1,1,32,1024]{5,4,3,2,1,0:T(8,128)(2,1)S(1)}, u32[]{:S(2)}, u32[]{:S(2)}) collective-permute-start(bf16[1,1,1,1,32,1024]{5,4,3,2,1,0:T(8,128)(2,1)S(1)} %slice.205), channel_id=1, source_target_pairs={{0,16},{1,17},{2,18},{3,19},{4,20},{5,21},{6,22},{7,23},{8,24},{9,... | collective-permute-start | bytes 196616 | tf_op jit(solution)/shard_map/ppermute | solution.py:31
  126.4 4.3 %collective-permute-start.26 = (bf16[1,1,1,1,32,1024]{5,4,3,2,1,0:T(8,128)(2,1)S(1)}, bf16[1,1,1,1,32,1024]{5,4,3,2,1,0:T(8,128)(2,1)S(1)}, u32[]{:S(2)}, u32[]{:S(2)}) collective-permute-start(bf16[1,1,1,1,32,1024]{5,4,3,2,1,0:T(8,128)(2,1)S(1)} %slice.215), channel_id=1, source_target_pairs={{0,2},{1,5},{2,0},{3,7},{4,6},{5,1},{6,4},{7,3},{8,10},{9,13},{10,... | collective-permute-start | bytes 196616 | tf_op jit(solution)/shard_map/ppermute | solution.py:31

commit v2 on v1

--- a/solution.py
+++ b/solution.py
@@ -7,20 +7,25 @@
 DEPTH_TILE = 256
 
 
-def plan(experts, feature_count):
+def split(feature_count, parts):
+    tiles = feature_count // DEPTH_TILE
+    edges = [DEPTH_TILE * (tiles * sum(parts[:i]) // sum(parts)) for i in range(len(parts))] + [feature_count]
+    return [(low, high - low) for low, high in zip(edges, edges[1:])]
+
+
+def plan(experts):
     bits = experts.bit_length() - 1
     if experts == 16:
-        orders = ((3, 2, 0, 1), (0, 3, 2, 1), (3, 2, 1, 0), (1, 3, 2, 0))
+        gather = (((3, 0, 1, 2), 5), ((3, 1, 2, 0), 5), ((3, 2, 0, 1), 4))
+        reduce = (((3, 0, 2, 1), 4), ((2, 3, 0, 1), 5), ((3, 0, 1, 2), 5))
         mirror = (1, 0, 2, 3)
     else:
-        orders = tuple(tuple((turn + step) % bits for step in range(bits)) for turn in range(0, bits, max(1, bits // 4)))[:4]
+        turns = range(0, bits, max(1, bits // 4))
+        gather = tuple((tuple((turn + step) % bits for step in range(bits)), 1) for turn in turns)[:4]
+        reduce = gather
         half = bits // 2
         mirror = tuple((bit + half) % bits if bits % 2 == 0 else bit for bit in range(bits))
-    tiles = feature_count // DEPTH_TILE
-    count = len(orders)
-    widths = [DEPTH_TILE * (tiles // count + (1 if i < tiles % count else 0)) for i in range(count)]
-    widths[-1] += feature_count - sum(widths)
-    return orders, mirror, widths
+    return gather, reduce, mirror
 
 
 def cross(block, bit, experts, mirror):
@@ -40,8 +45,8 @@
     bits = experts.bit_length() - 1
     tok_rows, top_count = expert_ids.shape
     feature_count = tokens.shape[1]
-    orders, mirror, widths = plan(experts, feature_count)
-    starts = [sum(widths[:i]) for i in range(len(widths))]
+    gather, reduce, mirror = plan(experts)
+    columns = split(feature_count, [share for _, share in gather])
     rows = experts * tok_rows
 
     fixed_point = gate_fixed.astype(jnp.float32)
@@ -57,35 +62,42 @@
     far = [other_core(w) for w in own]
 
     held = []
-    for start, width in zip(starts, widths):
+    for start, width in columns:
         piece = tokens[:, start : start + width]
-        if start == 0:
+        if start + width == feature_count:
             piece = jnp.concatenate([piece, shares], axis=1)
         held.append(piece.reshape((1,) * bits + piece.shape))
     for step in range(bits):
-        for i, order in enumerate(orders):
-            held[i] = jnp.concatenate([held[i], cross(held[i], order[step], experts, mirror)], axis=order[step])
+        for i, (order, _) in enumerate(gather):
+            axis = order[step]
+            held[i] = jnp.concatenate([held[i], cross(held[i], axis, experts, mirror)], axis=axis)
     held = [piece.reshape(rows, -1) for piece in held]
 
     mine = lax.axis_index("expert")
     lane = jnp.arange(shares.shape[1], dtype=jnp.int32)
     picked = (lane == mine) | (lane == mine + experts)
-    weight = jnp.sum(jnp.where(picked[None, :], held[0][:, widths[0] :].astype(jnp.float32), 0.0), axis=1, keepdims=True)
-    held[0] = held[0][:, : widths[0]]
-    x = jnp.concatenate(held, axis=1)
+    weight = jnp.sum(jnp.where(picked[None, :], held[-1][:, columns[-1][1] :].astype(jnp.float32), 0.0), axis=1, keepdims=True)
 
-    hidden = []
-    for w in (own, far):
-        gate_proj = jnp.dot(x, w[0], preferred_element_type=jnp.float32)
-        up_proj = jnp.dot(x, w[1], preferred_element_type=jnp.float32)
-        hidden.append((jax.nn.silu(gate_proj) * up_proj).astype(jnp.bfloat16))
+    def project(matrix):
+        total = None
+        for i in (len(columns) - 1,) + tuple(range(len(columns) - 1)):
+            start, width = columns[i]
+            part = jnp.dot(held[i][:, :width], matrix[start : start + width], preferred_element_type=jnp.float32)
+            total = part if total is None else total + part
+        return total
+
+    hidden = [(jax.nn.silu(project(w[0])) * project(w[1])).astype(jnp.bfloat16) for w in (own, far)]
 
     sums = []
-    for start, width in zip(starts, widths):
-        part = sum(jnp.dot(h, w[2][:, start : start + width], preferred_element_type=jnp.float32) for h, w in zip(hidden, (own, far)))
+    for start, width in split(feature_count, [share for _, share in reduce]):
+        part = sum(
+            jnp.dot(h, w[2][:, start : start + width], preferred_element_type=jnp.float32)
+            for h, w in zip(hidden, (own, far))
+        )
         sums.append((part * weight).astype(jnp.bfloat16).reshape((2,) * bits + (tok_rows, width)))
+    sums = lax.optimization_barrier(sums)
     for step in reversed(range(bits)):
-        for i, order in enumerate(orders):
+        for i, (order, _) in enumerate(reduce):
             axis = order[step]
             keep = lax.slice_in_dim(sums[i], 0, 1, axis=axis)
             arrived = cross(lax.slice_in_dim(sums[i], 1, 2, axis=axis), axis, experts, mirror)

time: 132 us -> 121 us (0.917)
  starting transfers between devices: 44.3 us -> 35.4 us
  other arithmetic: 9.35 us -> 4.66 us
  matrix products: 18.3 us -> 22.4 us
  waiting for transfers between devices: 56.7 us -> 55.1 us
    ppermute x32 -> x24, starting transfers between devices: 43.8 us -> 35.1 us  [cross(): return lax.ppermute(block, ('expert', 'sub'), pairs)]
    concatenate x16 -> x12, other arithmetic: 5.39 us -> 0.79 us  [per_device(): jnp.concatenate([held[i], cross(held[i], axis, experts, mirror)], axis=axis)]
    dot_general x4 -> x12, matrix products: 13.1 us -> 17.5 us  [project(): jnp.dot(held[i][:, :width], matrix[start:start + width], preferred_elemen...]
    ppermute x32 -> x24, waiting for transfers between devices: 56.7 us -> 55.1 us  [cross(): return lax.ppermute(block, ('expert', 'sub'), pairs)]
    dot_general x8 -> x6, matrix products: 5.19 us -> 4.91 us  [per_device(): jnp.dot(h, w[2][:, start:start + width], preferred_element_type=jnp.float32)]
  transfers between devices with their start and end apart: 35 -> 27, of which waited for: 17 -> 14; matrix products, arithmetic and copies ran while one was open for 21% -> 19% of each run, Pallas kernels for 0% -> 0%
where the time goes in v2:
time: 121 us; the launch traced here: 120 us
  waiting for transfers between devices  55.1 us (46%)
  starting transfers between devices  35.4 us (29%)
  matrix products  22.4 us (19%)
  other arithmetic  4.66 us (4%)
  local copies, waits for them, and re-layouts  2.13 us (2%)
    ppermute x24, waiting for transfers between devices, cross(): return lax.ppermute(block, ('expert', 'sub'), pairs)  55.1 us
    ppermute x24, starting transfers between devices, cross(): return lax.ppermute(block, ('expert', 'sub'), pairs)  35.1 us
    dot_general x12, matrix products, project(): jnp.dot(held[i][:, :width], matrix[start:start + width], preferred_elemen...  17.5 us
    dot_general x6, matrix products, per_device(): jnp.dot(h, w[2][:, start:start + width], preferred_element_type=jnp.float32)  4.91 us
  transfers between devices with their start and end apart: 27, of which 14 were waited for; matrix products, arithmetic and copies ran while one was open for 19% of the time, Pallas kernels for 0%

profile of v2, /device:TPU:0, one launch (start us, length us, event | category | flops | bytes accessed | tf_op | source)
XLA Modules:
  0.0 120.3 jit_solution(2692267464448307946)
XLA Ops:
  0.0 0.7 convert_reduce_fusion
  0.7 0.7 convert_divide_fusion
  1.4 0.7 select_reduce_fusion.1
  2.2 0.9 slice.162
  3.1 4.1 %collective-permute-start = (bf16[1,1,1,1,32,1152]{5,4,3,2,1,0:T(8,128)(2,1)S(1)}, bf16[1,1,1,1,32,1152]{5,4,3,2,1,0:T(8,128)(2,1)S(1)}, u32[]{:S(2)}, u32[]{:S(2)}) collective-permute-start(bf16[1,1,1,1,32,1152]{5,4,3,2,1,0:T(8,128)(2,1)S(1)} %fusion.57), channel_id=1, source_target_pairs={{0,16},{1,17},{2,18},{3,19},{4,20},{5,21},{6,22},{7,23},{8,24},{9,... | collective-permute-start | bytes 221192 | tf_op jit(solution)/shard_map/ppermute | solution.py:36
  7.2 0.9 slice_bitcast_fusion.1
  8.3 2.8 %collective-permute-start.8 = (bf16[1,1,1,1,32,1280]{5,4,3,2,1,0:T(8,128)(2,1)S(1)}, bf16[1,1,1,1,32,1280]{5,4,3,2,1,0:T(8,128)(2,1)S(1)}, u32[]{:S(2)}, u32[]{:S(2)}) collective-permute-start(bf16[1,1,1,1,32,1280]{5,4,3,2,1,0:T(8,128)(2,1)S(1)} %get-tuple-element.12), channel_id=1, source_target_pairs={{0,16},{1,17},{2,18},{3,19},{4,20},{5,21},{6,22},{7,23},{8,24},{9,... | collective-permute-start | bytes 245768 | tf_op jit(solution)/shard_map/ppermute | solution.py:36
  11.1 0.2 collective-permute-start.13
  11.4 4.1 %collective-permute-start.1 = (bf16[1,1,1,2,32,1152]{5,4,3,2,1,0:T(8,128)(2,1)S(1)}, bf16[1,1,1,2,32,1152]{5,4,3,2,1,0:T(8,128)(2,1)S(1)}, u32[]{:S(2)}, u32[]{:S(2)}) collective-permute-start(bf16[1,1,1,2,32,1152]{5,4,3,2,1,0:T(8,128)(2,1)S(1)} %pad_maximum_fusion.12), channel_id=1, source_target_pairs={{0,8},{1,9},{2,10},{3,11},{4,12},{5,13},{6,14},{7,15},{8,0},{9,1},... | collective-permute-start | bytes 442376 | tf_op jit(solution)/shard_map/ppermute | solution.py:36
  15.4 2.1 %collective-permute-done.4 = bf16[1,1,1,1,32,1280]{5,4,3,2,1,0:T(8,128)(2,1)S(1)} collective-permute-done((bf16[1,1,1,1,32,1280]{5,4,3,2,1,0:T(8,128)(2,1)S(1)}, bf16[1,1,1,1,32,1280]{5,4,3,2,1,0:T(8,128)(2,1)S(1)}, u32[]{:S(2)}, u32[]{:S(2)}) %collective-permute-start.4) | collective-permute-done | bytes 81952 | tf_op jit(solution)/shard_map/ppermute | solution.py:36
  17.6 1.6 %collective-permute-start.5 = (bf16[1,1,1,2,32,1280]{5,4,3,2,1,0:T(8,128)(2,1)S(1)}, bf16[1,1,1,2,32,1280]{5,4,3,2,1,0:T(8,128)(2,1)S(1)}, u32[]{:S(2)}, u32[]{:S(2)}) collective-permute-start(bf16[1,1,1,2,32,1280]{5,4,3,2,1,0:T(8,128)(2,1)S(1)} %pad_maximum_fusion.10), channel_id=1, source_target_pairs={{0,2},{1,5},{2,0},{3,7},{4,6},{5,1},{6,4},{7,3},{8,10},{9,13},{10,... | collective-permute-start | bytes 491528 | tf_op jit(solution)/shard_map/ppermute | solution.py:36
  19.2 1.6 %collective-permute-start.9 = (bf16[1,1,1,2,32,1280]{5,4,3,2,1,0:T(8,128)(2,1)S(1)}, bf16[1,1,1,2,32,1280]{5,4,3,2,1,0:T(8,128)(2,1)S(1)}, u32[]{:S(2)}, u32[]{:S(2)}) collective-permute-start(bf16[1,1,1,2,32,1280]{5,4,3,2,1,0:T(8,128)(2,1)S(1)} %pad_maximum_fusion.11), channel_id=1, source_target_pairs={{0,4},{1,3},{2,6},{3,1},{4,0},{5,7},{6,2},{7,5},{8,12},{9,11},{10,... | collective-permute-start | bytes 491528 | tf_op jit(solution)/shard_map/ppermute | solution.py:36
  20.8 0.9 collective-permute-start.2
  21.7 2.9 %collective-permute-done.5 = bf16[1,1,1,2,32,1280]{5,4,3,2,1,0:T(8,128)(2,1)S(1)} collective-permute-done((bf16[1,1,1,2,32,1280]{5,4,3,2,1,0:T(8,128)(2,1)S(1)}, bf16[1,1,1,2,32,1280]{5,4,3,2,1,0:T(8,128)(2,1)S(1)}, u32[]{:S(2)}, u32[]{:S(2)}) %collective-permute-start.5) | collective-permute-done | bytes 163872 | tf_op jit(solution)/shard_map/ppermute | solution.py:36
  24.6 1.7 %collective-permute-start.6 = (bf16[2,1,1,2,32,1280]{5,4,3,2,1,0:T(8,128)(2,1)S(1)}, bf16[2,1,1,2,32,1280]{5,4,3,2,1,0:T(8,128)(2,1)S(1)}, u32[]{:S(2)}, u32[]{:S(2)}) collective-permute-start(bf16[2,1,1,2,32,1280]{5,4,3,2,1,0:T(8,128)(2,1)S(1)} %pad_maximum_fusion.6), channel_id=1, source_target_pairs={{0,4},{1,3},{2,6},{3,1},{4,0},{5,7},{6,2},{7,5},{8,12},{9,11},{10,... | collective-permute-start | bytes 983048 | tf_op jit(solution)/shard_map/ppermute | solution.py:36
  26.5 4.4 %collective-permute-done.2 = bf16[1,1,2,2,32,1152]{5,4,3,2,1,0:T(8,128)(2,1)S(1)} collective-permute-done((bf16[1,1,2,2,32,1152]{5,4,3,2,1,0:T(8,128)(2,1)S(1)}, bf16[1,1,2,2,32,1152]{5,4,3,2,1,0:T(8,128)(2,1)S(1)}, u32[]{:S(2)}, u32[]{:S(2)}) %collective-permute-start.2) | collective-permute-done | bytes 294944 | tf_op jit(solution)/shard_map/ppermute | solution.py:36
  31.0 1.7 %collective-permute-start.3 = (bf16[2,1,2,2,32,1152]{5,4,3,2,1,0:T(8,128)(2,1)S(1)}, bf16[2,1,2,2,32,1152]{5,4,3,2,1,0:T(8,128)(2,1)S(1)}, u32[]{:S(2)}, u32[]{:S(2)}) collective-permute-start(bf16[2,1,2,2,32,1152]{5,4,3,2,1,0:T(8,128)(2,1)S(1)} %pad_maximum_fusion.5), channel_id=1, source_target_pairs={{0,4},{1,3},{2,6},{3,1},{4,0},{5,7},{6,2},{7,5},{8,12},{9,11},{10,... | collective-permute-start | bytes 1769480 | tf_op jit(solution)/shard_map/ppermute | solution.py:36
  32.9 1.2 collective-permute-done.10
  34.1 8.1 %collective-permute-done.3 = bf16[2,1,2,2,32,1152]{5,4,3,2,1,0:T(8,128)(2,1)S(1)} collective-permute-done((bf16[2,1,2,2,32,1152]{5,4,3,2,1,0:T(8,128)(2,1)S(1)}, bf16[2,1,2,2,32,1152]{5,4,3,2,1,0:T(8,128)(2,1)S(1)}, u32[]{:S(2)}, u32[]{:S(2)}) %collective-permute-start.3) | collective-permute-done | bytes 589856 | tf_op jit(solution)/shard_map/ppermute | solution.py:36
  42.3 1.8 %collective-permute-start.11 = (bf16[1,2,2,2,32,1280]{5,4,3,2,1,0:T(8,128)(2,1)S(1)}, bf16[1,2,2,2,32,1280]{5,4,3,2,1,0:T(8,128)(2,1)S(1)}, u32[]{:S(2)}, u32[]{:S(2)}) collective-permute-start(bf16[1,2,2,2,32,1280]{5,4,3,2,1,0:T(8,128)(2,1)S(1)} %pad_maximum_fusion.4), channel_id=1, source_target_pairs={{0,2},{1,5},{2,0},{3,7},{4,6},{5,1},{6,4},{7,3},{8,10},{9,13},{10,... | collective-permute-start | bytes 1966088 | tf_op jit(solution)/shard_map/ppermute | solution.py:36
  44.0 0.1 pad_maximum_fusion.2
  44.2 0.1 select_reduce_fusion
  44.3 3.3 %collective-permute-done.7 = bf16[2,2,1,2,32,1280]{5,4,3,2,1,0:T(8,128)(2,1)S(1)} collective-permute-done((bf16[2,2,1,2,32,1280]{5,4,3,2,1,0:T(8,128)(2,1)S(1)}, bf16[2,2,1,2,32,1280]{5,4,3,2,1,0:T(8,128)(2,1)S(1)}, u32[]{:S(2)}, u32[]{:S(2)}) %collective-permute-start.7) | collective-permute-done | bytes 655392 | tf_op jit(solution)/shard_map/ppermute | solution.py:36
  47.6 0.1 pad_maximum_fusion
  47.7 0.8 fusion.29
  48.6 4.3 %collective-permute-done.11 = bf16[1,2,2,2,32,1280]{5,4,3,2,1,0:T(8,128)(2,1)S(1)} collective-permute-done((bf16[1,2,2,2,32,1280]{5,4,3,2,1,0:T(8,128)(2,1)S(1)}, bf16[1,2,2,2,32,1280]{5,4,3,2,1,0:T(8,128)(2,1)S(1)}, u32[]{:S(2)}, u32[]{:S(2)}) %collective-permute-start.11) | collective-permute-done | bytes 655392 | tf_op jit(solution)/shard_map/ppermute | solution.py:36
  52.8 0.1 pad_maximum_fusion.1
  53.0 0.8 fusion.25
  53.8 0.8 fusion.27
  54.7 0.7 fusion.7
  55.4 0.8 fusion.23
  56.2 0.8 fusion.35
  57.1 0.7 fusion.39
  57.8 0.9 fusion.10
  58.7 0.9 fusion.13
  59.5 2.2 %fusion.21 = f32[512,512]{1,0:T(8,128)S(1)} fusion(bf16[512,1280]{1,0:T(8,128)(2,1)S(1)} %bitcast.70, bf16[3584,512]{1,0:T(8,128)(2,1)} %collective-permute-done.12), kind=kOutput, calls=%fused_computation.28 | convolution fusion | flops 671088640 | bytes 3670016 | tf_op jit(solution)/shard_map/dot_general | solution.py:85
  61.7 2.2 %fusion.19 = f32[512,512]{1,0:T(8,128)S(1)} fusion(bf16[512,1280]{1,0:T(8,128)(2,1)S(1)} %bitcast.74, bf16[3584,512]{1,0:T(8,128)(2,1)} %collective-permute-done.12), kind=kOutput, calls=%fused_computation.26 | convolution fusion | flops 671088640 | bytes 3670016 | tf_op jit(solution)/shard_map/dot_general | solution.py:85
  63.9 2.2 %fusion.17 = f32[512,512]{1,0:T(8,128)S(1)} fusion(bf16[512,1280]{1,0:T(8,128)(2,1)S(1)} %bitcast.71, bf16[3584,512]{1,0:T(8,128)(2,1)} %collective-permute-done.13), kind=kOutput, calls=%fused_computation.24 | convolution fusion | flops 671088640 | bytes 3670016 | tf_op jit(solution)/shard_map/dot_general | solution.py:85
  66.0 2.2 %fusion.15 = f32[512,512]{1,0:T(8,128)S(1)} fusion(bf16[512,1280]{1,0:T(8,128)(2,1)S(1)} %bitcast.75, bf16[3584,512]{1,0:T(8,128)(2,1)} %collective-permute-done.13), kind=kOutput, calls=%fused_computation.22 | convolution fusion | flops 671088640 | bytes 3670016 | tf_op jit(solution)/shard_map/dot_general | solution.py:85
  68.2 2.0 %fusion.5 = f32[512,512]{1,0:T(8,128)S(1)} fusion(f32[512,512]{1,0:T(8,128)S(1)} %fusion.19, f32[512,512]{1,0:T(8,128)S(1)} %fusion.21, bf16[3584,512]{1,0:T(8,128)(2,1)} %collective-permute-done.12, bf16[512,1152]{1,0:T(8,128)(2,1)S(1)} %bitcast.56), kind=kOutput, calls=%fused_computation.10 | convolution fusion | flops 537395200 | bytes 5242880 | tf_op jit(solution)/shard_map/dot_general | solution.py:85
  70.1 2.0 %multiply_convert_fusion.1 = bf16[512,512]{1,0:T(8,128)(2,1)S(1)} fusion(f32[512,512]{1,0:T(8,128)S(1)} %fusion.5, f32[512,512]{1,0:T(8,128)S(1)} %fusion.15, f32[512,512]{1,0:T(8,128)S(1)} %fusion.17, bf16[3584,512]{1,0:T(8,128)(2,1)} %collective-permute-done.13, bf16[512,1152]{1,0:T(8,128)(2,1)S(1)} %bitcast.57), kind=kOutput, calls=%fused_computation.56 | convolution fusion | flops 538968064 | bytes 5767168 | tf_op jit(solution)/shard_map/dot_general | solution.py:85
  72.2 0.9 fusion.3
  73.1 0.9 fusion.2
  74.0 0.7 multiply_convert_fusion
  74.8 1.9 %collective-permute-start.15 = (bf16[2,1,2,2,32,1024]{5,4,3,2,1,0:T(8,128)(2,1)S(1)}, bf16[2,1,2,2,32,1024]{5,4,3,2,1,0:T(8,128)(2,1)S(1)}, u32[]{:S(2)}, u32[]{:S(2)}) collective-permute-start(bf16[2,1,2,2,32,1024]{5,4,3,2,1,0:T(8,128)(2,1)S(1)} %slice.192), channel_id=1, source_target_pairs={{0,4},{1,3},{2,6},{3,1},{4,0},{5,7},{6,2},{7,5},{8,12},{9,11},{10,... | collective-permute-start | bytes 1572872 | tf_op jit(solution)/shard_map/ppermute | solution.py:36
  76.7 0.3 collective-permute-start.19
  77.1 6.9 %collective-permute-done.15 = bf16[2,1,2,2,32,1024]{5,4,3,2,1,0:T(8,128)(2,1)S(1)} collective-permute-done((bf16[2,1,2,2,32,1024]{5,4,3,2,1,0:T(8,128)(2,1)S(1)}, bf16[2,1,2,2,32,1024]{5,4,3,2,1,0:T(8,128)(2,1)S(1)}, u32[]{:S(2)}, u32[]{:S(2)}) %collective-permute-start.15) | collective-permute-done | bytes 524320 | tf_op jit(solution)/shard_map/ppermute | solution.py:36
  84.0 0.2 add_convert_fusion.2
  84.3 9.4 %collective-permute-done.19 = bf16[2,1,2,2,32,1280]{5,4,3,2,1,0:T(8,128)(2,1)S(1)} collective-permute-done((bf16[2,1,2,2,32,1280]{5,4,3,2,1,0:T(8,128)(2,1)S(1)}, bf16[2,1,2,2,32,1280]{5,4,3,2,1,0:T(8,128)(2,1)S(1)}, u32[]{:S(2)}, u32[]{:S(2)}) %collective-permute-start.19) | collective-permute-done | bytes 655392 | tf_op jit(solution)/shard_map/ppermute | solution.py:36
  93.8 0.2 add_convert_fusion.1
  94.0 2.0 %collective-permute-start.20 = (bf16[1,1,2,2,32,1280]{5,4,3,2,1,0:T(8,128)(2,1)S(1)}, bf16[1,1,2,2,32,1280]{5,4,3,2,1,0:T(8,128)(2,1)S(1)}, u32[]{:S(2)}, u32[]{:S(2)}) collective-permute-start(bf16[1,1,2,2,32,1280]{5,4,3,2,1,0:T(8,128)(2,1)S(1)} %slice.236), channel_id=1, source_target_pairs={{0,2},{1,5},{2,0},{3,7},{4,6},{5,1},{6,4},{7,3},{8,10},{9,13},{10,... | collective-permute-start | bytes 983048 | tf_op jit(solution)/shard_map/ppermute | solution.py:36
  96.0 0.2 collective-permute-start.17
  96.2 0.2 add_convert_fusion
  96.4 2.0 %collective-permute-start.24 = (bf16[2,1,1,2,32,1280]{5,4,3,2,1,0:T(8,128)(2,1)S(1)}, bf16[2,1,1,2,32,1280]{5,4,3,2,1,0:T(8,128)(2,1)S(1)}, u32[]{:S(2)}, u32[]{:S(2)}) collective-permute-start(bf16[2,1,1,2,32,1280]{5,4,3,2,1,0:T(8,128)(2,1)S(1)} %slice.242), channel_id=1, source_target_pairs={{0,4},{1,3},{2,6},{3,1},{4,0},{5,7},{6,2},{7,5},{8,12},{9,11},{10,... | collective-permute-start | bytes 983048 | tf_op jit(solution)/shard_map/ppermute | solution.py:36
  98.4 4.1 %collective-permute-done.17 = bf16[1,1,1,2,32,1024]{5,4,3,2,1,0:T(8,128)(2,1)S(1)} collective-permute-done((bf16[1,1,1,2,32,1024]{5,4,3,2,1,0:T(8,128)(2,1)S(1)}, bf16[1,1,1,2,32,1024]{5,4,3,2,1,0:T(8,128)(2,1)S(1)}, u32[]{:S(2)}, u32[]{:S(2)}) %collective-permute-start.17) | collective-permute-done | bytes 131104 | tf_op jit(solution)/shard_map/ppermute | solution.py:36
  102.6 0.7 collective-permute-start.18
  103.4 2.3 %collective-permute-start.21 = (bf16[1,1,2,1,32,1280]{5,4,3,2,1,0:T(8,128)(2,1)S(1)}, bf16[1,1,2,1,32,1280]{5,4,3,2,1,0:T(8,128)(2,1)S(1)}, u32[]{:S(2)}, u32[]{:S(2)}) collective-permute-start(bf16[1,1,2,1,32,1280]{5,4,3,2,1,0:T(8,128)(2,1)S(1)} %slice.238), channel_id=1, source_target_pairs={{0,16},{1,17},{2,18},{3,19},{4,20},{5,21},{6,22},{7,23},{8,24},{9,... | collective-permute-start | bytes 491528 | tf_op jit(solution)/shard_map/ppermute | solution.py:36
  105.8 2.0 %collective-permute-start.25 = (bf16[1,1,1,2,32,1280]{5,4,3,2,1,0:T(8,128)(2,1)S(1)}, bf16[1,1,1,2,32,1280]{5,4,3,2,1,0:T(8,128)(2,1)S(1)}, u32[]{:S(2)}, u32[]{:S(2)}) collective-permute-start(bf16[1,1,1,2,32,1280]{5,4,3,2,1,0:T(8,128)(2,1)S(1)} %slice.244), channel_id=1, source_target_pairs={{0,2},{1,5},{2,0},{3,7},{4,6},{5,1},{6,4},{7,3},{8,10},{9,13},{10,... | collective-permute-start | bytes 491528 | tf_op jit(solution)/shard_map/ppermute | solution.py:36
  107.8 0.7 collective-permute-done.18
  108.5 5.2 %collective-permute-done.21 = bf16[1,1,2,1,32,1280]{5,4,3,2,1,0:T(8,128)(2,1)S(1)} collective-permute-done((bf16[1,1,2,1,32,1280]{5,4,3,2,1,0:T(8,128)(2,1)S(1)}, bf16[1,1,2,1,32,1280]{5,4,3,2,1,0:T(8,128)(2,1)S(1)}, u32[]{:S(2)}, u32[]{:S(2)}) %collective-permute-start.21) | collective-permute-done | bytes 163872 | tf_op jit(solution)/shard_map/ppermute | solution.py:36
  114.0 3.1 %collective-permute-start.26 = (bf16[1,1,1,1,32,1280]{5,4,3,2,1,0:T(8,128)(2,1)S(1)}, bf16[1,1,1,1,32,1280]{5,4,3,2,1,0:T(8,128)(2,1)S(1)}, u32[]{:S(2)}, u32[]{:S(2)}) collective-permute-start(bf16[1,1,1,1,32,1280]{5,4,3,2,1,0:T(8,128)(2,1)S(1)} %slice.246), channel_id=1, source_target_pairs={{0,16},{1,17},{2,18},{3,19},{4,20},{5,21},{6,22},{7,23},{8,24},{9,... | collective-permute-start | bytes 245768 | tf_op jit(solution)/shard_map/ppermute | solution.py:36
  117.1 1.2 %collective-permute-done.22 = bf16[1,1,1,1,32,1280]{5,4,3,2,1,0:T(8,128)(2,1)S(1)} collective-permute-done((bf16[1,1,1,1,32,1280]{5,4,3,2,1,0:T(8,128)(2,1)S(1)}, bf16[1,1,1,1,32,1280]{5,4,3,2,1,0:T(8,128)(2,1)S(1)}, u32[]{:S(2)}, u32[]{:S(2)}) %collective-permute-start.22) | collective-permute-done | bytes 81952 | tf_op jit(solution)/shard_map/ppermute | solution.py:36
  118.3 1.2 collective-permute-done.26
  119.6 0.7 pad_maximum_fusion.9
  (62 shorter events, 1.7 us)
Async XLA Ops:
  3.1 8.3 %collective-permute-start = (bf16[1,1,1,1,32,1152]{5,4,3,2,1,0:T(8,128)(2,1)S(1)}, bf16[1,1,1,1,32,1152]{5,4,3,2,1,0:T(8,128)(2,1)S(1)}, u32[]{:S(2)}, u32[]{:S(2)}) collective-permute-start(bf16[1,1,1,1,32,1152]{5,4,3,2,1,0:T(8,128)(2,1)S(1)} %fusion.57), channel_id=1, source_target_pairs={{0,16},{1,17},{2,18},{3,19},{4,20},{5,21},{6,22},{7,23},{8,24},{9,... | collective-permute-start | bytes 221192 | tf_op jit(solution)/shard_map/ppermute | solution.py:36
  8.1 9.4 %collective-permute-start.4 = (bf16[1,1,1,1,32,1280]{5,4,3,2,1,0:T(8,128)(2,1)S(1)}, bf16[1,1,1,1,32,1280]{5,4,3,2,1,0:T(8,128)(2,1)S(1)}, u32[]{:S(2)}, u32[]{:S(2)}) collective-permute-start(bf16[1,1,1,1,32,1280]{5,4,3,2,1,0:T(8,128)(2,1)S(1)} %get-tuple-element.11), channel_id=1, source_target_pairs={{0,16},{1,17},{2,18},{3,19},{4,20},{5,21},{6,22},{7,23},{8,24},{9,... | collective-permute-start | bytes 245768 | tf_op jit(solution)/shard_map/ppermute | solution.py:36
  8.2 51.3 %collective-permute-start.12 = (bf16[3584,512]{1,0:T(8,128)(2,1)}, bf16[3584,512]{1,0:T(8,128)(2,1)}, u32[]{:S(2)}, u32[]{:S(2)}) collective-permute-start(bf16[3584,512]{1,0:T(8,128)(2,1)} %bitcast.76), channel_id=1, source_target_pairs={{0,1},{1,0},{2,3},{3,2},{4,5},{5,4},{6,7},{7,6},{8,9},{9,8},{10,11... | collective-permute-start | bytes 11010056 | tf_op jit(solution)/shard_map/ppermute | solution.py:40
  8.3 10.9 %collective-permute-start.8 = (bf16[1,1,1,1,32,1280]{5,4,3,2,1,0:T(8,128)(2,1)S(1)}, bf16[1,1,1,1,32,1280]{5,4,3,2,1,0:T(8,128)(2,1)S(1)}, u32[]{:S(2)}, u32[]{:S(2)}) collective-permute-start(bf16[1,1,1,1,32,1280]{5,4,3,2,1,0:T(8,128)(2,1)S(1)} %get-tuple-element.12), channel_id=1, source_target_pairs={{0,16},{1,17},{2,18},{3,19},{4,20},{5,21},{6,22},{7,23},{8,24},{9,... | collective-permute-start | bytes 245768 | tf_op jit(solution)/shard_map/ppermute | solution.py:36
  11.1 52.7 %collective-permute-start.13 = (bf16[3584,512]{1,0:T(8,128)(2,1)}, bf16[3584,512]{1,0:T(8,128)(2,1)}, u32[]{:S(2)}, u32[]{:S(2)}) collective-permute-start(bf16[3584,512]{1,0:T(8,128)(2,1)} %bitcast.77), channel_id=1, source_target_pairs={{0,1},{1,0},{2,3},{3,2},{4,5},{5,4},{6,7},{7,6},{8,9},{9,8},{10,11... | collective-permute-start | bytes 11010056 | tf_op jit(solution)/shard_map/ppermute | solution.py:40
  11.4 9.4 %collective-permute-start.1 = (bf16[1,1,1,2,32,1152]{5,4,3,2,1,0:T(8,128)(2,1)S(1)}, bf16[1,1,1,2,32,1152]{5,4,3,2,1,0:T(8,128)(2,1)S(1)}, u32[]{:S(2)}, u32[]{:S(2)}) collective-permute-start(bf16[1,1,1,2,32,1152]{5,4,3,2,1,0:T(8,128)(2,1)S(1)} %pad_maximum_fusion.12), channel_id=1, source_target_pairs={{0,8},{1,9},{2,10},{3,11},{4,12},{5,13},{6,14},{7,15},{8,0},{9,1},... | collective-permute-start | bytes 442376 | tf_op jit(solution)/shard_map/ppermute | solution.py:36
  17.6 7.0 %collective-permute-start.5 = (bf16[1,1,1,2,32,1280]{5,4,3,2,1,0:T(8,128)(2,1)S(1)}, bf16[1,1,1,2,32,1280]{5,4,3,2,1,0:T(8,128)(2,1)S(1)}, u32[]{:S(2)}, u32[]{:S(2)}) collective-permute-start(bf16[1,1,1,2,32,1280]{5,4,3,2,1,0:T(8,128)(2,1)S(1)} %pad_maximum_fusion.10), channel_id=1, source_target_pairs={{0,2},{1,5},{2,0},{3,7},{4,6},{5,1},{6,4},{7,3},{8,10},{9,13},{10,... | collective-permute-start | bytes 491528 | tf_op jit(solution)/shard_map/ppermute | solution.py:36
  19.2 7.2 %collective-permute-start.9 = (bf16[1,1,1,2,32,1280]{5,4,3,2,1,0:T(8,128)(2,1)S(1)}, bf16[1,1,1,2,32,1280]{5,4,3,2,1,0:T(8,128)(2,1)S(1)}, u32[]{:S(2)}, u32[]{:S(2)}) collective-permute-start(bf16[1,1,1,2,32,1280]{5,4,3,2,1,0:T(8,128)(2,1)S(1)} %pad_maximum_fusion.11), channel_id=1, source_target_pairs={{0,4},{1,3},{2,6},{3,1},{4,0},{5,7},{6,2},{7,5},{8,12},{9,11},{10,... | collective-permute-start | bytes 491528 | tf_op jit(solution)/shard_map/ppermute | solution.py:36
  20.8 10.1 %collective-permute-start.2 = (bf16[1,1,2,2,32,1152]{5,4,3,2,1,0:T(8,128)(2,1)S(1)}, bf16[1,1,2,2,32,1152]{5,4,3,2,1,0:T(8,128)(2,1)S(1)}, u32[]{:S(2)}, u32[]{:S(2)}) collective-permute-start(bf16[1,1,2,2,32,1152]{5,4,3,2,1,0:T(8,128)(2,1)S(1)} %pad_maximum_fusion.8), channel_id=1, source_target_pairs={{0,2},{1,5},{2,0},{3,7},{4,6},{5,1},{6,4},{7,3},{8,10},{9,13},{10,... | collective-permute-start | bytes 884744 | tf_op jit(solution)/shard_map/ppermute | solution.py:36
  24.6 9.5 %copy-start = (bf16[1,512,3584]{2,1,0:T(8,128)(2,1)S(1)}, bf16[1,512,3584]{2,1,0:T(8,128)(2,1)}, u32[]{:S(2)}) copy-start(bf16[1,512,3584]{2,1,0:T(8,128)(2,1)} %param.9) | copy-start | bytes 11010052
  24.6 8.1 %collective-permute-start.6 = (bf16[2,1,1,2,32,1280]{5,4,3,2,1,0:T(8,128)(2,1)S(1)}, bf16[2,1,1,2,32,1280]{5,4,3,2,1,0:T(8,128)(2,1)S(1)}, u32[]{:S(2)}, u32[]{:S(2)}) collective-permute-start(bf16[2,1,1,2,32,1280]{5,4,3,2,1,0:T(8,128)(2,1)S(1)} %pad_maximum_fusion.6), channel_id=1, source_target_pairs={{0,4},{1,3},{2,6},{3,1},{4,0},{5,7},{6,2},{7,5},{8,12},{9,11},{10,... | collective-permute-start | bytes 983048 | tf_op jit(solution)/shard_map/ppermute | solution.py:36
  26.4 7.7 %collective-permute-start.10 = (bf16[1,2,1,2,32,1280]{5,4,3,2,1,0:T(8,128)(2,1)S(1)}, bf16[1,2,1,2,32,1280]{5,4,3,2,1,0:T(8,128)(2,1)S(1)}, u32[]{:S(2)}, u32[]{:S(2)}) collective-permute-start(bf16[1,2,1,2,32,1280]{5,4,3,2,1,0:T(8,128)(2,1)S(1)} %pad_maximum_fusion.7), channel_id=1, source_target_pairs={{0,8},{1,9},{2,10},{3,11},{4,12},{5,13},{6,14},{7,15},{8,0},{9,1},... | collective-permute-start | bytes 983048 | tf_op jit(solution)/shard_map/ppermute | solution.py:36
  31.0 11.3 %collective-permute-start.3 = (bf16[2,1,2,2,32,1152]{5,4,3,2,1,0:T(8,128)(2,1)S(1)}, bf16[2,1,2,2,32,1152]{5,4,3,2,1,0:T(8,128)(2,1)S(1)}, u32[]{:S(2)}, u32[]{:S(2)}) collective-permute-start(bf16[2,1,2,2,32,1152]{5,4,3,2,1,0:T(8,128)(2,1)S(1)} %pad_maximum_fusion.5), channel_id=1, source_target_pairs={{0,4},{1,3},{2,6},{3,1},{4,0},{5,7},{6,2},{7,5},{8,12},{9,11},{10,... | collective-permute-start | bytes 1769480 | tf_op jit(solution)/shard_map/ppermute | solution.py:36
  32.8 14.8 %collective-permute-start.7 = (bf16[2,2,1,2,32,1280]{5,4,3,2,1,0:T(8,128)(2,1)S(1)}, bf16[2,2,1,2,32,1280]{5,4,3,2,1,0:T(8,128)(2,1)S(1)}, u32[]{:S(2)}, u32[]{:S(2)}) collective-permute-start(bf16[2,2,1,2,32,1280]{5,4,3,2,1,0:T(8,128)(2,1)S(1)} %pad_maximum_fusion.3), channel_id=1, source_target_pairs={{0,8},{1,9},{2,10},{3,11},{4,12},{5,13},{6,14},{7,15},{8,0},{9,1},... | collective-permute-start | bytes 1966088 | tf_op jit(solution)/shard_map/ppermute | solution.py:36
  34.1 38.1 %collective-permute-start.14 = (bf16[512,3584]{1,0:T(8,128)(2,1)S(1)}, bf16[512,3584]{1,0:T(8,128)(2,1)S(1)}, u32[]{:S(2)}, u32[]{:S(2)}) collective-permute-start(bf16[512,3584]{1,0:T(8,128)(2,1)S(1)} %bitcast.64), channel_id=1, source_target_pairs={{0,1},{1,0},{2,3},{3,2},{4,5},{5,4},{6,7},{7,6},{8,9},{9,8},{10,11... | collective-permute-start | bytes 11010056 | tf_op jit(solution)/shard_map/ppermute | solution.py:40
  42.3 10.6 %collective-permute-start.11 = (bf16[1,2,2,2,32,1280]{5,4,3,2,1,0:T(8,128)(2,1)S(1)}, bf16[1,2,2,2,32,1280]{5,4,3,2,1,0:T(8,128)(2,1)S(1)}, u32[]{:S(2)}, u32[]{:S(2)}) collective-permute-start(bf16[1,2,2,2,32,1280]{5,4,3,2,1,0:T(8,128)(2,1)S(1)} %pad_maximum_fusion.4), channel_id=1, source_target_pairs={{0,2},{1,5},{2,0},{3,7},{4,6},{5,1},{6,4},{7,3},{8,10},{9,13},{10,... | collective-permute-start | bytes 1966088 | tf_op jit(solution)/shard_map/ppermute | solution.py:36
  44.0 3.7 %copy-start.1 = (bf16[1,3584,512]{2,1,0:T(8,128)(2,1)S(1)}, bf16[1,3584,512]{2,1,0:T(8,128)(2,1)}, u32[]{:S(2)}) copy-start(bf16[1,3584,512]{2,1,0:T(8,128)(2,1)} %param.7) | copy-start | bytes 11010052
  47.7 5.3 %copy-start.2 = (bf16[1,3584,512]{2,1,0:T(8,128)(2,1)S(1)}, bf16[1,3584,512]{2,1,0:T(8,128)(2,1)}, u32[]{:S(2)}) copy-start(bf16[1,3584,512]{2,1,0:T(8,128)(2,1)} %param.8) | copy-start | bytes 11010052
  74.8 9.2 %collective-permute-start.15 = (bf16[2,1,2,2,32,1024]{5,4,3,2,1,0:T(8,128)(2,1)S(1)}, bf16[2,1,2,2,32,1024]{5,4,3,2,1,0:T(8,128)(2,1)S(1)}, u32[]{:S(2)}, u32[]{:S(2)}) collective-permute-start(bf16[2,1,2,2,32,1024]{5,4,3,2,1,0:T(8,128)(2,1)S(1)} %slice.192), channel_id=1, source_target_pairs={{0,4},{1,3},{2,6},{3,1},{4,0},{5,7},{6,2},{7,5},{8,12},{9,11},{10,... | collective-permute-start | bytes 1572872 | tf_op jit(solution)/shard_map/ppermute | solution.py:36
  76.7 17.1 %collective-permute-start.19 = (bf16[2,1,2,2,32,1280]{5,4,3,2,1,0:T(8,128)(2,1)S(1)}, bf16[2,1,2,2,32,1280]{5,4,3,2,1,0:T(8,128)(2,1)S(1)}, u32[]{:S(2)}, u32[]{:S(2)}) collective-permute-start(bf16[2,1,2,2,32,1280]{5,4,3,2,1,0:T(8,128)(2,1)S(1)} %slice.200), channel_id=1, source_target_pairs={{0,4},{1,3},{2,6},{3,1},{4,0},{5,7},{6,2},{7,5},{8,12},{9,11},{10,... | collective-permute-start | bytes 1966088 | tf_op jit(solution)/shard_map/ppermute | solution.py:36
  77.0 19.2 %collective-permute-start.23 = (bf16[2,2,1,2,32,1280]{5,4,3,2,1,0:T(8,128)(2,1)S(1)}, bf16[2,2,1,2,32,1280]{5,4,3,2,1,0:T(8,128)(2,1)S(1)}, u32[]{:S(2)}, u32[]{:S(2)}) collective-permute-start(bf16[2,2,1,2,32,1280]{5,4,3,2,1,0:T(8,128)(2,1)S(1)} %slice.208), channel_id=1, source_target_pairs={{0,8},{1,9},{2,10},{3,11},{4,12},{5,13},{6,14},{7,15},{8,0},{9,1},... | collective-permute-start | bytes 1966088 | tf_op jit(solution)/shard_map/ppermute | solution.py:36
  84.2 11.7 %collective-permute-start.16 = (bf16[2,1,1,2,32,1024]{5,4,3,2,1,0:T(8,128)(2,1)S(1)}, bf16[2,1,1,2,32,1024]{5,4,3,2,1,0:T(8,128)(2,1)S(1)}, u32[]{:S(2)}, u32[]{:S(2)}) collective-permute-start(bf16[2,1,1,2,32,1024]{5,4,3,2,1,0:T(8,128)(2,1)S(1)} %slice.230), channel_id=1, source_target_pairs={{0,8},{1,9},{2,10},{3,11},{4,12},{5,13},{6,14},{7,15},{8,0},{9,1},... | collective-permute-start | bytes 786440 | tf_op jit(solution)/shard_map/ppermute | solution.py:36
  94.0 9.3 %collective-permute-start.20 = (bf16[1,1,2,2,32,1280]{5,4,3,2,1,0:T(8,128)(2,1)S(1)}, bf16[1,1,2,2,32,1280]{5,4,3,2,1,0:T(8,128)(2,1)S(1)}, u32[]{:S(2)}, u32[]{:S(2)}) collective-permute-start(bf16[1,1,2,2,32,1280]{5,4,3,2,1,0:T(8,128)(2,1)S(1)} %slice.236), channel_id=1, source_target_pairs={{0,2},{1,5},{2,0},{3,7},{4,6},{5,1},{6,4},{7,3},{8,10},{9,13},{10,... | collective-permute-start | bytes 983048 | tf_op jit(solution)/shard_map/ppermute | solution.py:36
  96.0 6.5 %collective-permute-start.17 = (bf16[1,1,1,2,32,1024]{5,4,3,2,1,0:T(8,128)(2,1)S(1)}, bf16[1,1,1,2,32,1024]{5,4,3,2,1,0:T(8,128)(2,1)S(1)}, u32[]{:S(2)}, u32[]{:S(2)}) collective-permute-start(bf16[1,1,1,2,32,1024]{5,4,3,2,1,0:T(8,128)(2,1)S(1)} %slice.232), channel_id=1, source_target_pairs={{0,2},{1,5},{2,0},{3,7},{4,6},{5,1},{6,4},{7,3},{8,10},{9,13},{10,... | collective-permute-start | bytes 393224 | tf_op jit(solution)/shard_map/ppermute | solution.py:36
  96.4 9.3 %collective-permute-start.24 = (bf16[2,1,1,2,32,1280]{5,4,3,2,1,0:T(8,128)(2,1)S(1)}, bf16[2,1,1,2,32,1280]{5,4,3,2,1,0:T(8,128)(2,1)S(1)}, u32[]{:S(2)}, u32[]{:S(2)}) collective-permute-start(bf16[2,1,1,2,32,1280]{5,4,3,2,1,0:T(8,128)(2,1)S(1)} %slice.242), channel_id=1, source_target_pairs={{0,4},{1,3},{2,6},{3,1},{4,0},{5,7},{6,2},{7,5},{8,12},{9,11},{10,... | collective-permute-start | bytes 983048 | tf_op jit(solution)/shard_map/ppermute | solution.py:36
  102.6 5.9 %collective-permute-start.18 = (bf16[1,1,1,1,32,1024]{5,4,3,2,1,0:T(8,128)(2,1)S(1)}, bf16[1,1,1,1,32,1024]{5,4,3,2,1,0:T(8,128)(2,1)S(1)}, u32[]{:S(2)}, u32[]{:S(2)}) collective-permute-start(bf16[1,1,1,1,32,1024]{5,4,3,2,1,0:T(8,128)(2,1)S(1)} %slice.234), channel_id=1, source_target_pairs={{0,16},{1,17},{2,18},{3,19},{4,20},{5,21},{6,22},{7,23},{8,24},{9,... | collective-permute-start | bytes 196616 | tf_op jit(solution)/shard_map/ppermute | solution.py:36
  103.4 10.4 %collective-permute-start.21 = (bf16[1,1,2,1,32,1280]{5,4,3,2,1,0:T(8,128)(2,1)S(1)}, bf16[1,1,2,1,32,1280]{5,4,3,2,1,0:T(8,128)(2,1)S(1)}, u32[]{:S(2)}, u32[]{:S(2)}) collective-permute-start(bf16[1,1,2,1,32,1280]{5,4,3,2,1,0:T(8,128)(2,1)S(1)} %slice.238), channel_id=1, source_target_pairs={{0,16},{1,17},{2,18},{3,19},{4,20},{5,21},{6,22},{7,23},{8,24},{9,... | collective-permute-start | bytes 491528 | tf_op jit(solution)/shard_map/ppermute | solution.py:36
  105.8 8.1 %collective-permute-start.25 = (bf16[1,1,1,2,32,1280]{5,4,3,2,1,0:T(8,128)(2,1)S(1)}, bf16[1,1,1,2,32,1280]{5,4,3,2,1,0:T(8,128)(2,1)S(1)}, u32[]{:S(2)}, u32[]{:S(2)}) collective-permute-start(bf16[1,1,1,2,32,1280]{5,4,3,2,1,0:T(8,128)(2,1)S(1)} %slice.244), channel_id=1, source_target_pairs={{0,2},{1,5},{2,0},{3,7},{4,6},{5,1},{6,4},{7,3},{8,10},{9,13},{10,... | collective-permute-start | bytes 491528 | tf_op jit(solution)/shard_map/ppermute | solution.py:36
  113.8 4.5 %collective-permute-start.22 = (bf16[1,1,1,1,32,1280]{5,4,3,2,1,0:T(8,128)(2,1)S(1)}, bf16[1,1,1,1,32,1280]{5,4,3,2,1,0:T(8,128)(2,1)S(1)}, u32[]{:S(2)}, u32[]{:S(2)}) collective-permute-start(bf16[1,1,1,1,32,1280]{5,4,3,2,1,0:T(8,128)(2,1)S(1)} %slice.240), channel_id=1, source_target_pairs={{0,8},{1,9},{2,10},{3,11},{4,12},{5,13},{6,14},{7,15},{8,0},{9,1},... | collective-permute-start | bytes 245768 | tf_op jit(solution)/shard_map/ppermute | solution.py:36
  114.0 5.6 %collective-permute-start.26 = (bf16[1,1,1,1,32,1280]{5,4,3,2,1,0:T(8,128)(2,1)S(1)}, bf16[1,1,1,1,32,1280]{5,4,3,2,1,0:T(8,128)(2,1)S(1)}, u32[]{:S(2)}, u32[]{:S(2)}) collective-permute-start(bf16[1,1,1,1,32,1280]{5,4,3,2,1,0:T(8,128)(2,1)S(1)} %slice.246), channel_id=1, source_target_pairs={{0,16},{1,17},{2,18},{3,19},{4,20},{5,21},{6,22},{7,23},{8,24},{9,... | collective-permute-start | bytes 245768 | tf_op jit(solution)/shard_map/ppermute | solution.py:36

commit v3 on v2

--- a/solution.py
+++ b/solution.py
@@ -1,6 +1,9 @@
+import functools
+
 import jax
 import jax.numpy as jnp
 from jax import lax
+from jax.experimental import pallas as pl
 from jax.sharding import PartitionSpec as P
 
 LANES = 128
@@ -40,6 +43,33 @@
     return lax.ppermute(block, "sub", [(0, 1), (1, 0)])
 
 
+def piece_kernel(columns, experts, tokens_ref, ids_ref, fixed_ref, *out_refs):
+    for out_ref, (start, width) in zip(out_refs, columns):
+        out_ref[:, :width] = tokens_ref[:, start : start + width]
+    last_ref, width = out_refs[-1], columns[-1][1]
+    fixed_point = fixed_ref[...].T.astype(jnp.float32)
+    ids = ids_ref[...].T
+    share = fixed_point / jnp.sum(fixed_point, axis=1, keepdims=True)
+    lane = lax.broadcasted_iota(jnp.int32, (tokens_ref.shape[0], last_ref.shape[1] - width), 1)
+    expert = jnp.where(lane < experts, lane, lane - experts)
+    dense = jnp.zeros(lane.shape, jnp.float32)
+    for k in range(share.shape[1]):
+        dense = dense + jnp.where(expert == ids[:, k : k + 1], share[:, k : k + 1], 0.0)
+    high = dense.astype(jnp.bfloat16).astype(jnp.float32)
+    last_ref[:, width:] = jnp.where(lane < experts, high, dense - high).astype(last_ref.dtype)
+
+
+def cut_pieces(tokens, expert_ids, gate_fixed, columns, experts):
+    tok_rows = tokens.shape[0]
+    extra = -(-2 * experts // LANES) * LANES
+    widths = [width for _, width in columns]
+    widths[-1] += extra
+    return pl.pallas_call(
+        functools.partial(piece_kernel, columns, experts),
+        out_shape=[jax.ShapeDtypeStruct((tok_rows, width), tokens.dtype) for width in widths],
+    )(tokens, expert_ids.T, gate_fixed.T)
+
+
 def per_device(tokens, gate_weight, up_weight, down_weight, expert_ids, gate_fixed):
     experts = lax.axis_size("expert")
     bits = experts.bit_length() - 1
@@ -49,38 +79,32 @@
     columns = split(feature_count, [share for _, share in gather])
     rows = experts * tok_rows
 
-    fixed_point = gate_fixed.astype(jnp.float32)
-    route_share = fixed_point / jnp.sum(fixed_point, axis=1, keepdims=True)
-    chosen = expert_ids[:, :, None] == jnp.arange(experts, dtype=jnp.int32)[None, None, :]
-    dense_share = jnp.sum(jnp.where(chosen, route_share[:, :, None], 0.0), axis=1)
-    high = lax.reduce_precision(dense_share, 8, 7)
-    low = dense_share - high
-    shares = jnp.concatenate([high, low], axis=1)
-    shares = jnp.pad(shares, ((0, 0), (0, -2 * experts % LANES))).astype(jnp.bfloat16)
+    own = [w[0] for w in (gate_weight, up_weight, down_weight)]
+    far = [other_core(w) for w in own[:1]]
 
-    own = [w[0] for w in (gate_weight, up_weight, down_weight)]
-    far = [other_core(w) for w in own]
-
-    held = []
-    for start, width in columns:
-        piece = tokens[:, start : start + width]
-        if start + width == feature_count:
-            piece = jnp.concatenate([piece, shares], axis=1)
-        held.append(piece.reshape((1,) * bits + piece.shape))
+    held = [
+        piece.reshape((1,) * bits + piece.shape)
+        for piece in cut_pieces(tokens, expert_ids, gate_fixed, columns, experts)
+    ]
     for step in range(bits):
         for i, (order, _) in enumerate(gather):
             axis = order[step]
             held[i] = jnp.concatenate([held[i], cross(held[i], axis, experts, mirror)], axis=axis)
     held = [piece.reshape(rows, -1) for piece in held]
+    held[0], near = lax.optimization_barrier((held[0], own[1]))
+    far.append(other_core(near))
+    held[0], near = lax.optimization_barrier((held[0], own[2]))
+    far.append(other_core(near))
 
     mine = lax.axis_index("expert")
+    shares = held[-1][:, columns[-1][1] :]
     lane = jnp.arange(shares.shape[1], dtype=jnp.int32)
     picked = (lane == mine) | (lane == mine + experts)
-    weight = jnp.sum(jnp.where(picked[None, :], held[-1][:, columns[-1][1] :].astype(jnp.float32), 0.0), axis=1, keepdims=True)
+    weight = jnp.sum(jnp.where(picked[None, :], shares.astype(jnp.float32), 0.0), axis=1, keepdims=True)
 
     def project(matrix):
         total = None
-        for i in (len(columns) - 1,) + tuple(range(len(columns) - 1)):
+        for i in range(len(columns)):
             start, width = columns[i]
             part = jnp.dot(held[i][:, :width], matrix[start : start + width], preferred_element_type=jnp.float32)
             total = part if total is None else total + part

time: 121 us -> 117 us (0.967)
  waiting for transfers between devices: 55.1 us -> 45.7 us
  starting transfers between devices: 35.4 us -> 42.1 us
  matrix products: 22.4 us -> 18.5 us
  Pallas kernels: 0 us -> 1.97 us
  other arithmetic: 4.66 us -> 6.25 us
    ppermute x24, waiting for transfers between devices: 55.1 us -> 45.7 us  [cross(): return lax.ppermute(block, ('expert', 'sub'), pairs)]
    ppermute x24, starting transfers between devices: 35.1 us -> 42 us  [cross(): return lax.ppermute(block, ('expert', 'sub'), pairs)]
    dot_general x12, matrix products: 17.5 us -> 13.7 us  [project(): jnp.dot(held[i][:, :width], matrix[start:start + width], preferred_elemen...]
    concatenate x12, other arithmetic: 0.79 us -> 4.48 us  [per_device(): jnp.concatenate([held[i], cross(held[i], axis, experts, mirror)], axis=axis)]
    pallas_call x0 -> x1, Pallas kernels: none -> 1.97 us  [cut_pieces(): pl.pallas_call(functools.partial(piece_kernel, columns, experts), out_sha...]
    reduce_sum x3 -> x1, other arithmetic: 1.53 us -> 0.12 us  [per_device(): jnp.sum(jnp.where(picked[None, :], shares.astype(jnp.float32), 0.0), axis...]
    unnamed x7 -> x12, local copies, waits for them, and re-layouts: 0.1 us -> 1.5 us
  transfers between devices with their start and end apart: 27 -> 27, of which waited for: 14 -> 15; matrix products, arithmetic and copies ran while one was open for 19% -> 19% of each run, Pallas kernels for 0% -> 0%
where the time goes in v3:
time: 117 us
  waiting for transfers between devices  45.7 us (39%)
  starting transfers between devices  42.1 us (36%)
  matrix products  18.5 us (16%)
  other arithmetic  6.25 us (5%)
  Pallas kernels  1.97 us (2%)
  local copies, waits for them, and re-layouts  1.75 us (1%)
    ppermute x24, waiting for transfers between devices, cross(): return lax.ppermute(block, ('expert', 'sub'), pairs)  45.7 us
    ppermute x24, starting transfers between devices, cross(): return lax.ppermute(block, ('expert', 'sub'), pairs)  42 us
    dot_general x12, matrix products, project(): jnp.dot(held[i][:, :width], matrix[start:start + width], preferred_elemen...  13.7 us
    dot_general x6, matrix products, per_device(): jnp.dot(h, w[2][:, start:start + width], preferred_element_type=jnp.float32)  4.82 us
    concatenate x12, other arithmetic, per_device(): jnp.concatenate([held[i], cross(held[i], axis, experts, mirror)], axis=axis)  4.48 us
  transfers between devices with their start and end apart: 27, of which 15 were waited for; matrix products, arithmetic and copies ran while one was open for 19% of the time, Pallas kernels for 0%

profile of v3, /device:TPU:0, one launch (start us, length us, event | category | flops | bytes accessed | tf_op | source)
XLA Modules:
  0.0 116.7 jit_solution(8029927632329460516)
XLA Ops:
  0.0 2.0 %shard_map.64 = (bf16[32,1280]{1,0:T(8,128)(2,1)}, bf16[32,1280]{1,0:T(8,128)(2,1)}, bf16[32,1152]{1,0:T(8,128)(2,1)}) custom-call(bf16[32,3584]{1,0:T(8,128)(2,1)} %tokens_ref.1, s32[8,32]{1,0:T(8,128)} %bitcast.90, s32[8,32]{1,0:T(8,128)} %bitcast.91), custom_call_target="tpu_custom_call" | custom-call | tf_op jit(solution)/shard_map/pallas_call | solution.py:67
  2.0 4.0 %collective-permute-start.8 = (bf16[1,1,1,1,32,1152]{5,4,3,2,1,0:T(8,128)(2,1)}, bf16[1,1,1,1,32,1152]{5,4,3,2,1,0:T(8,128)(2,1)S(1)}, u32[]{:S(2)}, u32[]{:S(2)}) collective-permute-start(bf16[1,1,1,1,32,1152]{5,4,3,2,1,0:T(8,128)(2,1)} %bitcast.85), channel_id=1, source_target_pairs={{0,16},{1,17},{2,18},{3,19},{4,20},{5,21},{6,22},{7,23},{8,24},{9,... | collective-permute-start | bytes 221192 | tf_op jit(solution)/shard_map/ppermute | solution.py:39
  6.1 2.9 %collective-permute-start.4 = (bf16[1,1,1,1,32,1280]{5,4,3,2,1,0:T(8,128)(2,1)}, bf16[1,1,1,1,32,1280]{5,4,3,2,1,0:T(8,128)(2,1)S(1)}, u32[]{:S(2)}, u32[]{:S(2)}) collective-permute-start(bf16[1,1,1,1,32,1280]{5,4,3,2,1,0:T(8,128)(2,1)} %bitcast.71), channel_id=1, source_target_pairs={{0,16},{1,17},{2,18},{3,19},{4,20},{5,21},{6,22},{7,23},{8,24},{9,... | collective-permute-start | bytes 245768 | tf_op jit(solution)/shard_map/ppermute | solution.py:39
  8.9 2.2 %collective-permute-done.8 = bf16[1,1,1,1,32,1152]{5,4,3,2,1,0:T(8,128)(2,1)S(1)} collective-permute-done((bf16[1,1,1,1,32,1152]{5,4,3,2,1,0:T(8,128)(2,1)}, bf16[1,1,1,1,32,1152]{5,4,3,2,1,0:T(8,128)(2,1)S(1)}, u32[]{:S(2)}, u32[]{:S(2)}) %collective-permute-start.8) | collective-permute-done | bytes 73760 | tf_op jit(solution)/shard_map/ppermute | solution.py:39
  11.2 0.9 pad_maximum_fusion.12
  12.1 3.4 %collective-permute-start.9 = (bf16[1,1,1,2,32,1152]{5,4,3,2,1,0:T(8,128)(2,1)S(1)}, bf16[1,1,1,2,32,1152]{5,4,3,2,1,0:T(8,128)(2,1)S(1)}, u32[]{:S(2)}, u32[]{:S(2)}) collective-permute-start(bf16[1,1,1,2,32,1152]{5,4,3,2,1,0:T(8,128)(2,1)S(1)} %pad_maximum_fusion.12), channel_id=1, source_target_pairs={{0,8},{1,9},{2,10},{3,11},{4,12},{5,13},{6,14},{7,15},{8,0},{9,1},... | collective-permute-start | bytes 442376 | tf_op jit(solution)/shard_map/ppermute | solution.py:39
  15.6 0.9 pad_maximum_fusion.10
  16.5 2.0 %collective-permute-start.1 = (bf16[1,1,1,2,32,1280]{5,4,3,2,1,0:T(8,128)(2,1)S(1)}, bf16[1,1,1,2,32,1280]{5,4,3,2,1,0:T(8,128)(2,1)S(1)}, u32[]{:S(2)}, u32[]{:S(2)}) collective-permute-start(bf16[1,1,1,2,32,1280]{5,4,3,2,1,0:T(8,128)(2,1)S(1)} %pad_maximum_fusion.10), channel_id=1, source_target_pairs={{0,2},{1,5},{2,0},{3,7},{4,6},{5,1},{6,4},{7,3},{8,10},{9,13},{10,... | collective-permute-start | bytes 491528 | tf_op jit(solution)/shard_map/ppermute | solution.py:39
  18.5 1.1 pad_maximum_fusion.11
  19.6 1.6 %collective-permute-start.5 = (bf16[1,1,1,2,32,1280]{5,4,3,2,1,0:T(8,128)(2,1)S(1)}, bf16[1,1,1,2,32,1280]{5,4,3,2,1,0:T(8,128)(2,1)S(1)}, u32[]{:S(2)}, u32[]{:S(2)}) collective-permute-start(bf16[1,1,1,2,32,1280]{5,4,3,2,1,0:T(8,128)(2,1)S(1)} %pad_maximum_fusion.11), channel_id=1, source_target_pairs={{0,4},{1,3},{2,6},{3,1},{4,0},{5,7},{6,2},{7,5},{8,12},{9,11},{10,... | collective-permute-start | bytes 491528 | tf_op jit(solution)/shard_map/ppermute | solution.py:39
  21.2 0.9 pad_maximum_fusion.8
  22.1 0.9 collective-permute-start.10
  23.1 2.5 %collective-permute-start.2 = (bf16[2,1,1,2,32,1280]{5,4,3,2,1,0:T(8,128)(2,1)S(1)}, bf16[2,1,1,2,32,1280]{5,4,3,2,1,0:T(8,128)(2,1)S(1)}, u32[]{:S(2)}, u32[]{:S(2)}) collective-permute-start(bf16[2,1,1,2,32,1280]{5,4,3,2,1,0:T(8,128)(2,1)S(1)} %pad_maximum_fusion.6), channel_id=1, source_target_pairs={{0,4},{1,3},{2,6},{3,1},{4,0},{5,7},{6,2},{7,5},{8,12},{9,11},{10,... | collective-permute-start | bytes 983048 | tf_op jit(solution)/shard_map/ppermute | solution.py:39
  25.6 0.5 collective-permute-done.5
  26.1 2.0 %collective-permute-start.6 = (bf16[1,2,1,2,32,1280]{5,4,3,2,1,0:T(8,128)(2,1)S(1)}, bf16[1,2,1,2,32,1280]{5,4,3,2,1,0:T(8,128)(2,1)S(1)}, u32[]{:S(2)}, u32[]{:S(2)}) collective-permute-start(bf16[1,2,1,2,32,1280]{5,4,3,2,1,0:T(8,128)(2,1)S(1)} %pad_maximum_fusion.7), channel_id=1, source_target_pairs={{0,8},{1,9},{2,10},{3,11},{4,12},{5,13},{6,14},{7,15},{8,0},{9,1},... | collective-permute-start | bytes 983048 | tf_op jit(solution)/shard_map/ppermute | solution.py:39
  28.1 2.9 %collective-permute-done.10 = bf16[1,1,2,2,32,1152]{5,4,3,2,1,0:T(8,128)(2,1)S(1)} collective-permute-done((bf16[1,1,2,2,32,1152]{5,4,3,2,1,0:T(8,128)(2,1)S(1)}, bf16[1,1,2,2,32,1152]{5,4,3,2,1,0:T(8,128)(2,1)S(1)}, u32[]{:S(2)}, u32[]{:S(2)}) %collective-permute-start.10) | collective-permute-done | bytes 294944 | tf_op jit(solution)/shard_map/ppermute | solution.py:39
  31.1 1.6 %collective-permute-start.11 = (bf16[2,1,2,2,32,1152]{5,4,3,2,1,0:T(8,128)(2,1)S(1)}, bf16[2,1,2,2,32,1152]{5,4,3,2,1,0:T(8,128)(2,1)S(1)}, u32[]{:S(2)}, u32[]{:S(2)}) collective-permute-start(bf16[2,1,2,2,32,1152]{5,4,3,2,1,0:T(8,128)(2,1)S(1)} %pad_maximum_fusion.5), channel_id=1, source_target_pairs={{0,4},{1,3},{2,6},{3,1},{4,0},{5,7},{6,2},{7,5},{8,12},{9,11},{10,... | collective-permute-start | bytes 1769480 | tf_op jit(solution)/shard_map/ppermute | solution.py:39
  32.7 1.1 collective-permute-start.3
  33.8 0.5 collective-permute-done.6
  34.3 2.2 %collective-permute-start.7 = (bf16[1,2,2,2,32,1280]{5,4,3,2,1,0:T(8,128)(2,1)S(1)}, bf16[1,2,2,2,32,1280]{5,4,3,2,1,0:T(8,128)(2,1)S(1)}, u32[]{:S(2)}, u32[]{:S(2)}) collective-permute-start(bf16[1,2,2,2,32,1280]{5,4,3,2,1,0:T(8,128)(2,1)S(1)} %pad_maximum_fusion.4), channel_id=1, source_target_pairs={{0,2},{1,5},{2,0},{3,7},{4,6},{5,1},{6,4},{7,3},{8,10},{9,13},{10,... | collective-permute-start | bytes 1966088 | tf_op jit(solution)/shard_map/ppermute | solution.py:39
  36.5 10.6 %collective-permute-done.11 = bf16[2,1,2,2,32,1152]{5,4,3,2,1,0:T(8,128)(2,1)S(1)} collective-permute-done((bf16[2,1,2,2,32,1152]{5,4,3,2,1,0:T(8,128)(2,1)S(1)}, bf16[2,1,2,2,32,1152]{5,4,3,2,1,0:T(8,128)(2,1)S(1)}, u32[]{:S(2)}, u32[]{:S(2)}) %collective-permute-start.11) | collective-permute-done | bytes 589856 | tf_op jit(solution)/shard_map/ppermute | solution.py:39
  47.2 0.1 pad_maximum_fusion.2
  47.7 1.5 %copy-done = bf16[1,512,3584]{2,1,0:T(8,128)(2,1)S(1)} copy-done((bf16[1,512,3584]{2,1,0:T(8,128)(2,1)S(1)}, bf16[1,512,3584]{2,1,0:T(8,128)(2,1)}, u32[]{:S(2)}) %copy-start) | copy-done | bytes 3670040
  49.2 0.8 fusion.23
  50.0 0.8 fusion.20
  50.9 0.1 pad_maximum_fusion.1
  51.0 0.8 convolution_add_fusion.7
  51.9 0.8 convolution_add_fusion.6
  52.7 0.7 convolution_add_fusion.3
  53.4 0.8 fusion.29
  54.3 0.7 fusion.35
  55.0 0.8 fusion.8
  55.8 0.8 fusion.11
  56.7 1.9 %fusion.33 = f32[512,512]{1,0:T(8,128)S(1)} fusion(bf16[3584,512]{1,0:T(8,128)(2,1)} %collective-permute-done.12, bf16[512,1152]{1,0:T(8,128)(2,1)S(1)} %bitcast.69), kind=kOutput, calls=%fused_computation.47 | convolution fusion | flops 536870912 | bytes 3145728 | tf_op jit(solution)/shard_map/dot_general | solution.py:109
  58.6 2.2 %fusion.16 = f32[512,512]{1,0:T(8,128)S(1)} fusion(bf16[512,1280]{1,0:T(8,128)(2,1)S(1)} %bitcast.83, bf16[3584,512]{1,0:T(8,128)(2,1)} %collective-permute-done.12), kind=kOutput, calls=%fused_computation.25 | convolution fusion | flops 671088640 | bytes 3670016 | tf_op jit(solution)/shard_map/dot_general | solution.py:109
  60.8 2.2 %fusion.6 = f32[512,512]{1,0:T(8,128)S(1)} fusion(f32[512,512]{1,0:T(8,128)S(1)} %fusion.33, f32[512,512]{1,0:T(8,128)S(1)} %fusion.16, bf16[512,1280]{1,0:T(8,128)(2,1)S(1)} %bitcast.54, bf16[3584,512]{1,0:T(8,128)(2,1)} %collective-permute-done.12), kind=kOutput, calls=%fused_computation.13 | convolution fusion | flops 671612928 | bytes 5767168 | tf_op jit(solution)/shard_map/dot_general | solution.py:109
  63.0 0.7 fusion.31
  63.7 0.8 fusion.13
  64.5 1.0 multiply_convert_fusion.1
  65.5 0.9 fusion.3
  66.4 0.9 fusion.2
  67.3 0.7 multiply_convert_fusion
  68.0 1.7 %collective-permute-start.15 = (bf16[2,1,2,2,32,1024]{5,4,3,2,1,0:T(8,128)(2,1)S(1)}, bf16[2,1,2,2,32,1024]{5,4,3,2,1,0:T(8,128)(2,1)S(1)}, u32[]{:S(2)}, u32[]{:S(2)}) collective-permute-start(bf16[2,1,2,2,32,1024]{5,4,3,2,1,0:T(8,128)(2,1)S(1)} %slice.180), channel_id=1, source_target_pairs={{0,4},{1,3},{2,6},{3,1},{4,0},{5,7},{6,2},{7,5},{8,12},{9,11},{10,... | collective-permute-start | bytes 1572872 | tf_op jit(solution)/shard_map/ppermute | solution.py:39
  69.8 0.5 collective-permute-start.19
  70.3 1.1 collective-permute-start.23
  71.4 5.9 %collective-permute-done.15 = bf16[2,1,2,2,32,1024]{5,4,3,2,1,0:T(8,128)(2,1)S(1)} collective-permute-done((bf16[2,1,2,2,32,1024]{5,4,3,2,1,0:T(8,128)(2,1)S(1)}, bf16[2,1,2,2,32,1024]{5,4,3,2,1,0:T(8,128)(2,1)S(1)}, u32[]{:S(2)}, u32[]{:S(2)}) %collective-permute-start.15) | collective-permute-done | bytes 524320 | tf_op jit(solution)/shard_map/ppermute | solution.py:39
  77.3 0.2 add_convert_fusion.2
  77.5 1.1 collective-permute-start.16
  78.6 5.7 %collective-permute-done.19 = bf16[2,1,2,2,32,1280]{5,4,3,2,1,0:T(8,128)(2,1)S(1)} collective-permute-done((bf16[2,1,2,2,32,1280]{5,4,3,2,1,0:T(8,128)(2,1)S(1)}, bf16[2,1,2,2,32,1280]{5,4,3,2,1,0:T(8,128)(2,1)S(1)}, u32[]{:S(2)}, u32[]{:S(2)}) %collective-permute-start.19) | collective-permute-done | bytes 655392 | tf_op jit(solution)/shard_map/ppermute | solution.py:39
  84.3 0.2 add_convert_fusion.1
  84.5 1.7 %collective-permute-start.20 = (bf16[1,1,2,2,32,1280]{5,4,3,2,1,0:T(8,128)(2,1)S(1)}, bf16[1,1,2,2,32,1280]{5,4,3,2,1,0:T(8,128)(2,1)S(1)}, u32[]{:S(2)}, u32[]{:S(2)}) collective-permute-start(bf16[1,1,2,2,32,1280]{5,4,3,2,1,0:T(8,128)(2,1)S(1)} %slice.224), channel_id=1, source_target_pairs={{0,2},{1,5},{2,0},{3,7},{4,6},{5,1},{6,4},{7,3},{8,10},{9,13},{10,... | collective-permute-start | bytes 983048 | tf_op jit(solution)/shard_map/ppermute | solution.py:39
  86.2 6.3 %collective-permute-done.16 = bf16[2,1,1,2,32,1024]{5,4,3,2,1,0:T(8,128)(2,1)S(1)} collective-permute-done((bf16[2,1,1,2,32,1024]{5,4,3,2,1,0:T(8,128)(2,1)S(1)}, bf16[2,1,1,2,32,1024]{5,4,3,2,1,0:T(8,128)(2,1)S(1)}, u32[]{:S(2)}, u32[]{:S(2)}) %collective-permute-start.16) | collective-permute-done | bytes 262176 | tf_op jit(solution)/shard_map/ppermute | solution.py:39
  92.7 1.7 %collective-permute-start.17 = (bf16[1,1,1,2,32,1024]{5,4,3,2,1,0:T(8,128)(2,1)S(1)}, bf16[1,1,1,2,32,1024]{5,4,3,2,1,0:T(8,128)(2,1)S(1)}, u32[]{:S(2)}, u32[]{:S(2)}) collective-permute-start(bf16[1,1,1,2,32,1024]{5,4,3,2,1,0:T(8,128)(2,1)S(1)} %slice.220), channel_id=1, source_target_pairs={{0,2},{1,5},{2,0},{3,7},{4,6},{5,1},{6,4},{7,3},{8,10},{9,13},{10,... | collective-permute-start | bytes 393224 | tf_op jit(solution)/shard_map/ppermute | solution.py:39
  94.4 0.2 add_convert_fusion
  94.6 2.0 %collective-permute-start.24 = (bf16[2,1,1,2,32,1280]{5,4,3,2,1,0:T(8,128)(2,1)S(1)}, bf16[2,1,1,2,32,1280]{5,4,3,2,1,0:T(8,128)(2,1)S(1)}, u32[]{:S(2)}, u32[]{:S(2)}) collective-permute-start(bf16[2,1,1,2,32,1280]{5,4,3,2,1,0:T(8,128)(2,1)S(1)} %slice.230), channel_id=1, source_target_pairs={{0,4},{1,3},{2,6},{3,1},{4,0},{5,7},{6,2},{7,5},{8,12},{9,11},{10,... | collective-permute-start | bytes 983048 | tf_op jit(solution)/shard_map/ppermute | solution.py:39
  96.6 2.2 %collective-permute-done.17 = bf16[1,1,1,2,32,1024]{5,4,3,2,1,0:T(8,128)(2,1)S(1)} collective-permute-done((bf16[1,1,1,2,32,1024]{5,4,3,2,1,0:T(8,128)(2,1)S(1)}, bf16[1,1,1,2,32,1024]{5,4,3,2,1,0:T(8,128)(2,1)S(1)}, u32[]{:S(2)}, u32[]{:S(2)}) %collective-permute-start.17) | collective-permute-done | bytes 131104 | tf_op jit(solution)/shard_map/ppermute | solution.py:39
  98.8 3.0 %collective-permute-start.18 = (bf16[1,1,1,1,32,1024]{5,4,3,2,1,0:T(8,128)(2,1)S(1)}, bf16[1,1,1,1,32,1024]{5,4,3,2,1,0:T(8,128)(2,1)S(1)}, u32[]{:S(2)}, u32[]{:S(2)}) collective-permute-start(bf16[1,1,1,1,32,1024]{5,4,3,2,1,0:T(8,128)(2,1)S(1)} %slice.222), channel_id=1, source_target_pairs={{0,16},{1,17},{2,18},{3,19},{4,20},{5,21},{6,22},{7,23},{8,24},{9,... | collective-permute-start | bytes 196616 | tf_op jit(solution)/shard_map/ppermute | solution.py:39
  102.1 1.9 %collective-permute-start.25 = (bf16[1,1,1,2,32,1280]{5,4,3,2,1,0:T(8,128)(2,1)S(1)}, bf16[1,1,1,2,32,1280]{5,4,3,2,1,0:T(8,128)(2,1)S(1)}, u32[]{:S(2)}, u32[]{:S(2)}) collective-permute-start(bf16[1,1,1,2,32,1280]{5,4,3,2,1,0:T(8,128)(2,1)S(1)} %slice.232), channel_id=1, source_target_pairs={{0,2},{1,5},{2,0},{3,7},{4,6},{5,1},{6,4},{7,3},{8,10},{9,13},{10,... | collective-permute-start | bytes 491528 | tf_op jit(solution)/shard_map/ppermute | solution.py:39
  104.1 2.7 %collective-permute-done.18 = bf16[1,1,1,1,32,1024]{5,4,3,2,1,0:T(8,128)(2,1)S(1)} collective-permute-done((bf16[1,1,1,1,32,1024]{5,4,3,2,1,0:T(8,128)(2,1)S(1)}, bf16[1,1,1,1,32,1024]{5,4,3,2,1,0:T(8,128)(2,1)S(1)}, u32[]{:S(2)}, u32[]{:S(2)}) %collective-permute-start.18) | collective-permute-done | bytes 65568 | tf_op jit(solution)/shard_map/ppermute | solution.py:39
  106.8 3.6 %collective-permute-done.21 = bf16[1,1,2,1,32,1280]{5,4,3,2,1,0:T(8,128)(2,1)S(1)} collective-permute-done((bf16[1,1,2,1,32,1280]{5,4,3,2,1,0:T(8,128)(2,1)S(1)}, bf16[1,1,2,1,32,1280]{5,4,3,2,1,0:T(8,128)(2,1)S(1)}, u32[]{:S(2)}, u32[]{:S(2)}) %collective-permute-start.21) | collective-permute-done | bytes 163872 | tf_op jit(solution)/shard_map/ppermute | solution.py:39
  110.5 2.9 %collective-permute-start.26 = (bf16[1,1,1,1,32,1280]{5,4,3,2,1,0:T(8,128)(2,1)S(1)}, bf16[1,1,1,1,32,1280]{5,4,3,2,1,0:T(8,128)(2,1)S(1)}, u32[]{:S(2)}, u32[]{:S(2)}) collective-permute-start(bf16[1,1,1,1,32,1280]{5,4,3,2,1,0:T(8,128)(2,1)S(1)} %slice.234), channel_id=1, source_target_pairs={{0,16},{1,17},{2,18},{3,19},{4,20},{5,21},{6,22},{7,23},{8,24},{9,... | collective-permute-start | bytes 245768 | tf_op jit(solution)/shard_map/ppermute | solution.py:39
  113.5 1.4 %collective-permute-done.22 = bf16[1,1,1,1,32,1280]{5,4,3,2,1,0:T(8,128)(2,1)S(1)} collective-permute-done((bf16[1,1,1,1,32,1280]{5,4,3,2,1,0:T(8,128)(2,1)S(1)}, bf16[1,1,1,1,32,1280]{5,4,3,2,1,0:T(8,128)(2,1)S(1)}, u32[]{:S(2)}, u32[]{:S(2)}) %collective-permute-start.22) | collective-permute-done | bytes 81952 | tf_op jit(solution)/shard_map/ppermute | solution.py:39
  114.9 1.0 collective-permute-done.26
  116.0 0.7 pad_maximum_fusion.9
  (60 shorter events, 1.7 us)
Async XLA Ops:
  2.0 21.0 %copy-start.2 = (bf16[32,1280]{1,0:T(8,128)(2,1)S(1)}, bf16[32,1280]{1,0:T(8,128)(2,1)}, u32[]{:S(2)}) copy-start(bf16[32,1280]{1,0:T(8,128)(2,1)} %get-tuple-element.15) | copy-start | bytes 245764
  2.0 24.1 %copy-start.1 = (bf16[32,1280]{1,0:T(8,128)(2,1)S(1)}, bf16[32,1280]{1,0:T(8,128)(2,1)}, u32[]{:S(2)}) copy-start(bf16[32,1280]{1,0:T(8,128)(2,1)} %get-tuple-element.18) | copy-start | bytes 245764
  2.0 9.2 %collective-permute-start.8 = (bf16[1,1,1,1,32,1152]{5,4,3,2,1,0:T(8,128)(2,1)}, bf16[1,1,1,1,32,1152]{5,4,3,2,1,0:T(8,128)(2,1)S(1)}, u32[]{:S(2)}, u32[]{:S(2)}) collective-permute-start(bf16[1,1,1,1,32,1152]{5,4,3,2,1,0:T(8,128)(2,1)} %bitcast.85), channel_id=1, source_target_pairs={{0,16},{1,17},{2,18},{3,19},{4,20},{5,21},{6,22},{7,23},{8,24},{9,... | collective-permute-start | bytes 221192 | tf_op jit(solution)/shard_map/ppermute | solution.py:39
  6.0 9.6 %collective-permute-start = (bf16[1,1,1,1,32,1280]{5,4,3,2,1,0:T(8,128)(2,1)}, bf16[1,1,1,1,32,1280]{5,4,3,2,1,0:T(8,128)(2,1)S(1)}, u32[]{:S(2)}, u32[]{:S(2)}) collective-permute-start(bf16[1,1,1,1,32,1280]{5,4,3,2,1,0:T(8,128)(2,1)} %bitcast.76), channel_id=1, source_target_pairs={{0,16},{1,17},{2,18},{3,19},{4,20},{5,21},{6,22},{7,23},{8,24},{9,... | collective-permute-start | bytes 245768 | tf_op jit(solution)/shard_map/ppermute | solution.py:39
  6.1 50.6 %collective-permute-start.12 = (bf16[3584,512]{1,0:T(8,128)(2,1)}, bf16[3584,512]{1,0:T(8,128)(2,1)}, u32[]{:S(2)}, u32[]{:S(2)}) collective-permute-start(bf16[3584,512]{1,0:T(8,128)(2,1)} %bitcast.92), channel_id=1, source_target_pairs={{0,1},{1,0},{2,3},{3,2},{4,5},{5,4},{6,7},{7,6},{8,9},{9,8},{10,11... | collective-permute-start | bytes 11010056 | tf_op jit(solution)/shard_map/ppermute | solution.py:43
  6.1 12.4 %collective-permute-start.4 = (bf16[1,1,1,1,32,1280]{5,4,3,2,1,0:T(8,128)(2,1)}, bf16[1,1,1,1,32,1280]{5,4,3,2,1,0:T(8,128)(2,1)S(1)}, u32[]{:S(2)}, u32[]{:S(2)}) collective-permute-start(bf16[1,1,1,1,32,1280]{5,4,3,2,1,0:T(8,128)(2,1)} %bitcast.71), channel_id=1, source_target_pairs={{0,16},{1,17},{2,18},{3,19},{4,20},{5,21},{6,22},{7,23},{8,24},{9,... | collective-permute-start | bytes 245768 | tf_op jit(solution)/shard_map/ppermute | solution.py:39
  12.1 18.9 %copy-start.3 = (bf16[32,1152]{1,0:T(8,128)(2,1)S(1)}, bf16[32,1152]{1,0:T(8,128)(2,1)}, u32[]{:S(2)}) copy-start(bf16[32,1152]{1,0:T(8,128)(2,1)} %get-tuple-element.19) | copy-start | bytes 221188
  12.1 9.1 %collective-permute-start.9 = (bf16[1,1,1,2,32,1152]{5,4,3,2,1,0:T(8,128)(2,1)S(1)}, bf16[1,1,1,2,32,1152]{5,4,3,2,1,0:T(8,128)(2,1)S(1)}, u32[]{:S(2)}, u32[]{:S(2)}) collective-permute-start(bf16[1,1,1,2,32,1152]{5,4,3,2,1,0:T(8,128)(2,1)S(1)} %pad_maximum_fusion.12), channel_id=1, source_target_pairs={{0,8},{1,9},{2,10},{3,11},{4,12},{5,13},{6,14},{7,15},{8,0},{9,1},... | collective-permute-start | bytes 442376 | tf_op jit(solution)/shard_map/ppermute | solution.py:39
  16.5 6.5 %collective-permute-start.1 = (bf16[1,1,1,2,32,1280]{5,4,3,2,1,0:T(8,128)(2,1)S(1)}, bf16[1,1,1,2,32,1280]{5,4,3,2,1,0:T(8,128)(2,1)S(1)}, u32[]{:S(2)}, u32[]{:S(2)}) collective-permute-start(bf16[1,1,1,2,32,1280]{5,4,3,2,1,0:T(8,128)(2,1)S(1)} %pad_maximum_fusion.10), channel_id=1, source_target_pairs={{0,2},{1,5},{2,0},{3,7},{4,6},{5,1},{6,4},{7,3},{8,10},{9,13},{10,... | collective-permute-start | bytes 491528 | tf_op jit(solution)/shard_map/ppermute | solution.py:39
  18.5 29.1 %copy-start.5 = (bf16[1,3584,512]{2,1,0:T(8,128)(2,1)S(1)}, bf16[1,3584,512]{2,1,0:T(8,128)(2,1)}, u32[]{:S(2)}) copy-start(bf16[1,3584,512]{2,1,0:T(8,128)(2,1)} %param.8) | copy-start | bytes 11010052
  19.6 6.4 %collective-permute-start.5 = (bf16[1,1,1,2,32,1280]{5,4,3,2,1,0:T(8,128)(2,1)S(1)}, bf16[1,1,1,2,32,1280]{5,4,3,2,1,0:T(8,128)(2,1)S(1)}, u32[]{:S(2)}, u32[]{:S(2)}) collective-permute-start(bf16[1,1,1,2,32,1280]{5,4,3,2,1,0:T(8,128)(2,1)S(1)} %pad_maximum_fusion.11), channel_id=1, source_target_pairs={{0,4},{1,3},{2,6},{3,1},{4,0},{5,7},{6,2},{7,5},{8,12},{9,11},{10,... | collective-permute-start | bytes 491528 | tf_op jit(solution)/shard_map/ppermute | solution.py:39
  22.1 8.9 %collective-permute-start.10 = (bf16[1,1,2,2,32,1152]{5,4,3,2,1,0:T(8,128)(2,1)S(1)}, bf16[1,1,2,2,32,1152]{5,4,3,2,1,0:T(8,128)(2,1)S(1)}, u32[]{:S(2)}, u32[]{:S(2)}) collective-permute-start(bf16[1,1,2,2,32,1152]{5,4,3,2,1,0:T(8,128)(2,1)S(1)} %pad_maximum_fusion.8), channel_id=1, source_target_pairs={{0,2},{1,5},{2,0},{3,7},{4,6},{5,1},{6,4},{7,3},{8,10},{9,13},{10,... | collective-permute-start | bytes 884744 | tf_op jit(solution)/shard_map/ppermute | solution.py:39
  23.1 9.6 %collective-permute-start.2 = (bf16[2,1,1,2,32,1280]{5,4,3,2,1,0:T(8,128)(2,1)S(1)}, bf16[2,1,1,2,32,1280]{5,4,3,2,1,0:T(8,128)(2,1)S(1)}, u32[]{:S(2)}, u32[]{:S(2)}) collective-permute-start(bf16[2,1,1,2,32,1280]{5,4,3,2,1,0:T(8,128)(2,1)S(1)} %pad_maximum_fusion.6), channel_id=1, source_target_pairs={{0,4},{1,3},{2,6},{3,1},{4,0},{5,7},{6,2},{7,5},{8,12},{9,11},{10,... | collective-permute-start | bytes 983048 | tf_op jit(solution)/shard_map/ppermute | solution.py:39
  26.1 8.2 %collective-permute-start.6 = (bf16[1,2,1,2,32,1280]{5,4,3,2,1,0:T(8,128)(2,1)S(1)}, bf16[1,2,1,2,32,1280]{5,4,3,2,1,0:T(8,128)(2,1)S(1)}, u32[]{:S(2)}, u32[]{:S(2)}) collective-permute-start(bf16[1,2,1,2,32,1280]{5,4,3,2,1,0:T(8,128)(2,1)S(1)} %pad_maximum_fusion.7), channel_id=1, source_target_pairs={{0,8},{1,9},{2,10},{3,11},{4,12},{5,13},{6,14},{7,15},{8,0},{9,1},... | collective-permute-start | bytes 983048 | tf_op jit(solution)/shard_map/ppermute | solution.py:39
  31.1 16.1 %collective-permute-start.11 = (bf16[2,1,2,2,32,1152]{5,4,3,2,1,0:T(8,128)(2,1)S(1)}, bf16[2,1,2,2,32,1152]{5,4,3,2,1,0:T(8,128)(2,1)S(1)}, u32[]{:S(2)}, u32[]{:S(2)}) collective-permute-start(bf16[2,1,2,2,32,1152]{5,4,3,2,1,0:T(8,128)(2,1)S(1)} %pad_maximum_fusion.5), channel_id=1, source_target_pairs={{0,4},{1,3},{2,6},{3,1},{4,0},{5,7},{6,2},{7,5},{8,12},{9,11},{10,... | collective-permute-start | bytes 1769480 | tf_op jit(solution)/shard_map/ppermute | solution.py:39
  32.6 16.6 %copy-start.4 = (bf16[1,3584,512]{2,1,0:T(8,128)(2,1)S(1)}, bf16[1,3584,512]{2,1,0:T(8,128)(2,1)}, u32[]{:S(2)}) copy-start(bf16[1,3584,512]{2,1,0:T(8,128)(2,1)} %param.7) | copy-start | bytes 11010052
  32.7 14.8 %collective-permute-start.3 = (bf16[2,2,1,2,32,1280]{5,4,3,2,1,0:T(8,128)(2,1)S(1)}, bf16[2,2,1,2,32,1280]{5,4,3,2,1,0:T(8,128)(2,1)S(1)}, u32[]{:S(2)}, u32[]{:S(2)}) collective-permute-start(bf16[2,2,1,2,32,1280]{5,4,3,2,1,0:T(8,128)(2,1)S(1)} %pad_maximum_fusion.3), channel_id=1, source_target_pairs={{0,8},{1,9},{2,10},{3,11},{4,12},{5,13},{6,14},{7,15},{8,0},{9,1},... | collective-permute-start | bytes 1966088 | tf_op jit(solution)/shard_map/ppermute | solution.py:39
  34.3 16.6 %collective-permute-start.7 = (bf16[1,2,2,2,32,1280]{5,4,3,2,1,0:T(8,128)(2,1)S(1)}, bf16[1,2,2,2,32,1280]{5,4,3,2,1,0:T(8,128)(2,1)S(1)}, u32[]{:S(2)}, u32[]{:S(2)}) collective-permute-start(bf16[1,2,2,2,32,1280]{5,4,3,2,1,0:T(8,128)(2,1)S(1)} %pad_maximum_fusion.4), channel_id=1, source_target_pairs={{0,2},{1,5},{2,0},{3,7},{4,6},{5,1},{6,4},{7,3},{8,10},{9,13},{10,... | collective-permute-start | bytes 1966088 | tf_op jit(solution)/shard_map/ppermute | solution.py:39
  47.2 2.0 %copy-start = (bf16[1,512,3584]{2,1,0:T(8,128)(2,1)S(1)}, bf16[1,512,3584]{2,1,0:T(8,128)(2,1)}, u32[]{:S(2)}) copy-start(bf16[1,512,3584]{2,1,0:T(8,128)(2,1)} %param.9) | copy-start | bytes 11010052
  47.6 15.3 %collective-permute-start.13 = (bf16[3584,512]{1,0:T(8,128)(2,1)S(1)}, bf16[3584,512]{1,0:T(8,128)(2,1)S(1)}, u32[]{:S(2)}, u32[]{:S(2)}) collective-permute-start(bf16[3584,512]{1,0:T(8,128)(2,1)S(1)} %bitcast.93), channel_id=1, source_target_pairs={{0,1},{1,0},{2,3},{3,2},{4,5},{5,4},{6,7},{7,6},{8,9},{9,8},{10,11... | collective-permute-start | bytes 11010056 | tf_op jit(solution)/shard_map/ppermute | solution.py:43
  49.2 16.3 %collective-permute-start.14 = (bf16[512,3584]{1,0:T(8,128)(2,1)S(1)}, bf16[512,3584]{1,0:T(8,128)(2,1)S(1)}, u32[]{:S(2)}, u32[]{:S(2)}) collective-permute-start(bf16[512,3584]{1,0:T(8,128)(2,1)S(1)} %bitcast.62), channel_id=1, source_target_pairs={{0,1},{1,0},{2,3},{3,2},{4,5},{5,4},{6,7},{7,6},{8,9},{9,8},{10,11... | collective-permute-start | bytes 11010056 | tf_op jit(solution)/shard_map/ppermute | solution.py:43
  68.0 9.2 %collective-permute-start.15 = (bf16[2,1,2,2,32,1024]{5,4,3,2,1,0:T(8,128)(2,1)S(1)}, bf16[2,1,2,2,32,1024]{5,4,3,2,1,0:T(8,128)(2,1)S(1)}, u32[]{:S(2)}, u32[]{:S(2)}) collective-permute-start(bf16[2,1,2,2,32,1024]{5,4,3,2,1,0:T(8,128)(2,1)S(1)} %slice.180), channel_id=1, source_target_pairs={{0,4},{1,3},{2,6},{3,1},{4,0},{5,7},{6,2},{7,5},{8,12},{9,11},{10,... | collective-permute-start | bytes 1572872 | tf_op jit(solution)/shard_map/ppermute | solution.py:39
  69.8 14.6 %collective-permute-start.19 = (bf16[2,1,2,2,32,1280]{5,4,3,2,1,0:T(8,128)(2,1)S(1)}, bf16[2,1,2,2,32,1280]{5,4,3,2,1,0:T(8,128)(2,1)S(1)}, u32[]{:S(2)}, u32[]{:S(2)}) collective-permute-start(bf16[2,1,2,2,32,1280]{5,4,3,2,1,0:T(8,128)(2,1)S(1)} %slice.188), channel_id=1, source_target_pairs={{0,4},{1,3},{2,6},{3,1},{4,0},{5,7},{6,2},{7,5},{8,12},{9,11},{10,... | collective-permute-start | bytes 1966088 | tf_op jit(solution)/shard_map/ppermute | solution.py:39
  70.3 24.1 %collective-permute-start.23 = (bf16[2,2,1,2,32,1280]{5,4,3,2,1,0:T(8,128)(2,1)S(1)}, bf16[2,2,1,2,32,1280]{5,4,3,2,1,0:T(8,128)(2,1)S(1)}, u32[]{:S(2)}, u32[]{:S(2)}) collective-permute-start(bf16[2,2,1,2,32,1280]{5,4,3,2,1,0:T(8,128)(2,1)S(1)} %slice.196), channel_id=1, source_target_pairs={{0,8},{1,9},{2,10},{3,11},{4,12},{5,13},{6,14},{7,15},{8,0},{9,1},... | collective-permute-start | bytes 1966088 | tf_op jit(solution)/shard_map/ppermute | solution.py:39
  77.5 15.0 %collective-permute-start.16 = (bf16[2,1,1,2,32,1024]{5,4,3,2,1,0:T(8,128)(2,1)S(1)}, bf16[2,1,1,2,32,1024]{5,4,3,2,1,0:T(8,128)(2,1)S(1)}, u32[]{:S(2)}, u32[]{:S(2)}) collective-permute-start(bf16[2,1,1,2,32,1024]{5,4,3,2,1,0:T(8,128)(2,1)S(1)} %slice.218), channel_id=1, source_target_pairs={{0,8},{1,9},{2,10},{3,11},{4,12},{5,13},{6,14},{7,15},{8,0},{9,1},... | collective-permute-start | bytes 786440 | tf_op jit(solution)/shard_map/ppermute | solution.py:39
  84.5 17.3 %collective-permute-start.20 = (bf16[1,1,2,2,32,1280]{5,4,3,2,1,0:T(8,128)(2,1)S(1)}, bf16[1,1,2,2,32,1280]{5,4,3,2,1,0:T(8,128)(2,1)S(1)}, u32[]{:S(2)}, u32[]{:S(2)}) collective-permute-start(bf16[1,1,2,2,32,1280]{5,4,3,2,1,0:T(8,128)(2,1)S(1)} %slice.224), channel_id=1, source_target_pairs={{0,2},{1,5},{2,0},{3,7},{4,6},{5,1},{6,4},{7,3},{8,10},{9,13},{10,... | collective-permute-start | bytes 983048 | tf_op jit(solution)/shard_map/ppermute | solution.py:39
  92.7 6.1 %collective-permute-start.17 = (bf16[1,1,1,2,32,1024]{5,4,3,2,1,0:T(8,128)(2,1)S(1)}, bf16[1,1,1,2,32,1024]{5,4,3,2,1,0:T(8,128)(2,1)S(1)}, u32[]{:S(2)}, u32[]{:S(2)}) collective-permute-start(bf16[1,1,1,2,32,1024]{5,4,3,2,1,0:T(8,128)(2,1)S(1)} %slice.220), channel_id=1, source_target_pairs={{0,2},{1,5},{2,0},{3,7},{4,6},{5,1},{6,4},{7,3},{8,10},{9,13},{10,... | collective-permute-start | bytes 393224 | tf_op jit(solution)/shard_map/ppermute | solution.py:39
  94.6 7.4 %collective-permute-start.24 = (bf16[2,1,1,2,32,1280]{5,4,3,2,1,0:T(8,128)(2,1)S(1)}, bf16[2,1,1,2,32,1280]{5,4,3,2,1,0:T(8,128)(2,1)S(1)}, u32[]{:S(2)}, u32[]{:S(2)}) collective-permute-start(bf16[2,1,1,2,32,1280]{5,4,3,2,1,0:T(8,128)(2,1)S(1)} %slice.230), channel_id=1, source_target_pairs={{0,4},{1,3},{2,6},{3,1},{4,0},{5,7},{6,2},{7,5},{8,12},{9,11},{10,... | collective-permute-start | bytes 983048 | tf_op jit(solution)/shard_map/ppermute | solution.py:39
  98.8 7.9 %collective-permute-start.18 = (bf16[1,1,1,1,32,1024]{5,4,3,2,1,0:T(8,128)(2,1)S(1)}, bf16[1,1,1,1,32,1024]{5,4,3,2,1,0:T(8,128)(2,1)S(1)}, u32[]{:S(2)}, u32[]{:S(2)}) collective-permute-start(bf16[1,1,1,1,32,1024]{5,4,3,2,1,0:T(8,128)(2,1)S(1)} %slice.222), channel_id=1, source_target_pairs={{0,16},{1,17},{2,18},{3,19},{4,20},{5,21},{6,22},{7,23},{8,24},{9,... | collective-permute-start | bytes 196616 | tf_op jit(solution)/shard_map/ppermute | solution.py:39
  101.9 8.4 %collective-permute-start.21 = (bf16[1,1,2,1,32,1280]{5,4,3,2,1,0:T(8,128)(2,1)S(1)}, bf16[1,1,2,1,32,1280]{5,4,3,2,1,0:T(8,128)(2,1)S(1)}, u32[]{:S(2)}, u32[]{:S(2)}) collective-permute-start(bf16[1,1,2,1,32,1280]{5,4,3,2,1,0:T(8,128)(2,1)S(1)} %slice.226), channel_id=1, source_target_pairs={{0,16},{1,17},{2,18},{3,19},{4,20},{5,21},{6,22},{7,23},{8,24},{9,... | collective-permute-start | bytes 491528 | tf_op jit(solution)/shard_map/ppermute | solution.py:39
  102.1 8.4 %collective-permute-start.25 = (bf16[1,1,1,2,32,1280]{5,4,3,2,1,0:T(8,128)(2,1)S(1)}, bf16[1,1,1,2,32,1280]{5,4,3,2,1,0:T(8,128)(2,1)S(1)}, u32[]{:S(2)}, u32[]{:S(2)}) collective-permute-start(bf16[1,1,1,2,32,1280]{5,4,3,2,1,0:T(8,128)(2,1)S(1)} %slice.232), channel_id=1, source_target_pairs={{0,2},{1,5},{2,0},{3,7},{4,6},{5,1},{6,4},{7,3},{8,10},{9,13},{10,... | collective-permute-start | bytes 491528 | tf_op jit(solution)/shard_map/ppermute | solution.py:39
  110.4 4.5 %collective-permute-start.22 = (bf16[1,1,1,1,32,1280]{5,4,3,2,1,0:T(8,128)(2,1)S(1)}, bf16[1,1,1,1,32,1280]{5,4,3,2,1,0:T(8,128)(2,1)S(1)}, u32[]{:S(2)}, u32[]{:S(2)}) collective-permute-start(bf16[1,1,1,1,32,1280]{5,4,3,2,1,0:T(8,128)(2,1)S(1)} %slice.228), channel_id=1, source_target_pairs={{0,8},{1,9},{2,10},{3,11},{4,12},{5,13},{6,14},{7,15},{8,0},{9,1},... | collective-permute-start | bytes 245768 | tf_op jit(solution)/shard_map/ppermute | solution.py:39
  110.5 5.4 %collective-permute-start.26 = (bf16[1,1,1,1,32,1280]{5,4,3,2,1,0:T(8,128)(2,1)S(1)}, bf16[1,1,1,1,32,1280]{5,4,3,2,1,0:T(8,128)(2,1)S(1)}, u32[]{:S(2)}, u32[]{:S(2)}) collective-permute-start(bf16[1,1,1,1,32,1280]{5,4,3,2,1,0:T(8,128)(2,1)S(1)} %slice.234), channel_id=1, source_target_pairs={{0,16},{1,17},{2,18},{3,19},{4,20},{5,21},{6,22},{7,23},{8,24},{9,... | collective-permute-start | bytes 245768 | tf_op jit(solution)/shard_map/ppermute | solution.py:39

commit v4 on v3

--- a/solution.py
+++ b/solution.py
@@ -20,7 +20,7 @@
     bits = experts.bit_length() - 1
     if experts == 16:
         gather = (((3, 0, 1, 2), 5), ((3, 1, 2, 0), 5), ((3, 2, 0, 1), 4))
-        reduce = (((3, 0, 2, 1), 4), ((2, 3, 0, 1), 5), ((3, 0, 1, 2), 5))
+        reduce = (((3, 1, 2, 0), 5), ((3, 2, 0, 1), 5), ((3, 0, 1, 2), 4))
         mirror = (1, 0, 2, 3)
     else:
         turns = range(0, bits, max(1, bits // 4))
@@ -80,7 +80,7 @@
     rows = experts * tok_rows
 
     own = [w[0] for w in (gate_weight, up_weight, down_weight)]
-    far = [other_core(w) for w in own[:1]]
+    far = []
 
     held = [
         piece.reshape((1,) * bits + piece.shape)
@@ -90,6 +90,9 @@
         for i, (order, _) in enumerate(gather):
             axis = order[step]
             held[i] = jnp.concatenate([held[i], cross(held[i], axis, experts, mirror)], axis=axis)
+        if step == bits - 2:
+            held[0], near = lax.optimization_barrier((held[0], own[0]))
+            far.append(other_core(near))
     held = [piece.reshape(rows, -1) for piece in held]
     held[0], near = lax.optimization_barrier((held[0], own[1]))
     far.append(other_core(near))

time: 117 us -> 109 us (0.932)
  matrix products: 18.5 us -> 14.7 us
  waiting for transfers between devices: 45.7 us -> 43.8 us
  starting transfers between devices: 42.1 us -> 40.8 us
    dot_general x12, matrix products: 13.7 us -> 9.88 us  [project(): jnp.dot(held[i][:, :width], matrix[start:start + width], preferred_elemen...]
    ppermute x24, waiting for transfers between devices: 45.7 us -> 43.8 us  [cross(): return lax.ppermute(block, ('expert', 'sub'), pairs)]
    ppermute x24, starting transfers between devices: 42 us -> 40.2 us  [cross(): return lax.ppermute(block, ('expert', 'sub'), pairs)]
  transfers between devices with their start and end apart: 27 -> 27, of which waited for: 15 -> 16; matrix products, arithmetic and copies ran while one was open for 19% -> 16% of each run, Pallas kernels for 0% -> 0%
where the time goes in v4:
time: 109 us
  waiting for transfers between devices  43.8 us (40%)
  starting transfers between devices  40.8 us (37%)
  matrix products  14.7 us (13%)
  other arithmetic  6.05 us (6%)
  Pallas kernels  1.98 us (2%)
    ppermute x24, waiting for transfers between devices, cross(): return lax.ppermute(block, ('expert', 'sub'), pairs)  43.8 us
    ppermute x24, starting transfers between devices, cross(): return lax.ppermute(block, ('expert', 'sub'), pairs)  40.2 us
    dot_general x12, matrix products, project(): jnp.dot(held[i][:, :width], matrix[start:start + width], preferred_elemen...  9.88 us
    dot_general x6, matrix products, per_device(): jnp.dot(h, w[2][:, start:start + width], preferred_element_type=jnp.float32)  4.85 us
    concatenate x12, other arithmetic, per_device(): jnp.concatenate([held[i], cross(held[i], axis, experts, mirror)], axis=axis)  4.32 us
  transfers between devices with their start and end apart: 27, of which 16 were waited for; matrix products, arithmetic and copies ran while one was open for 16% of the time, Pallas kernels for 0%

profile of v4, /device:TPU:0, one launch (start us, length us, event | category | flops | bytes accessed | tf_op | source)
XLA Modules:
  0.0 108.6 jit_solution(773969216904513386)
XLA Ops:
  0.0 2.0 %shard_map.64 = (bf16[32,1280]{1,0:T(8,128)(2,1)}, bf16[32,1280]{1,0:T(8,128)(2,1)}, bf16[32,1152]{1,0:T(8,128)(2,1)}) custom-call(bf16[32,3584]{1,0:T(8,128)(2,1)} %tokens_ref.1, s32[8,32]{1,0:T(8,128)} %bitcast.89, s32[8,32]{1,0:T(8,128)} %bitcast.90), custom_call_target="tpu_custom_call" | custom-call | tf_op jit(solution)/shard_map/pallas_call | solution.py:67
  2.0 4.0 %collective-permute-start.8 = (bf16[1,1,1,1,32,1152]{5,4,3,2,1,0:T(8,128)(2,1)}, bf16[1,1,1,1,32,1152]{5,4,3,2,1,0:T(8,128)(2,1)S(1)}, u32[]{:S(2)}, u32[]{:S(2)}) collective-permute-start(bf16[1,1,1,1,32,1152]{5,4,3,2,1,0:T(8,128)(2,1)} %bitcast.80), channel_id=1, source_target_pairs={{0,16},{1,17},{2,18},{3,19},{4,20},{5,21},{6,22},{7,23},{8,24},{9,... | collective-permute-start | bytes 221192 | tf_op jit(solution)/shard_map/ppermute | solution.py:39
  6.1 2.9 %collective-permute-start.4 = (bf16[1,1,1,1,32,1280]{5,4,3,2,1,0:T(8,128)(2,1)}, bf16[1,1,1,1,32,1280]{5,4,3,2,1,0:T(8,128)(2,1)S(1)}, u32[]{:S(2)}, u32[]{:S(2)}) collective-permute-start(bf16[1,1,1,1,32,1280]{5,4,3,2,1,0:T(8,128)(2,1)} %bitcast.71), channel_id=1, source_target_pairs={{0,16},{1,17},{2,18},{3,19},{4,20},{5,21},{6,22},{7,23},{8,24},{9,... | collective-permute-start | bytes 245768 | tf_op jit(solution)/shard_map/ppermute | solution.py:39
  8.9 4.9 %collective-permute-done.8 = bf16[1,1,1,1,32,1152]{5,4,3,2,1,0:T(8,128)(2,1)S(1)} collective-permute-done((bf16[1,1,1,1,32,1152]{5,4,3,2,1,0:T(8,128)(2,1)}, bf16[1,1,1,1,32,1152]{5,4,3,2,1,0:T(8,128)(2,1)S(1)}, u32[]{:S(2)}, u32[]{:S(2)}) %collective-permute-start.8) | collective-permute-done | bytes 73760 | tf_op jit(solution)/shard_map/ppermute | solution.py:39
  13.8 0.9 pad_maximum_fusion.12
  14.7 0.8 collective-permute-start.9
  15.6 0.9 pad_maximum_fusion.10
  16.5 2.0 %collective-permute-start.1 = (bf16[1,1,1,2,32,1280]{5,4,3,2,1,0:T(8,128)(2,1)S(1)}, bf16[1,1,1,2,32,1280]{5,4,3,2,1,0:T(8,128)(2,1)S(1)}, u32[]{:S(2)}, u32[]{:S(2)}) collective-permute-start(bf16[1,1,1,2,32,1280]{5,4,3,2,1,0:T(8,128)(2,1)S(1)} %pad_maximum_fusion.10), channel_id=1, source_target_pairs={{0,2},{1,5},{2,0},{3,7},{4,6},{5,1},{6,4},{7,3},{8,10},{9,13},{10,... | collective-permute-start | bytes 491528 | tf_op jit(solution)/shard_map/ppermute | solution.py:39
  18.5 0.9 pad_maximum_fusion.11
  19.4 1.6 %collective-permute-start.5 = (bf16[1,1,1,2,32,1280]{5,4,3,2,1,0:T(8,128)(2,1)S(1)}, bf16[1,1,1,2,32,1280]{5,4,3,2,1,0:T(8,128)(2,1)S(1)}, u32[]{:S(2)}, u32[]{:S(2)}) collective-permute-start(bf16[1,1,1,2,32,1280]{5,4,3,2,1,0:T(8,128)(2,1)S(1)} %pad_maximum_fusion.11), channel_id=1, source_target_pairs={{0,4},{1,3},{2,6},{3,1},{4,0},{5,7},{6,2},{7,5},{8,12},{9,11},{10,... | collective-permute-start | bytes 491528 | tf_op jit(solution)/shard_map/ppermute | solution.py:39
  21.0 0.9 pad_maximum_fusion.8
  21.9 1.1 collective-permute-start.10
  23.1 2.7 %collective-permute-start.2 = (bf16[2,1,1,2,32,1280]{5,4,3,2,1,0:T(8,128)(2,1)S(1)}, bf16[2,1,1,2,32,1280]{5,4,3,2,1,0:T(8,128)(2,1)S(1)}, u32[]{:S(2)}, u32[]{:S(2)}) collective-permute-start(bf16[2,1,1,2,32,1280]{5,4,3,2,1,0:T(8,128)(2,1)S(1)} %pad_maximum_fusion.6), channel_id=1, source_target_pairs={{0,4},{1,3},{2,6},{3,1},{4,0},{5,7},{6,2},{7,5},{8,12},{9,11},{10,... | collective-permute-start | bytes 983048 | tf_op jit(solution)/shard_map/ppermute | solution.py:39
  25.7 0.6 collective-permute-done.5
  26.4 1.5 %collective-permute-start.6 = (bf16[1,2,1,2,32,1280]{5,4,3,2,1,0:T(8,128)(2,1)S(1)}, bf16[1,2,1,2,32,1280]{5,4,3,2,1,0:T(8,128)(2,1)S(1)}, u32[]{:S(2)}, u32[]{:S(2)}) collective-permute-start(bf16[1,2,1,2,32,1280]{5,4,3,2,1,0:T(8,128)(2,1)S(1)} %pad_maximum_fusion.7), channel_id=1, source_target_pairs={{0,8},{1,9},{2,10},{3,11},{4,12},{5,13},{6,14},{7,15},{8,0},{9,1},... | collective-permute-start | bytes 983048 | tf_op jit(solution)/shard_map/ppermute | solution.py:39
  27.9 2.9 %collective-permute-done.10 = bf16[1,1,2,2,32,1152]{5,4,3,2,1,0:T(8,128)(2,1)S(1)} collective-permute-done((bf16[1,1,2,2,32,1152]{5,4,3,2,1,0:T(8,128)(2,1)S(1)}, bf16[1,1,2,2,32,1152]{5,4,3,2,1,0:T(8,128)(2,1)S(1)}, u32[]{:S(2)}, u32[]{:S(2)}) %collective-permute-start.10) | collective-permute-done | bytes 294944 | tf_op jit(solution)/shard_map/ppermute | solution.py:39
  30.9 1.7 %collective-permute-start.11 = (bf16[2,1,2,2,32,1152]{5,4,3,2,1,0:T(8,128)(2,1)S(1)}, bf16[2,1,2,2,32,1152]{5,4,3,2,1,0:T(8,128)(2,1)S(1)}, u32[]{:S(2)}, u32[]{:S(2)}) collective-permute-start(bf16[2,1,2,2,32,1152]{5,4,3,2,1,0:T(8,128)(2,1)S(1)} %pad_maximum_fusion.5), channel_id=1, source_target_pairs={{0,4},{1,3},{2,6},{3,1},{4,0},{5,7},{6,2},{7,5},{8,12},{9,11},{10,... | collective-permute-start | bytes 1769480 | tf_op jit(solution)/shard_map/ppermute | solution.py:39
  32.6 0.9 collective-permute-start.3
  33.6 0.9 collective-permute-done.6
  34.5 2.0 %collective-permute-start.7 = (bf16[1,2,2,2,32,1280]{5,4,3,2,1,0:T(8,128)(2,1)S(1)}, bf16[1,2,2,2,32,1280]{5,4,3,2,1,0:T(8,128)(2,1)S(1)}, u32[]{:S(2)}, u32[]{:S(2)}) collective-permute-start(bf16[1,2,2,2,32,1280]{5,4,3,2,1,0:T(8,128)(2,1)S(1)} %pad_maximum_fusion.4), channel_id=1, source_target_pairs={{0,2},{1,5},{2,0},{3,7},{4,6},{5,1},{6,4},{7,3},{8,10},{9,13},{10,... | collective-permute-start | bytes 1966088 | tf_op jit(solution)/shard_map/ppermute | solution.py:39
  36.5 8.3 %collective-permute-done.11 = bf16[2,1,2,2,32,1152]{5,4,3,2,1,0:T(8,128)(2,1)S(1)} collective-permute-done((bf16[2,1,2,2,32,1152]{5,4,3,2,1,0:T(8,128)(2,1)S(1)}, bf16[2,1,2,2,32,1152]{5,4,3,2,1,0:T(8,128)(2,1)S(1)}, u32[]{:S(2)}, u32[]{:S(2)}) %collective-permute-start.11) | collective-permute-done | bytes 589856 | tf_op jit(solution)/shard_map/ppermute | solution.py:39
  45.1 2.5 %collective-permute-done.3 = bf16[2,2,1,2,32,1280]{5,4,3,2,1,0:T(8,128)(2,1)S(1)} collective-permute-done((bf16[2,2,1,2,32,1280]{5,4,3,2,1,0:T(8,128)(2,1)S(1)}, bf16[2,2,1,2,32,1280]{5,4,3,2,1,0:T(8,128)(2,1)S(1)}, u32[]{:S(2)}, u32[]{:S(2)}) %collective-permute-start.3) | collective-permute-done | bytes 655392 | tf_op jit(solution)/shard_map/ppermute | solution.py:39
  47.8 0.5 collective-permute-start.14
  48.3 0.8 fusion.23
  49.2 0.6 copy-done.5
  49.8 0.8 fusion.20
  50.8 0.8 convolution_add_fusion.7
  51.6 0.8 convolution_add_fusion.6
  52.4 0.7 convolution_add_fusion.3
  53.2 0.8 fusion.29
  54.0 0.7 fusion.31
  54.7 0.9 fusion.8
  55.6 0.9 fusion.17
  56.5 0.7 fusion.35
  57.2 0.8 fusion.14
  58.0 0.9 fusion.6
  58.9 0.7 fusion.33
  59.6 0.8 fusion.11
  60.5 1.0 multiply_convert_fusion.1
  61.5 0.7 multiply_convert_fusion
  62.2 0.9 fusion.3
  63.1 0.9 fusion.2
  64.0 1.5 %collective-permute-start.23 = (bf16[2,2,1,2,32,1024]{5,4,3,2,1,0:T(8,128)(2,1)S(1)}, bf16[2,2,1,2,32,1024]{5,4,3,2,1,0:T(8,128)(2,1)S(1)}, u32[]{:S(2)}, u32[]{:S(2)}) collective-permute-start(bf16[2,2,1,2,32,1024]{5,4,3,2,1,0:T(8,128)(2,1)S(1)} %slice.196), channel_id=1, source_target_pairs={{0,8},{1,9},{2,10},{3,11},{4,12},{5,13},{6,14},{7,15},{8,0},{9,1},... | collective-permute-start | bytes 1572872 | tf_op jit(solution)/shard_map/ppermute | solution.py:39
  65.5 1.7 %collective-permute-start.15 = (bf16[1,2,2,2,32,1280]{5,4,3,2,1,0:T(8,128)(2,1)S(1)}, bf16[1,2,2,2,32,1280]{5,4,3,2,1,0:T(8,128)(2,1)S(1)}, u32[]{:S(2)}, u32[]{:S(2)}) collective-permute-start(bf16[1,2,2,2,32,1280]{5,4,3,2,1,0:T(8,128)(2,1)S(1)} %slice.180), channel_id=1, source_target_pairs={{0,2},{1,5},{2,0},{3,7},{4,6},{5,1},{6,4},{7,3},{8,10},{9,13},{10,... | collective-permute-start | bytes 1966088 | tf_op jit(solution)/shard_map/ppermute | solution.py:39
  67.3 0.9 collective-permute-start.19
  68.3 9.6 %collective-permute-done.23 = bf16[2,2,1,2,32,1024]{5,4,3,2,1,0:T(8,128)(2,1)S(1)} collective-permute-done((bf16[2,2,1,2,32,1024]{5,4,3,2,1,0:T(8,128)(2,1)S(1)}, bf16[2,2,1,2,32,1024]{5,4,3,2,1,0:T(8,128)(2,1)S(1)}, u32[]{:S(2)}, u32[]{:S(2)}) %collective-permute-start.23) | collective-permute-done | bytes 524320 | tf_op jit(solution)/shard_map/ppermute | solution.py:39
  78.1 2.0 %collective-permute-start.24 = (bf16[2,1,1,2,32,1024]{5,4,3,2,1,0:T(8,128)(2,1)S(1)}, bf16[2,1,1,2,32,1024]{5,4,3,2,1,0:T(8,128)(2,1)S(1)}, u32[]{:S(2)}, u32[]{:S(2)}) collective-permute-start(bf16[2,1,1,2,32,1024]{5,4,3,2,1,0:T(8,128)(2,1)S(1)} %slice.230), channel_id=1, source_target_pairs={{0,4},{1,3},{2,6},{3,1},{4,0},{5,7},{6,2},{7,5},{8,12},{9,11},{10,... | collective-permute-start | bytes 786440 | tf_op jit(solution)/shard_map/ppermute | solution.py:39
  80.1 3.1 %collective-permute-done.15 = bf16[1,2,2,2,32,1280]{5,4,3,2,1,0:T(8,128)(2,1)S(1)} collective-permute-done((bf16[1,2,2,2,32,1280]{5,4,3,2,1,0:T(8,128)(2,1)S(1)}, bf16[1,2,2,2,32,1280]{5,4,3,2,1,0:T(8,128)(2,1)S(1)}, u32[]{:S(2)}, u32[]{:S(2)}) %collective-permute-start.15) | collective-permute-done | bytes 655392 | tf_op jit(solution)/shard_map/ppermute | solution.py:39
  83.4 0.2 collective-permute-start.16
  83.6 1.2 %collective-permute-done.24 = bf16[2,1,1,2,32,1024]{5,4,3,2,1,0:T(8,128)(2,1)S(1)} collective-permute-done((bf16[2,1,1,2,32,1024]{5,4,3,2,1,0:T(8,128)(2,1)S(1)}, bf16[2,1,1,2,32,1024]{5,4,3,2,1,0:T(8,128)(2,1)S(1)}, u32[]{:S(2)}, u32[]{:S(2)}) %collective-permute-start.24) | collective-permute-done | bytes 262176 | tf_op jit(solution)/shard_map/ppermute | solution.py:39
  84.9 1.7 %collective-permute-start.25 = (bf16[1,1,1,2,32,1024]{5,4,3,2,1,0:T(8,128)(2,1)S(1)}, bf16[1,1,1,2,32,1024]{5,4,3,2,1,0:T(8,128)(2,1)S(1)}, u32[]{:S(2)}, u32[]{:S(2)}) collective-permute-start(bf16[1,1,1,2,32,1024]{5,4,3,2,1,0:T(8,128)(2,1)S(1)} %slice.232), channel_id=1, source_target_pairs={{0,2},{1,5},{2,0},{3,7},{4,6},{5,1},{6,4},{7,3},{8,10},{9,13},{10,... | collective-permute-start | bytes 393224 | tf_op jit(solution)/shard_map/ppermute | solution.py:39
  86.8 0.4 collective-permute-start.20
  87.2 2.7 %collective-permute-done.25 = bf16[1,1,1,2,32,1024]{5,4,3,2,1,0:T(8,128)(2,1)S(1)} collective-permute-done((bf16[1,1,1,2,32,1024]{5,4,3,2,1,0:T(8,128)(2,1)S(1)}, bf16[1,1,1,2,32,1024]{5,4,3,2,1,0:T(8,128)(2,1)S(1)}, u32[]{:S(2)}, u32[]{:S(2)}) %collective-permute-start.25) | collective-permute-done | bytes 131104 | tf_op jit(solution)/shard_map/ppermute | solution.py:39
  90.0 2.9 %collective-permute-start.26 = (bf16[1,1,1,1,32,1024]{5,4,3,2,1,0:T(8,128)(2,1)S(1)}, bf16[1,1,1,1,32,1024]{5,4,3,2,1,0:T(8,128)(2,1)S(1)}, u32[]{:S(2)}, u32[]{:S(2)}) collective-permute-start(bf16[1,1,1,1,32,1024]{5,4,3,2,1,0:T(8,128)(2,1)S(1)} %slice.234), channel_id=1, source_target_pairs={{0,16},{1,17},{2,18},{3,19},{4,20},{5,21},{6,22},{7,23},{8,24},{9,... | collective-permute-start | bytes 196616 | tf_op jit(solution)/shard_map/ppermute | solution.py:39
  93.0 1.4 %collective-permute-start.17 = (bf16[1,1,1,2,32,1280]{5,4,3,2,1,0:T(8,128)(2,1)S(1)}, bf16[1,1,1,2,32,1280]{5,4,3,2,1,0:T(8,128)(2,1)S(1)}, u32[]{:S(2)}, u32[]{:S(2)}) collective-permute-start(bf16[1,1,1,2,32,1280]{5,4,3,2,1,0:T(8,128)(2,1)S(1)} %slice.220), channel_id=1, source_target_pairs={{0,4},{1,3},{2,6},{3,1},{4,0},{5,7},{6,2},{7,5},{8,12},{9,11},{10,... | collective-permute-start | bytes 491528 | tf_op jit(solution)/shard_map/ppermute | solution.py:39
  94.5 1.0 collective-permute-start.21
  95.5 1.0 collective-permute-done.26
  96.6 1.8 %collective-permute-done.17 = bf16[1,1,1,2,32,1280]{5,4,3,2,1,0:T(8,128)(2,1)S(1)} collective-permute-done((bf16[1,1,1,2,32,1280]{5,4,3,2,1,0:T(8,128)(2,1)S(1)}, bf16[1,1,1,2,32,1280]{5,4,3,2,1,0:T(8,128)(2,1)S(1)}, u32[]{:S(2)}, u32[]{:S(2)}) %collective-permute-start.17) | collective-permute-done | bytes 163872 | tf_op jit(solution)/shard_map/ppermute | solution.py:39
  98.4 0.9 collective-permute-start.18
  99.3 0.9 collective-permute-done.21
  100.2 4.3 %collective-permute-start.22 = (bf16[1,1,1,1,32,1280]{5,4,3,2,1,0:T(8,128)(2,1)S(1)}, bf16[1,1,1,1,32,1280]{5,4,3,2,1,0:T(8,128)(2,1)S(1)}, u32[]{:S(2)}, u32[]{:S(2)}) collective-permute-start(bf16[1,1,1,1,32,1280]{5,4,3,2,1,0:T(8,128)(2,1)S(1)} %slice.228), channel_id=1, source_target_pairs={{0,16},{1,17},{2,18},{3,19},{4,20},{5,21},{6,22},{7,23},{8,24},{9,... | collective-permute-start | bytes 245768 | tf_op jit(solution)/shard_map/ppermute | solution.py:39
  104.5 1.7 %collective-permute-done.18 = bf16[1,1,1,1,32,1280]{5,4,3,2,1,0:T(8,128)(2,1)S(1)} collective-permute-done((bf16[1,1,1,1,32,1280]{5,4,3,2,1,0:T(8,128)(2,1)S(1)}, bf16[1,1,1,1,32,1280]{5,4,3,2,1,0:T(8,128)(2,1)S(1)}, u32[]{:S(2)}, u32[]{:S(2)}) %collective-permute-start.18) | collective-permute-done | bytes 81952 | tf_op jit(solution)/shard_map/ppermute | solution.py:39
  106.2 1.7 %collective-permute-done.22 = bf16[1,1,1,1,32,1280]{5,4,3,2,1,0:T(8,128)(2,1)S(1)} collective-permute-done((bf16[1,1,1,1,32,1280]{5,4,3,2,1,0:T(8,128)(2,1)S(1)}, bf16[1,1,1,1,32,1280]{5,4,3,2,1,0:T(8,128)(2,1)S(1)}, u32[]{:S(2)}, u32[]{:S(2)}) %collective-permute-start.22) | collective-permute-done | bytes 81952 | tf_op jit(solution)/shard_map/ppermute | solution.py:39
  107.9 0.7 pad_maximum_fusion.9
  (60 shorter events, 2.3 us)
Async XLA Ops:
  2.0 21.0 %copy-start.3 = (bf16[32,1280]{1,0:T(8,128)(2,1)S(1)}, bf16[32,1280]{1,0:T(8,128)(2,1)}, u32[]{:S(2)}) copy-start(bf16[32,1280]{1,0:T(8,128)(2,1)} %get-tuple-element.17) | copy-start | bytes 245764
  2.0 24.4 %copy-start.1 = (bf16[32,1280]{1,0:T(8,128)(2,1)S(1)}, bf16[32,1280]{1,0:T(8,128)(2,1)}, u32[]{:S(2)}) copy-start(bf16[32,1280]{1,0:T(8,128)(2,1)} %get-tuple-element.21) | copy-start | bytes 245764
  2.0 11.8 %collective-permute-start.8 = (bf16[1,1,1,1,32,1152]{5,4,3,2,1,0:T(8,128)(2,1)}, bf16[1,1,1,1,32,1152]{5,4,3,2,1,0:T(8,128)(2,1)S(1)}, u32[]{:S(2)}, u32[]{:S(2)}) collective-permute-start(bf16[1,1,1,1,32,1152]{5,4,3,2,1,0:T(8,128)(2,1)} %bitcast.80), channel_id=1, source_target_pairs={{0,16},{1,17},{2,18},{3,19},{4,20},{5,21},{6,22},{7,23},{8,24},{9,... | collective-permute-start | bytes 221192 | tf_op jit(solution)/shard_map/ppermute | solution.py:39
  6.0 9.6 %collective-permute-start = (bf16[1,1,1,1,32,1280]{5,4,3,2,1,0:T(8,128)(2,1)}, bf16[1,1,1,1,32,1280]{5,4,3,2,1,0:T(8,128)(2,1)S(1)}, u32[]{:S(2)}, u32[]{:S(2)}) collective-permute-start(bf16[1,1,1,1,32,1280]{5,4,3,2,1,0:T(8,128)(2,1)} %bitcast.85), channel_id=1, source_target_pairs={{0,16},{1,17},{2,18},{3,19},{4,20},{5,21},{6,22},{7,23},{8,24},{9,... | collective-permute-start | bytes 245768 | tf_op jit(solution)/shard_map/ppermute | solution.py:39
  6.1 12.4 %collective-permute-start.4 = (bf16[1,1,1,1,32,1280]{5,4,3,2,1,0:T(8,128)(2,1)}, bf16[1,1,1,1,32,1280]{5,4,3,2,1,0:T(8,128)(2,1)S(1)}, u32[]{:S(2)}, u32[]{:S(2)}) collective-permute-start(bf16[1,1,1,1,32,1280]{5,4,3,2,1,0:T(8,128)(2,1)} %bitcast.71), channel_id=1, source_target_pairs={{0,16},{1,17},{2,18},{3,19},{4,20},{5,21},{6,22},{7,23},{8,24},{9,... | collective-permute-start | bytes 245768 | tf_op jit(solution)/shard_map/ppermute | solution.py:39
  14.7 16.1 %copy-start.2 = (bf16[32,1152]{1,0:T(8,128)(2,1)S(1)}, bf16[32,1152]{1,0:T(8,128)(2,1)}, u32[]{:S(2)}) copy-start(bf16[32,1152]{1,0:T(8,128)(2,1)} %get-tuple-element.22) | copy-start | bytes 221188
  14.7 6.3 %collective-permute-start.9 = (bf16[1,1,1,2,32,1152]{5,4,3,2,1,0:T(8,128)(2,1)S(1)}, bf16[1,1,1,2,32,1152]{5,4,3,2,1,0:T(8,128)(2,1)S(1)}, u32[]{:S(2)}, u32[]{:S(2)}) collective-permute-start(bf16[1,1,1,2,32,1152]{5,4,3,2,1,0:T(8,128)(2,1)S(1)} %pad_maximum_fusion.12), channel_id=1, source_target_pairs={{0,8},{1,9},{2,10},{3,11},{4,12},{5,13},{6,14},{7,15},{8,0},{9,1},... | collective-permute-start | bytes 442376 | tf_op jit(solution)/shard_map/ppermute | solution.py:39
  16.5 6.5 %collective-permute-start.1 = (bf16[1,1,1,2,32,1280]{5,4,3,2,1,0:T(8,128)(2,1)S(1)}, bf16[1,1,1,2,32,1280]{5,4,3,2,1,0:T(8,128)(2,1)S(1)}, u32[]{:S(2)}, u32[]{:S(2)}) collective-permute-start(bf16[1,1,1,2,32,1280]{5,4,3,2,1,0:T(8,128)(2,1)S(1)} %pad_maximum_fusion.10), channel_id=1, source_target_pairs={{0,2},{1,5},{2,0},{3,7},{4,6},{5,1},{6,4},{7,3},{8,10},{9,13},{10,... | collective-permute-start | bytes 491528 | tf_op jit(solution)/shard_map/ppermute | solution.py:39
  19.4 6.9 %collective-permute-start.5 = (bf16[1,1,1,2,32,1280]{5,4,3,2,1,0:T(8,128)(2,1)S(1)}, bf16[1,1,1,2,32,1280]{5,4,3,2,1,0:T(8,128)(2,1)S(1)}, u32[]{:S(2)}, u32[]{:S(2)}) collective-permute-start(bf16[1,1,1,2,32,1280]{5,4,3,2,1,0:T(8,128)(2,1)S(1)} %pad_maximum_fusion.11), channel_id=1, source_target_pairs={{0,4},{1,3},{2,6},{3,1},{4,0},{5,7},{6,2},{7,5},{8,12},{9,11},{10,... | collective-permute-start | bytes 491528 | tf_op jit(solution)/shard_map/ppermute | solution.py:39
  21.9 8.9 %collective-permute-start.10 = (bf16[1,1,2,2,32,1152]{5,4,3,2,1,0:T(8,128)(2,1)S(1)}, bf16[1,1,2,2,32,1152]{5,4,3,2,1,0:T(8,128)(2,1)S(1)}, u32[]{:S(2)}, u32[]{:S(2)}) collective-permute-start(bf16[1,1,2,2,32,1152]{5,4,3,2,1,0:T(8,128)(2,1)S(1)} %pad_maximum_fusion.8), channel_id=1, source_target_pairs={{0,2},{1,5},{2,0},{3,7},{4,6},{5,1},{6,4},{7,3},{8,10},{9,13},{10,... | collective-permute-start | bytes 884744 | tf_op jit(solution)/shard_map/ppermute | solution.py:39
  23.0 10.5 %copy-start.4 = (bf16[1,3584,512]{2,1,0:T(8,128)(2,1)S(1)}, bf16[1,3584,512]{2,1,0:T(8,128)(2,1)}, u32[]{:S(2)}) copy-start(bf16[1,3584,512]{2,1,0:T(8,128)(2,1)} %param.7) | copy-start | bytes 11010052
  23.1 9.5 %collective-permute-start.2 = (bf16[2,1,1,2,32,1280]{5,4,3,2,1,0:T(8,128)(2,1)S(1)}, bf16[2,1,1,2,32,1280]{5,4,3,2,1,0:T(8,128)(2,1)S(1)}, u32[]{:S(2)}, u32[]{:S(2)}) collective-permute-start(bf16[2,1,1,2,32,1280]{5,4,3,2,1,0:T(8,128)(2,1)S(1)} %pad_maximum_fusion.6), channel_id=1, source_target_pairs={{0,4},{1,3},{2,6},{3,1},{4,0},{5,7},{6,2},{7,5},{8,12},{9,11},{10,... | collective-permute-start | bytes 983048 | tf_op jit(solution)/shard_map/ppermute | solution.py:39
  26.4 8.1 %collective-permute-start.6 = (bf16[1,2,1,2,32,1280]{5,4,3,2,1,0:T(8,128)(2,1)S(1)}, bf16[1,2,1,2,32,1280]{5,4,3,2,1,0:T(8,128)(2,1)S(1)}, u32[]{:S(2)}, u32[]{:S(2)}) collective-permute-start(bf16[1,2,1,2,32,1280]{5,4,3,2,1,0:T(8,128)(2,1)S(1)} %pad_maximum_fusion.7), channel_id=1, source_target_pairs={{0,8},{1,9},{2,10},{3,11},{4,12},{5,13},{6,14},{7,15},{8,0},{9,1},... | collective-permute-start | bytes 983048 | tf_op jit(solution)/shard_map/ppermute | solution.py:39
  30.9 14.0 %collective-permute-start.11 = (bf16[2,1,2,2,32,1152]{5,4,3,2,1,0:T(8,128)(2,1)S(1)}, bf16[2,1,2,2,32,1152]{5,4,3,2,1,0:T(8,128)(2,1)S(1)}, u32[]{:S(2)}, u32[]{:S(2)}) collective-permute-start(bf16[2,1,2,2,32,1152]{5,4,3,2,1,0:T(8,128)(2,1)S(1)} %pad_maximum_fusion.5), channel_id=1, source_target_pairs={{0,4},{1,3},{2,6},{3,1},{4,0},{5,7},{6,2},{7,5},{8,12},{9,11},{10,... | collective-permute-start | bytes 1769480 | tf_op jit(solution)/shard_map/ppermute | solution.py:39
  32.6 14.9 %collective-permute-start.3 = (bf16[2,2,1,2,32,1280]{5,4,3,2,1,0:T(8,128)(2,1)S(1)}, bf16[2,2,1,2,32,1280]{5,4,3,2,1,0:T(8,128)(2,1)S(1)}, u32[]{:S(2)}, u32[]{:S(2)}) collective-permute-start(bf16[2,2,1,2,32,1280]{5,4,3,2,1,0:T(8,128)(2,1)S(1)} %pad_maximum_fusion.3), channel_id=1, source_target_pairs={{0,8},{1,9},{2,10},{3,11},{4,12},{5,13},{6,14},{7,15},{8,0},{9,1},... | collective-permute-start | bytes 1966088 | tf_op jit(solution)/shard_map/ppermute | solution.py:39
  33.5 22.9 %collective-permute-start.12 = (bf16[3584,512]{1,0:T(8,128)(2,1)S(1)}, bf16[3584,512]{1,0:T(8,128)(2,1)S(1)}, u32[]{:S(2)}, u32[]{:S(2)}) collective-permute-start(bf16[3584,512]{1,0:T(8,128)(2,1)S(1)} %bitcast.91), channel_id=1, source_target_pairs={{0,1},{1,0},{2,3},{3,2},{4,5},{5,4},{6,7},{7,6},{8,9},{9,8},{10,11... | collective-permute-start | bytes 11010056 | tf_op jit(solution)/shard_map/ppermute | solution.py:43
  34.5 16.1 %collective-permute-start.7 = (bf16[1,2,2,2,32,1280]{5,4,3,2,1,0:T(8,128)(2,1)S(1)}, bf16[1,2,2,2,32,1280]{5,4,3,2,1,0:T(8,128)(2,1)S(1)}, u32[]{:S(2)}, u32[]{:S(2)}) collective-permute-start(bf16[1,2,2,2,32,1280]{5,4,3,2,1,0:T(8,128)(2,1)S(1)} %pad_maximum_fusion.4), channel_id=1, source_target_pairs={{0,2},{1,5},{2,0},{3,7},{4,6},{5,1},{6,4},{7,3},{8,10},{9,13},{10,... | collective-permute-start | bytes 1966088 | tf_op jit(solution)/shard_map/ppermute | solution.py:39
  44.9 2.9 %copy-start = (bf16[1,512,3584]{2,1,0:T(8,128)(2,1)S(1)}, bf16[1,512,3584]{2,1,0:T(8,128)(2,1)}, u32[]{:S(2)}) copy-start(bf16[1,512,3584]{2,1,0:T(8,128)(2,1)} %param.9) | copy-start | bytes 11010052
  47.7 2.0 %copy-start.5 = (bf16[1,3584,512]{2,1,0:T(8,128)(2,1)S(1)}, bf16[1,3584,512]{2,1,0:T(8,128)(2,1)}, u32[]{:S(2)}) copy-start(bf16[1,3584,512]{2,1,0:T(8,128)(2,1)} %param.8) | copy-start | bytes 11010052
  47.7 11.2 %collective-permute-start.13 = (bf16[3584,512]{1,0:T(8,128)(2,1)}, bf16[3584,512]{1,0:T(8,128)(2,1)S(1)}, u32[]{:S(2)}, u32[]{:S(2)}) collective-permute-start(bf16[3584,512]{1,0:T(8,128)(2,1)} %bitcast.92), channel_id=1, source_target_pairs={{0,1},{1,0},{2,3},{3,2},{4,5},{5,4},{6,7},{7,6},{8,9},{9,8},{10,11... | collective-permute-start | bytes 11010056 | tf_op jit(solution)/shard_map/ppermute | solution.py:43
  47.8 13.7 %collective-permute-start.14 = (bf16[512,3584]{1,0:T(8,128)(2,1)S(1)}, bf16[512,3584]{1,0:T(8,128)(2,1)S(1)}, u32[]{:S(2)}, u32[]{:S(2)}) collective-permute-start(bf16[512,3584]{1,0:T(8,128)(2,1)S(1)} %bitcast.62), channel_id=1, source_target_pairs={{0,1},{1,0},{2,3},{3,2},{4,5},{5,4},{6,7},{7,6},{8,9},{9,8},{10,11... | collective-permute-start | bytes 11010056 | tf_op jit(solution)/shard_map/ppermute | solution.py:43
  64.0 13.9 %collective-permute-start.23 = (bf16[2,2,1,2,32,1024]{5,4,3,2,1,0:T(8,128)(2,1)S(1)}, bf16[2,2,1,2,32,1024]{5,4,3,2,1,0:T(8,128)(2,1)S(1)}, u32[]{:S(2)}, u32[]{:S(2)}) collective-permute-start(bf16[2,2,1,2,32,1024]{5,4,3,2,1,0:T(8,128)(2,1)S(1)} %slice.196), channel_id=1, source_target_pairs={{0,8},{1,9},{2,10},{3,11},{4,12},{5,13},{6,14},{7,15},{8,0},{9,1},... | collective-permute-start | bytes 1572872 | tf_op jit(solution)/shard_map/ppermute | solution.py:39
  65.5 17.6 %collective-permute-start.15 = (bf16[1,2,2,2,32,1280]{5,4,3,2,1,0:T(8,128)(2,1)S(1)}, bf16[1,2,2,2,32,1280]{5,4,3,2,1,0:T(8,128)(2,1)S(1)}, u32[]{:S(2)}, u32[]{:S(2)}) collective-permute-start(bf16[1,2,2,2,32,1280]{5,4,3,2,1,0:T(8,128)(2,1)S(1)} %slice.180), channel_id=1, source_target_pairs={{0,2},{1,5},{2,0},{3,7},{4,6},{5,1},{6,4},{7,3},{8,10},{9,13},{10,... | collective-permute-start | bytes 1966088 | tf_op jit(solution)/shard_map/ppermute | solution.py:39
  67.3 19.3 %collective-permute-start.19 = (bf16[2,1,2,2,32,1280]{5,4,3,2,1,0:T(8,128)(2,1)S(1)}, bf16[2,1,2,2,32,1280]{5,4,3,2,1,0:T(8,128)(2,1)S(1)}, u32[]{:S(2)}, u32[]{:S(2)}) collective-permute-start(bf16[2,1,2,2,32,1280]{5,4,3,2,1,0:T(8,128)(2,1)S(1)} %slice.188), channel_id=1, source_target_pairs={{0,4},{1,3},{2,6},{3,1},{4,0},{5,7},{6,2},{7,5},{8,12},{9,11},{10,... | collective-permute-start | bytes 1966088 | tf_op jit(solution)/shard_map/ppermute | solution.py:39
  78.1 6.7 %collective-permute-start.24 = (bf16[2,1,1,2,32,1024]{5,4,3,2,1,0:T(8,128)(2,1)S(1)}, bf16[2,1,1,2,32,1024]{5,4,3,2,1,0:T(8,128)(2,1)S(1)}, u32[]{:S(2)}, u32[]{:S(2)}) collective-permute-start(bf16[2,1,1,2,32,1024]{5,4,3,2,1,0:T(8,128)(2,1)S(1)} %slice.230), channel_id=1, source_target_pairs={{0,4},{1,3},{2,6},{3,1},{4,0},{5,7},{6,2},{7,5},{8,12},{9,11},{10,... | collective-permute-start | bytes 786440 | tf_op jit(solution)/shard_map/ppermute | solution.py:39
  83.4 9.5 %collective-permute-start.16 = (bf16[1,2,1,2,32,1280]{5,4,3,2,1,0:T(8,128)(2,1)S(1)}, bf16[1,2,1,2,32,1280]{5,4,3,2,1,0:T(8,128)(2,1)S(1)}, u32[]{:S(2)}, u32[]{:S(2)}) collective-permute-start(bf16[1,2,1,2,32,1280]{5,4,3,2,1,0:T(8,128)(2,1)S(1)} %slice.218), channel_id=1, source_target_pairs={{0,8},{1,9},{2,10},{3,11},{4,12},{5,13},{6,14},{7,15},{8,0},{9,1},... | collective-permute-start | bytes 983048 | tf_op jit(solution)/shard_map/ppermute | solution.py:39
  84.9 5.0 %collective-permute-start.25 = (bf16[1,1,1,2,32,1024]{5,4,3,2,1,0:T(8,128)(2,1)S(1)}, bf16[1,1,1,2,32,1024]{5,4,3,2,1,0:T(8,128)(2,1)S(1)}, u32[]{:S(2)}, u32[]{:S(2)}) collective-permute-start(bf16[1,1,1,2,32,1024]{5,4,3,2,1,0:T(8,128)(2,1)S(1)} %slice.232), channel_id=1, source_target_pairs={{0,2},{1,5},{2,0},{3,7},{4,6},{5,1},{6,4},{7,3},{8,10},{9,13},{10,... | collective-permute-start | bytes 393224 | tf_op jit(solution)/shard_map/ppermute | solution.py:39
  86.8 7.6 %collective-permute-start.20 = (bf16[1,1,2,2,32,1280]{5,4,3,2,1,0:T(8,128)(2,1)S(1)}, bf16[1,1,2,2,32,1280]{5,4,3,2,1,0:T(8,128)(2,1)S(1)}, u32[]{:S(2)}, u32[]{:S(2)}) collective-permute-start(bf16[1,1,2,2,32,1280]{5,4,3,2,1,0:T(8,128)(2,1)S(1)} %slice.224), channel_id=1, source_target_pairs={{0,2},{1,5},{2,0},{3,7},{4,6},{5,1},{6,4},{7,3},{8,10},{9,13},{10,... | collective-permute-start | bytes 983048 | tf_op jit(solution)/shard_map/ppermute | solution.py:39
  90.0 6.6 %collective-permute-start.26 = (bf16[1,1,1,1,32,1024]{5,4,3,2,1,0:T(8,128)(2,1)S(1)}, bf16[1,1,1,1,32,1024]{5,4,3,2,1,0:T(8,128)(2,1)S(1)}, u32[]{:S(2)}, u32[]{:S(2)}) collective-permute-start(bf16[1,1,1,1,32,1024]{5,4,3,2,1,0:T(8,128)(2,1)S(1)} %slice.234), channel_id=1, source_target_pairs={{0,16},{1,17},{2,18},{3,19},{4,20},{5,21},{6,22},{7,23},{8,24},{9,... | collective-permute-start | bytes 196616 | tf_op jit(solution)/shard_map/ppermute | solution.py:39
  93.0 5.4 %collective-permute-start.17 = (bf16[1,1,1,2,32,1280]{5,4,3,2,1,0:T(8,128)(2,1)S(1)}, bf16[1,1,1,2,32,1280]{5,4,3,2,1,0:T(8,128)(2,1)S(1)}, u32[]{:S(2)}, u32[]{:S(2)}) collective-permute-start(bf16[1,1,1,2,32,1280]{5,4,3,2,1,0:T(8,128)(2,1)S(1)} %slice.220), channel_id=1, source_target_pairs={{0,4},{1,3},{2,6},{3,1},{4,0},{5,7},{6,2},{7,5},{8,12},{9,11},{10,... | collective-permute-start | bytes 491528 | tf_op jit(solution)/shard_map/ppermute | solution.py:39
  94.5 5.7 %collective-permute-start.21 = (bf16[1,1,1,2,32,1280]{5,4,3,2,1,0:T(8,128)(2,1)S(1)}, bf16[1,1,1,2,32,1280]{5,4,3,2,1,0:T(8,128)(2,1)S(1)}, u32[]{:S(2)}, u32[]{:S(2)}) collective-permute-start(bf16[1,1,1,2,32,1280]{5,4,3,2,1,0:T(8,128)(2,1)S(1)} %slice.226), channel_id=1, source_target_pairs={{0,8},{1,9},{2,10},{3,11},{4,12},{5,13},{6,14},{7,15},{8,0},{9,1},... | collective-permute-start | bytes 491528 | tf_op jit(solution)/shard_map/ppermute | solution.py:39
  98.4 7.7 %collective-permute-start.18 = (bf16[1,1,1,1,32,1280]{5,4,3,2,1,0:T(8,128)(2,1)S(1)}, bf16[1,1,1,1,32,1280]{5,4,3,2,1,0:T(8,128)(2,1)S(1)}, u32[]{:S(2)}, u32[]{:S(2)}) collective-permute-start(bf16[1,1,1,1,32,1280]{5,4,3,2,1,0:T(8,128)(2,1)S(1)} %slice.222), channel_id=1, source_target_pairs={{0,16},{1,17},{2,18},{3,19},{4,20},{5,21},{6,22},{7,23},{8,24},{9,... | collective-permute-start | bytes 245768 | tf_op jit(solution)/shard_map/ppermute | solution.py:39
  100.2 7.7 %collective-permute-start.22 = (bf16[1,1,1,1,32,1280]{5,4,3,2,1,0:T(8,128)(2,1)S(1)}, bf16[1,1,1,1,32,1280]{5,4,3,2,1,0:T(8,128)(2,1)S(1)}, u32[]{:S(2)}, u32[]{:S(2)}) collective-permute-start(bf16[1,1,1,1,32,1280]{5,4,3,2,1,0:T(8,128)(2,1)S(1)} %slice.228), channel_id=1, source_target_pairs={{0,16},{1,17},{2,18},{3,19},{4,20},{5,21},{6,22},{7,23},{8,24},{9,... | collective-permute-start | bytes 245768 | tf_op jit(solution)/shard_map/ppermute | solution.py:39

commit v5 on v4

--- a/solution.py
+++ b/solution.py
@@ -93,9 +93,9 @@
         if step == bits - 2:
             held[0], near = lax.optimization_barrier((held[0], own[0]))
             far.append(other_core(near))
+            held[1], near = lax.optimization_barrier((held[1], own[1]))
+            far.append(other_core(near))
     held = [piece.reshape(rows, -1) for piece in held]
-    held[0], near = lax.optimization_barrier((held[0], own[1]))
-    far.append(other_core(near))
     held[0], near = lax.optimization_barrier((held[0], own[2]))
     far.append(other_core(near))
 

time: 109 us -> 108 us (level)
  transfers between devices with their start and end apart: 27 -> 27, of which waited for: 16 -> 16; matrix products, arithmetic and copies ran while one was open for 16% -> 17% of each run, Pallas kernels for 0% -> 0%
where the time goes in v5:
time: 108 us
  waiting for transfers between devices  42.8 us (40%)
  starting transfers between devices  40.7 us (38%)
  matrix products  14.8 us (14%)
  other arithmetic  6.04 us (6%)
  Pallas kernels  1.98 us (2%)
  local copies, waits for them, and re-layouts  1.46 us (1%)
    ppermute x24, waiting for transfers between devices, cross(): return lax.ppermute(block, ('expert', 'sub'), pairs)  42.8 us
    ppermute x24, starting transfers between devices, cross(): return lax.ppermute(block, ('expert', 'sub'), pairs)  40.5 us
    dot_general x12, matrix products, project(): jnp.dot(held[i][:, :width], matrix[start:start + width], preferred_elemen...  9.91 us
    dot_general x6, matrix products, per_device(): jnp.dot(h, w[2][:, start:start + width], preferred_element_type=jnp.float32)  4.85 us
    concatenate x12, other arithmetic, per_device(): jnp.concatenate([held[i], cross(held[i], axis, experts, mirror)], axis=axis)  4.31 us
  transfers between devices with their start and end apart: 27, of which 16 were waited for; matrix products, arithmetic and copies ran while one was open for 17% of the time, Pallas kernels for 0%

profile of v5, /device:TPU:0, one launch (start us, length us, event | category | flops | bytes accessed | tf_op | source)
XLA Modules:
  0.0 108.1 jit_solution(3707736537573830714)
XLA Ops:
  0.0 2.0 %shard_map.64 = (bf16[32,1280]{1,0:T(8,128)(2,1)}, bf16[32,1280]{1,0:T(8,128)(2,1)}, bf16[32,1152]{1,0:T(8,128)(2,1)}) custom-call(bf16[32,3584]{1,0:T(8,128)(2,1)} %tokens_ref.1, s32[8,32]{1,0:T(8,128)} %bitcast.88, s32[8,32]{1,0:T(8,128)} %bitcast.89), custom_call_target="tpu_custom_call" | custom-call | tf_op jit(solution)/shard_map/pallas_call | solution.py:67
  2.0 4.0 %collective-permute-start.8 = (bf16[1,1,1,1,32,1152]{5,4,3,2,1,0:T(8,128)(2,1)}, bf16[1,1,1,1,32,1152]{5,4,3,2,1,0:T(8,128)(2,1)S(1)}, u32[]{:S(2)}, u32[]{:S(2)}) collective-permute-start(bf16[1,1,1,1,32,1152]{5,4,3,2,1,0:T(8,128)(2,1)} %bitcast.75), channel_id=1, source_target_pairs={{0,16},{1,17},{2,18},{3,19},{4,20},{5,21},{6,22},{7,23},{8,24},{9,... | collective-permute-start | bytes 221192 | tf_op jit(solution)/shard_map/ppermute | solution.py:39
  6.1 2.9 %collective-permute-start.4 = (bf16[1,1,1,1,32,1280]{5,4,3,2,1,0:T(8,128)(2,1)}, bf16[1,1,1,1,32,1280]{5,4,3,2,1,0:T(8,128)(2,1)S(1)}, u32[]{:S(2)}, u32[]{:S(2)}) collective-permute-start(bf16[1,1,1,1,32,1280]{5,4,3,2,1,0:T(8,128)(2,1)} %bitcast.80), channel_id=1, source_target_pairs={{0,16},{1,17},{2,18},{3,19},{4,20},{5,21},{6,22},{7,23},{8,24},{9,... | collective-permute-start | bytes 245768 | tf_op jit(solution)/shard_map/ppermute | solution.py:39
  8.9 4.9 %collective-permute-done.8 = bf16[1,1,1,1,32,1152]{5,4,3,2,1,0:T(8,128)(2,1)S(1)} collective-permute-done((bf16[1,1,1,1,32,1152]{5,4,3,2,1,0:T(8,128)(2,1)}, bf16[1,1,1,1,32,1152]{5,4,3,2,1,0:T(8,128)(2,1)S(1)}, u32[]{:S(2)}, u32[]{:S(2)}) %collective-permute-start.8) | collective-permute-done | bytes 73760 | tf_op jit(solution)/shard_map/ppermute | solution.py:39
  13.8 0.9 pad_maximum_fusion.12
  14.7 0.8 collective-permute-start.9
  15.6 0.9 pad_maximum_fusion.10
  16.5 2.0 %collective-permute-start.1 = (bf16[1,1,1,2,32,1280]{5,4,3,2,1,0:T(8,128)(2,1)S(1)}, bf16[1,1,1,2,32,1280]{5,4,3,2,1,0:T(8,128)(2,1)S(1)}, u32[]{:S(2)}, u32[]{:S(2)}) collective-permute-start(bf16[1,1,1,2,32,1280]{5,4,3,2,1,0:T(8,128)(2,1)S(1)} %pad_maximum_fusion.10), channel_id=1, source_target_pairs={{0,2},{1,5},{2,0},{3,7},{4,6},{5,1},{6,4},{7,3},{8,10},{9,13},{10,... | collective-permute-start | bytes 491528 | tf_op jit(solution)/shard_map/ppermute | solution.py:39
  18.5 0.9 pad_maximum_fusion.11
  19.4 1.6 %collective-permute-start.5 = (bf16[1,1,1,2,32,1280]{5,4,3,2,1,0:T(8,128)(2,1)S(1)}, bf16[1,1,1,2,32,1280]{5,4,3,2,1,0:T(8,128)(2,1)S(1)}, u32[]{:S(2)}, u32[]{:S(2)}) collective-permute-start(bf16[1,1,1,2,32,1280]{5,4,3,2,1,0:T(8,128)(2,1)S(1)} %pad_maximum_fusion.11), channel_id=1, source_target_pairs={{0,4},{1,3},{2,6},{3,1},{4,0},{5,7},{6,2},{7,5},{8,12},{9,11},{10,... | collective-permute-start | bytes 491528 | tf_op jit(solution)/shard_map/ppermute | solution.py:39
  21.0 0.9 pad_maximum_fusion.8
  21.9 1.1 collective-permute-start.10
  23.1 2.7 %collective-permute-start.2 = (bf16[2,1,1,2,32,1280]{5,4,3,2,1,0:T(8,128)(2,1)S(1)}, bf16[2,1,1,2,32,1280]{5,4,3,2,1,0:T(8,128)(2,1)S(1)}, u32[]{:S(2)}, u32[]{:S(2)}) collective-permute-start(bf16[2,1,1,2,32,1280]{5,4,3,2,1,0:T(8,128)(2,1)S(1)} %pad_maximum_fusion.6), channel_id=1, source_target_pairs={{0,4},{1,3},{2,6},{3,1},{4,0},{5,7},{6,2},{7,5},{8,12},{9,11},{10,... | collective-permute-start | bytes 983048 | tf_op jit(solution)/shard_map/ppermute | solution.py:39
  25.7 0.6 collective-permute-done.5
  26.4 1.5 %collective-permute-start.6 = (bf16[1,2,1,2,32,1280]{5,4,3,2,1,0:T(8,128)(2,1)S(1)}, bf16[1,2,1,2,32,1280]{5,4,3,2,1,0:T(8,128)(2,1)S(1)}, u32[]{:S(2)}, u32[]{:S(2)}) collective-permute-start(bf16[1,2,1,2,32,1280]{5,4,3,2,1,0:T(8,128)(2,1)S(1)} %pad_maximum_fusion.7), channel_id=1, source_target_pairs={{0,8},{1,9},{2,10},{3,11},{4,12},{5,13},{6,14},{7,15},{8,0},{9,1},... | collective-permute-start | bytes 983048 | tf_op jit(solution)/shard_map/ppermute | solution.py:39
  27.9 2.9 %collective-permute-done.10 = bf16[1,1,2,2,32,1152]{5,4,3,2,1,0:T(8,128)(2,1)S(1)} collective-permute-done((bf16[1,1,2,2,32,1152]{5,4,3,2,1,0:T(8,128)(2,1)S(1)}, bf16[1,1,2,2,32,1152]{5,4,3,2,1,0:T(8,128)(2,1)S(1)}, u32[]{:S(2)}, u32[]{:S(2)}) %collective-permute-start.10) | collective-permute-done | bytes 294944 | tf_op jit(solution)/shard_map/ppermute | solution.py:39
  30.9 1.7 %collective-permute-start.11 = (bf16[2,1,2,2,32,1152]{5,4,3,2,1,0:T(8,128)(2,1)S(1)}, bf16[2,1,2,2,32,1152]{5,4,3,2,1,0:T(8,128)(2,1)S(1)}, u32[]{:S(2)}, u32[]{:S(2)}) collective-permute-start(bf16[2,1,2,2,32,1152]{5,4,3,2,1,0:T(8,128)(2,1)S(1)} %pad_maximum_fusion.5), channel_id=1, source_target_pairs={{0,4},{1,3},{2,6},{3,1},{4,0},{5,7},{6,2},{7,5},{8,12},{9,11},{10,... | collective-permute-start | bytes 1769480 | tf_op jit(solution)/shard_map/ppermute | solution.py:39
  32.6 0.9 collective-permute-start.3
  33.6 0.9 collective-permute-done.6
  34.5 2.0 %collective-permute-start.7 = (bf16[1,2,2,2,32,1280]{5,4,3,2,1,0:T(8,128)(2,1)S(1)}, bf16[1,2,2,2,32,1280]{5,4,3,2,1,0:T(8,128)(2,1)S(1)}, u32[]{:S(2)}, u32[]{:S(2)}) collective-permute-start(bf16[1,2,2,2,32,1280]{5,4,3,2,1,0:T(8,128)(2,1)S(1)} %pad_maximum_fusion.4), channel_id=1, source_target_pairs={{0,2},{1,5},{2,0},{3,7},{4,6},{5,1},{6,4},{7,3},{8,10},{9,13},{10,... | collective-permute-start | bytes 1966088 | tf_op jit(solution)/shard_map/ppermute | solution.py:39
  36.5 8.3 %collective-permute-done.11 = bf16[2,1,2,2,32,1152]{5,4,3,2,1,0:T(8,128)(2,1)S(1)} collective-permute-done((bf16[2,1,2,2,32,1152]{5,4,3,2,1,0:T(8,128)(2,1)S(1)}, bf16[2,1,2,2,32,1152]{5,4,3,2,1,0:T(8,128)(2,1)S(1)}, u32[]{:S(2)}, u32[]{:S(2)}) %collective-permute-start.11) | collective-permute-done | bytes 589856 | tf_op jit(solution)/shard_map/ppermute | solution.py:39
  45.1 2.5 %collective-permute-done.3 = bf16[2,2,1,2,32,1280]{5,4,3,2,1,0:T(8,128)(2,1)S(1)} collective-permute-done((bf16[2,2,1,2,32,1280]{5,4,3,2,1,0:T(8,128)(2,1)S(1)}, bf16[2,2,1,2,32,1280]{5,4,3,2,1,0:T(8,128)(2,1)S(1)}, u32[]{:S(2)}, u32[]{:S(2)}) %collective-permute-start.3) | collective-permute-done | bytes 655392 | tf_op jit(solution)/shard_map/ppermute | solution.py:39
  48.0 0.8 fusion.23
  48.8 1.2 %copy-done.5 = bf16[1,3584,512]{2,1,0:T(8,128)(2,1)S(1)} copy-done((bf16[1,3584,512]{2,1,0:T(8,128)(2,1)S(1)}, bf16[1,3584,512]{2,1,0:T(8,128)(2,1)}, u32[]{:S(2)}) %copy-start.5) | copy-done | bytes 3670040
  50.0 0.8 fusion.20
  50.8 0.8 convolution_add_fusion.7
  51.7 0.8 convolution_add_fusion.6
  52.5 0.7 convolution_add_fusion.3
  53.2 0.8 fusion.29
  54.1 0.7 fusion.31
  54.8 0.9 fusion.8
  55.7 0.9 fusion.17
  56.5 0.7 fusion.35
  57.3 0.7 fusion.33
  58.0 0.8 fusion.14
  58.8 0.8 fusion.11
  59.7 0.9 fusion.6
  60.5 1.0 multiply_convert_fusion.1
  61.6 0.7 multiply_convert_fusion
  62.3 0.9 fusion.3
  63.2 0.9 fusion.2
  64.1 1.5 %collective-permute-start.23 = (bf16[2,2,1,2,32,1024]{5,4,3,2,1,0:T(8,128)(2,1)S(1)}, bf16[2,2,1,2,32,1024]{5,4,3,2,1,0:T(8,128)(2,1)S(1)}, u32[]{:S(2)}, u32[]{:S(2)}) collective-permute-start(bf16[2,2,1,2,32,1024]{5,4,3,2,1,0:T(8,128)(2,1)S(1)} %slice.196), channel_id=1, source_target_pairs={{0,8},{1,9},{2,10},{3,11},{4,12},{5,13},{6,14},{7,15},{8,0},{9,1},... | collective-permute-start | bytes 1572872 | tf_op jit(solution)/shard_map/ppermute | solution.py:39
  65.6 1.7 %collective-permute-start.15 = (bf16[1,2,2,2,32,1280]{5,4,3,2,1,0:T(8,128)(2,1)S(1)}, bf16[1,2,2,2,32,1280]{5,4,3,2,1,0:T(8,128)(2,1)S(1)}, u32[]{:S(2)}, u32[]{:S(2)}) collective-permute-start(bf16[1,2,2,2,32,1280]{5,4,3,2,1,0:T(8,128)(2,1)S(1)} %slice.180), channel_id=1, source_target_pairs={{0,2},{1,5},{2,0},{3,7},{4,6},{5,1},{6,4},{7,3},{8,10},{9,13},{10,... | collective-permute-start | bytes 1966088 | tf_op jit(solution)/shard_map/ppermute | solution.py:39
  67.4 1.0 collective-permute-start.19
  68.4 10.0 %collective-permute-done.23 = bf16[2,2,1,2,32,1024]{5,4,3,2,1,0:T(8,128)(2,1)S(1)} collective-permute-done((bf16[2,2,1,2,32,1024]{5,4,3,2,1,0:T(8,128)(2,1)S(1)}, bf16[2,2,1,2,32,1024]{5,4,3,2,1,0:T(8,128)(2,1)S(1)}, u32[]{:S(2)}, u32[]{:S(2)}) %collective-permute-start.23) | collective-permute-done | bytes 524320 | tf_op jit(solution)/shard_map/ppermute | solution.py:39
  78.5 0.2 add_convert_fusion.2
  78.7 2.0 %collective-permute-start.24 = (bf16[2,1,1,2,32,1024]{5,4,3,2,1,0:T(8,128)(2,1)S(1)}, bf16[2,1,1,2,32,1024]{5,4,3,2,1,0:T(8,128)(2,1)S(1)}, u32[]{:S(2)}, u32[]{:S(2)}) collective-permute-start(bf16[2,1,1,2,32,1024]{5,4,3,2,1,0:T(8,128)(2,1)S(1)} %slice.230), channel_id=1, source_target_pairs={{0,4},{1,3},{2,6},{3,1},{4,0},{5,7},{6,2},{7,5},{8,12},{9,11},{10,... | collective-permute-start | bytes 786440 | tf_op jit(solution)/shard_map/ppermute | solution.py:39
  80.7 2.2 %collective-permute-done.15 = bf16[1,2,2,2,32,1280]{5,4,3,2,1,0:T(8,128)(2,1)S(1)} collective-permute-done((bf16[1,2,2,2,32,1280]{5,4,3,2,1,0:T(8,128)(2,1)S(1)}, bf16[1,2,2,2,32,1280]{5,4,3,2,1,0:T(8,128)(2,1)S(1)}, u32[]{:S(2)}, u32[]{:S(2)}) %collective-permute-start.15) | collective-permute-done | bytes 655392 | tf_op jit(solution)/shard_map/ppermute | solution.py:39
  82.9 0.2 add_convert_fusion.1
  83.2 2.2 %collective-permute-done.24 = bf16[2,1,1,2,32,1024]{5,4,3,2,1,0:T(8,128)(2,1)S(1)} collective-permute-done((bf16[2,1,1,2,32,1024]{5,4,3,2,1,0:T(8,128)(2,1)S(1)}, bf16[2,1,1,2,32,1024]{5,4,3,2,1,0:T(8,128)(2,1)S(1)}, u32[]{:S(2)}, u32[]{:S(2)}) %collective-permute-start.24) | collective-permute-done | bytes 262176 | tf_op jit(solution)/shard_map/ppermute | solution.py:39
  85.5 1.7 %collective-permute-start.25 = (bf16[1,1,1,2,32,1024]{5,4,3,2,1,0:T(8,128)(2,1)S(1)}, bf16[1,1,1,2,32,1024]{5,4,3,2,1,0:T(8,128)(2,1)S(1)}, u32[]{:S(2)}, u32[]{:S(2)}) collective-permute-start(bf16[1,1,1,2,32,1024]{5,4,3,2,1,0:T(8,128)(2,1)S(1)} %slice.232), channel_id=1, source_target_pairs={{0,2},{1,5},{2,0},{3,7},{4,6},{5,1},{6,4},{7,3},{8,10},{9,13},{10,... | collective-permute-start | bytes 393224 | tf_op jit(solution)/shard_map/ppermute | solution.py:39
  87.4 0.4 collective-permute-start.20
  87.8 2.7 %collective-permute-done.25 = bf16[1,1,1,2,32,1024]{5,4,3,2,1,0:T(8,128)(2,1)S(1)} collective-permute-done((bf16[1,1,1,2,32,1024]{5,4,3,2,1,0:T(8,128)(2,1)S(1)}, bf16[1,1,1,2,32,1024]{5,4,3,2,1,0:T(8,128)(2,1)S(1)}, u32[]{:S(2)}, u32[]{:S(2)}) %collective-permute-start.25) | collective-permute-done | bytes 131104 | tf_op jit(solution)/shard_map/ppermute | solution.py:39
  90.5 2.9 %collective-permute-start.26 = (bf16[1,1,1,1,32,1024]{5,4,3,2,1,0:T(8,128)(2,1)S(1)}, bf16[1,1,1,1,32,1024]{5,4,3,2,1,0:T(8,128)(2,1)S(1)}, u32[]{:S(2)}, u32[]{:S(2)}) collective-permute-start(bf16[1,1,1,1,32,1024]{5,4,3,2,1,0:T(8,128)(2,1)S(1)} %slice.234), channel_id=1, source_target_pairs={{0,16},{1,17},{2,18},{3,19},{4,20},{5,21},{6,22},{7,23},{8,24},{9,... | collective-permute-start | bytes 196616 | tf_op jit(solution)/shard_map/ppermute | solution.py:39
  93.6 1.4 %collective-permute-start.17 = (bf16[1,1,1,2,32,1280]{5,4,3,2,1,0:T(8,128)(2,1)S(1)}, bf16[1,1,1,2,32,1280]{5,4,3,2,1,0:T(8,128)(2,1)S(1)}, u32[]{:S(2)}, u32[]{:S(2)}) collective-permute-start(bf16[1,1,1,2,32,1280]{5,4,3,2,1,0:T(8,128)(2,1)S(1)} %slice.220), channel_id=1, source_target_pairs={{0,4},{1,3},{2,6},{3,1},{4,0},{5,7},{6,2},{7,5},{8,12},{9,11},{10,... | collective-permute-start | bytes 491528 | tf_op jit(solution)/shard_map/ppermute | solution.py:39
  95.1 1.0 collective-permute-start.21
  96.1 0.6 collective-permute-done.26
  96.7 2.2 %collective-permute-done.17 = bf16[1,1,1,2,32,1280]{5,4,3,2,1,0:T(8,128)(2,1)S(1)} collective-permute-done((bf16[1,1,1,2,32,1280]{5,4,3,2,1,0:T(8,128)(2,1)S(1)}, bf16[1,1,1,2,32,1280]{5,4,3,2,1,0:T(8,128)(2,1)S(1)}, u32[]{:S(2)}, u32[]{:S(2)}) %collective-permute-start.17) | collective-permute-done | bytes 163872 | tf_op jit(solution)/shard_map/ppermute | solution.py:39
  99.0 1.2 %collective-permute-start.18 = (bf16[1,1,1,1,32,1280]{5,4,3,2,1,0:T(8,128)(2,1)S(1)}, bf16[1,1,1,1,32,1280]{5,4,3,2,1,0:T(8,128)(2,1)S(1)}, u32[]{:S(2)}, u32[]{:S(2)}) collective-permute-start(bf16[1,1,1,1,32,1280]{5,4,3,2,1,0:T(8,128)(2,1)S(1)} %slice.222), channel_id=1, source_target_pairs={{0,16},{1,17},{2,18},{3,19},{4,20},{5,21},{6,22},{7,23},{8,24},{9,... | collective-permute-start | bytes 245768 | tf_op jit(solution)/shard_map/ppermute | solution.py:39
  100.3 0.3 collective-permute-done.21
  100.6 4.3 %collective-permute-start.22 = (bf16[1,1,1,1,32,1280]{5,4,3,2,1,0:T(8,128)(2,1)S(1)}, bf16[1,1,1,1,32,1280]{5,4,3,2,1,0:T(8,128)(2,1)S(1)}, u32[]{:S(2)}, u32[]{:S(2)}) collective-permute-start(bf16[1,1,1,1,32,1280]{5,4,3,2,1,0:T(8,128)(2,1)S(1)} %slice.228), channel_id=1, source_target_pairs={{0,16},{1,17},{2,18},{3,19},{4,20},{5,21},{6,22},{7,23},{8,24},{9,... | collective-permute-start | bytes 245768 | tf_op jit(solution)/shard_map/ppermute | solution.py:39
  105.0 1.3 %collective-permute-done.18 = bf16[1,1,1,1,32,1280]{5,4,3,2,1,0:T(8,128)(2,1)S(1)} collective-permute-done((bf16[1,1,1,1,32,1280]{5,4,3,2,1,0:T(8,128)(2,1)S(1)}, bf16[1,1,1,1,32,1280]{5,4,3,2,1,0:T(8,128)(2,1)S(1)}, u32[]{:S(2)}, u32[]{:S(2)}) %collective-permute-start.18) | collective-permute-done | bytes 81952 | tf_op jit(solution)/shard_map/ppermute | solution.py:39
  106.3 1.0 collective-permute-done.22
  107.4 0.7 pad_maximum_fusion.9
  (60 shorter events, 2.0 us)
Async XLA Ops:
  2.0 21.0 %copy-start.3 = (bf16[32,1280]{1,0:T(8,128)(2,1)S(1)}, bf16[32,1280]{1,0:T(8,128)(2,1)}, u32[]{:S(2)}) copy-start(bf16[32,1280]{1,0:T(8,128)(2,1)} %get-tuple-element.17) | copy-start | bytes 245764
  2.0 24.4 %copy-start.2 = (bf16[32,1280]{1,0:T(8,128)(2,1)S(1)}, bf16[32,1280]{1,0:T(8,128)(2,1)}, u32[]{:S(2)}) copy-start(bf16[32,1280]{1,0:T(8,128)(2,1)} %get-tuple-element.20) | copy-start | bytes 245764
  2.0 11.8 %collective-permute-start.8 = (bf16[1,1,1,1,32,1152]{5,4,3,2,1,0:T(8,128)(2,1)}, bf16[1,1,1,1,32,1152]{5,4,3,2,1,0:T(8,128)(2,1)S(1)}, u32[]{:S(2)}, u32[]{:S(2)}) collective-permute-start(bf16[1,1,1,1,32,1152]{5,4,3,2,1,0:T(8,128)(2,1)} %bitcast.75), channel_id=1, source_target_pairs={{0,16},{1,17},{2,18},{3,19},{4,20},{5,21},{6,22},{7,23},{8,24},{9,... | collective-permute-start | bytes 221192 | tf_op jit(solution)/shard_map/ppermute | solution.py:39
  6.0 9.6 %collective-permute-start = (bf16[1,1,1,1,32,1280]{5,4,3,2,1,0:T(8,128)(2,1)}, bf16[1,1,1,1,32,1280]{5,4,3,2,1,0:T(8,128)(2,1)S(1)}, u32[]{:S(2)}, u32[]{:S(2)}) collective-permute-start(bf16[1,1,1,1,32,1280]{5,4,3,2,1,0:T(8,128)(2,1)} %bitcast.84), channel_id=1, source_target_pairs={{0,16},{1,17},{2,18},{3,19},{4,20},{5,21},{6,22},{7,23},{8,24},{9,... | collective-permute-start | bytes 245768 | tf_op jit(solution)/shard_map/ppermute | solution.py:39
  6.1 12.4 %collective-permute-start.4 = (bf16[1,1,1,1,32,1280]{5,4,3,2,1,0:T(8,128)(2,1)}, bf16[1,1,1,1,32,1280]{5,4,3,2,1,0:T(8,128)(2,1)S(1)}, u32[]{:S(2)}, u32[]{:S(2)}) collective-permute-start(bf16[1,1,1,1,32,1280]{5,4,3,2,1,0:T(8,128)(2,1)} %bitcast.80), channel_id=1, source_target_pairs={{0,16},{1,17},{2,18},{3,19},{4,20},{5,21},{6,22},{7,23},{8,24},{9,... | collective-permute-start | bytes 245768 | tf_op jit(solution)/shard_map/ppermute | solution.py:39
  14.7 16.1 %copy-start.1 = (bf16[32,1152]{1,0:T(8,128)(2,1)S(1)}, bf16[32,1152]{1,0:T(8,128)(2,1)}, u32[]{:S(2)}) copy-start(bf16[32,1152]{1,0:T(8,128)(2,1)} %get-tuple-element.22) | copy-start | bytes 221188
  14.7 6.3 %collective-permute-start.9 = (bf16[1,1,1,2,32,1152]{5,4,3,2,1,0:T(8,128)(2,1)S(1)}, bf16[1,1,1,2,32,1152]{5,4,3,2,1,0:T(8,128)(2,1)S(1)}, u32[]{:S(2)}, u32[]{:S(2)}) collective-permute-start(bf16[1,1,1,2,32,1152]{5,4,3,2,1,0:T(8,128)(2,1)S(1)} %pad_maximum_fusion.12), channel_id=1, source_target_pairs={{0,8},{1,9},{2,10},{3,11},{4,12},{5,13},{6,14},{7,15},{8,0},{9,1},... | collective-permute-start | bytes 442376 | tf_op jit(solution)/shard_map/ppermute | solution.py:39
  16.5 6.5 %collective-permute-start.1 = (bf16[1,1,1,2,32,1280]{5,4,3,2,1,0:T(8,128)(2,1)S(1)}, bf16[1,1,1,2,32,1280]{5,4,3,2,1,0:T(8,128)(2,1)S(1)}, u32[]{:S(2)}, u32[]{:S(2)}) collective-permute-start(bf16[1,1,1,2,32,1280]{5,4,3,2,1,0:T(8,128)(2,1)S(1)} %pad_maximum_fusion.10), channel_id=1, source_target_pairs={{0,2},{1,5},{2,0},{3,7},{4,6},{5,1},{6,4},{7,3},{8,10},{9,13},{10,... | collective-permute-start | bytes 491528 | tf_op jit(solution)/shard_map/ppermute | solution.py:39
  19.4 6.9 %collective-permute-start.5 = (bf16[1,1,1,2,32,1280]{5,4,3,2,1,0:T(8,128)(2,1)S(1)}, bf16[1,1,1,2,32,1280]{5,4,3,2,1,0:T(8,128)(2,1)S(1)}, u32[]{:S(2)}, u32[]{:S(2)}) collective-permute-start(bf16[1,1,1,2,32,1280]{5,4,3,2,1,0:T(8,128)(2,1)S(1)} %pad_maximum_fusion.11), channel_id=1, source_target_pairs={{0,4},{1,3},{2,6},{3,1},{4,0},{5,7},{6,2},{7,5},{8,12},{9,11},{10,... | collective-permute-start | bytes 491528 | tf_op jit(solution)/shard_map/ppermute | solution.py:39
  21.9 8.9 %collective-permute-start.10 = (bf16[1,1,2,2,32,1152]{5,4,3,2,1,0:T(8,128)(2,1)S(1)}, bf16[1,1,2,2,32,1152]{5,4,3,2,1,0:T(8,128)(2,1)S(1)}, u32[]{:S(2)}, u32[]{:S(2)}) collective-permute-start(bf16[1,1,2,2,32,1152]{5,4,3,2,1,0:T(8,128)(2,1)S(1)} %pad_maximum_fusion.8), channel_id=1, source_target_pairs={{0,2},{1,5},{2,0},{3,7},{4,6},{5,1},{6,4},{7,3},{8,10},{9,13},{10,... | collective-permute-start | bytes 884744 | tf_op jit(solution)/shard_map/ppermute | solution.py:39
  23.0 10.5 %copy-start.4 = (bf16[1,3584,512]{2,1,0:T(8,128)(2,1)S(1)}, bf16[1,3584,512]{2,1,0:T(8,128)(2,1)}, u32[]{:S(2)}) copy-start(bf16[1,3584,512]{2,1,0:T(8,128)(2,1)} %param.7) | copy-start | bytes 11010052
  23.1 9.5 %collective-permute-start.2 = (bf16[2,1,1,2,32,1280]{5,4,3,2,1,0:T(8,128)(2,1)S(1)}, bf16[2,1,1,2,32,1280]{5,4,3,2,1,0:T(8,128)(2,1)S(1)}, u32[]{:S(2)}, u32[]{:S(2)}) collective-permute-start(bf16[2,1,1,2,32,1280]{5,4,3,2,1,0:T(8,128)(2,1)S(1)} %pad_maximum_fusion.6), channel_id=1, source_target_pairs={{0,4},{1,3},{2,6},{3,1},{4,0},{5,7},{6,2},{7,5},{8,12},{9,11},{10,... | collective-permute-start | bytes 983048 | tf_op jit(solution)/shard_map/ppermute | solution.py:39
  26.4 8.1 %collective-permute-start.6 = (bf16[1,2,1,2,32,1280]{5,4,3,2,1,0:T(8,128)(2,1)S(1)}, bf16[1,2,1,2,32,1280]{5,4,3,2,1,0:T(8,128)(2,1)S(1)}, u32[]{:S(2)}, u32[]{:S(2)}) collective-permute-start(bf16[1,2,1,2,32,1280]{5,4,3,2,1,0:T(8,128)(2,1)S(1)} %pad_maximum_fusion.7), channel_id=1, source_target_pairs={{0,8},{1,9},{2,10},{3,11},{4,12},{5,13},{6,14},{7,15},{8,0},{9,1},... | collective-permute-start | bytes 983048 | tf_op jit(solution)/shard_map/ppermute | solution.py:39
  30.9 14.0 %collective-permute-start.11 = (bf16[2,1,2,2,32,1152]{5,4,3,2,1,0:T(8,128)(2,1)S(1)}, bf16[2,1,2,2,32,1152]{5,4,3,2,1,0:T(8,128)(2,1)S(1)}, u32[]{:S(2)}, u32[]{:S(2)}) collective-permute-start(bf16[2,1,2,2,32,1152]{5,4,3,2,1,0:T(8,128)(2,1)S(1)} %pad_maximum_fusion.5), channel_id=1, source_target_pairs={{0,4},{1,3},{2,6},{3,1},{4,0},{5,7},{6,2},{7,5},{8,12},{9,11},{10,... | collective-permute-start | bytes 1769480 | tf_op jit(solution)/shard_map/ppermute | solution.py:39
  32.6 14.9 %collective-permute-start.3 = (bf16[2,2,1,2,32,1280]{5,4,3,2,1,0:T(8,128)(2,1)S(1)}, bf16[2,2,1,2,32,1280]{5,4,3,2,1,0:T(8,128)(2,1)S(1)}, u32[]{:S(2)}, u32[]{:S(2)}) collective-permute-start(bf16[2,2,1,2,32,1280]{5,4,3,2,1,0:T(8,128)(2,1)S(1)} %pad_maximum_fusion.3), channel_id=1, source_target_pairs={{0,8},{1,9},{2,10},{3,11},{4,12},{5,13},{6,14},{7,15},{8,0},{9,1},... | collective-permute-start | bytes 1966088 | tf_op jit(solution)/shard_map/ppermute | solution.py:39
  33.5 23.0 %collective-permute-start.12 = (bf16[3584,512]{1,0:T(8,128)(2,1)S(1)}, bf16[3584,512]{1,0:T(8,128)(2,1)S(1)}, u32[]{:S(2)}, u32[]{:S(2)}) collective-permute-start(bf16[3584,512]{1,0:T(8,128)(2,1)S(1)} %bitcast.90), channel_id=1, source_target_pairs={{0,1},{1,0},{2,3},{3,2},{4,5},{5,4},{6,7},{7,6},{8,9},{9,8},{10,11... | collective-permute-start | bytes 11010056 | tf_op jit(solution)/shard_map/ppermute | solution.py:43
  34.5 13.3 %collective-permute-start.7 = (bf16[1,2,2,2,32,1280]{5,4,3,2,1,0:T(8,128)(2,1)S(1)}, bf16[1,2,2,2,32,1280]{5,4,3,2,1,0:T(8,128)(2,1)S(1)}, u32[]{:S(2)}, u32[]{:S(2)}) collective-permute-start(bf16[1,2,2,2,32,1280]{5,4,3,2,1,0:T(8,128)(2,1)S(1)} %pad_maximum_fusion.4), channel_id=1, source_target_pairs={{0,2},{1,5},{2,0},{3,7},{4,6},{5,1},{6,4},{7,3},{8,10},{9,13},{10,... | collective-permute-start | bytes 1966088 | tf_op jit(solution)/shard_map/ppermute | solution.py:39
  36.5 20.7 %collective-permute-start.13 = (bf16[3584,512]{1,0:T(8,128)(2,1)}, bf16[3584,512]{1,0:T(8,128)(2,1)S(1)}, u32[]{:S(2)}, u32[]{:S(2)}) collective-permute-start(bf16[3584,512]{1,0:T(8,128)(2,1)} %bitcast.91), channel_id=1, source_target_pairs={{0,1},{1,0},{2,3},{3,2},{4,5},{5,4},{6,7},{7,6},{8,9},{9,8},{10,11... | collective-permute-start | bytes 11010056 | tf_op jit(solution)/shard_map/ppermute | solution.py:43
  44.9 2.9 %copy-start = (bf16[1,512,3584]{2,1,0:T(8,128)(2,1)S(1)}, bf16[1,512,3584]{2,1,0:T(8,128)(2,1)}, u32[]{:S(2)}) copy-start(bf16[1,512,3584]{2,1,0:T(8,128)(2,1)} %param.9) | copy-start | bytes 11010052
  47.7 13.8 %collective-permute-start.14 = (bf16[512,3584]{1,0:T(8,128)(2,1)S(1)}, bf16[512,3584]{1,0:T(8,128)(2,1)S(1)}, u32[]{:S(2)}, u32[]{:S(2)}) collective-permute-start(bf16[512,3584]{1,0:T(8,128)(2,1)S(1)} %bitcast.62), channel_id=1, source_target_pairs={{0,1},{1,0},{2,3},{3,2},{4,5},{5,4},{6,7},{7,6},{8,9},{9,8},{10,11... | collective-permute-start | bytes 11010056 | tf_op jit(solution)/shard_map/ppermute | solution.py:43
  48.0 2.0 %copy-start.5 = (bf16[1,3584,512]{2,1,0:T(8,128)(2,1)S(1)}, bf16[1,3584,512]{2,1,0:T(8,128)(2,1)}, u32[]{:S(2)}) copy-start(bf16[1,3584,512]{2,1,0:T(8,128)(2,1)} %param.8) | copy-start | bytes 11010052
  64.1 14.4 %collective-permute-start.23 = (bf16[2,2,1,2,32,1024]{5,4,3,2,1,0:T(8,128)(2,1)S(1)}, bf16[2,2,1,2,32,1024]{5,4,3,2,1,0:T(8,128)(2,1)S(1)}, u32[]{:S(2)}, u32[]{:S(2)}) collective-permute-start(bf16[2,2,1,2,32,1024]{5,4,3,2,1,0:T(8,128)(2,1)S(1)} %slice.196), channel_id=1, source_target_pairs={{0,8},{1,9},{2,10},{3,11},{4,12},{5,13},{6,14},{7,15},{8,0},{9,1},... | collective-permute-start | bytes 1572872 | tf_op jit(solution)/shard_map/ppermute | solution.py:39
  65.6 17.2 %collective-permute-start.15 = (bf16[1,2,2,2,32,1280]{5,4,3,2,1,0:T(8,128)(2,1)S(1)}, bf16[1,2,2,2,32,1280]{5,4,3,2,1,0:T(8,128)(2,1)S(1)}, u32[]{:S(2)}, u32[]{:S(2)}) collective-permute-start(bf16[1,2,2,2,32,1280]{5,4,3,2,1,0:T(8,128)(2,1)S(1)} %slice.180), channel_id=1, source_target_pairs={{0,2},{1,5},{2,0},{3,7},{4,6},{5,1},{6,4},{7,3},{8,10},{9,13},{10,... | collective-permute-start | bytes 1966088 | tf_op jit(solution)/shard_map/ppermute | solution.py:39
  67.4 19.8 %collective-permute-start.19 = (bf16[2,1,2,2,32,1280]{5,4,3,2,1,0:T(8,128)(2,1)S(1)}, bf16[2,1,2,2,32,1280]{5,4,3,2,1,0:T(8,128)(2,1)S(1)}, u32[]{:S(2)}, u32[]{:S(2)}) collective-permute-start(bf16[2,1,2,2,32,1280]{5,4,3,2,1,0:T(8,128)(2,1)S(1)} %slice.188), channel_id=1, source_target_pairs={{0,4},{1,3},{2,6},{3,1},{4,0},{5,7},{6,2},{7,5},{8,12},{9,11},{10,... | collective-permute-start | bytes 1966088 | tf_op jit(solution)/shard_map/ppermute | solution.py:39
  78.7 6.7 %collective-permute-start.24 = (bf16[2,1,1,2,32,1024]{5,4,3,2,1,0:T(8,128)(2,1)S(1)}, bf16[2,1,1,2,32,1024]{5,4,3,2,1,0:T(8,128)(2,1)S(1)}, u32[]{:S(2)}, u32[]{:S(2)}) collective-permute-start(bf16[2,1,1,2,32,1024]{5,4,3,2,1,0:T(8,128)(2,1)S(1)} %slice.230), channel_id=1, source_target_pairs={{0,4},{1,3},{2,6},{3,1},{4,0},{5,7},{6,2},{7,5},{8,12},{9,11},{10,... | collective-permute-start | bytes 786440 | tf_op jit(solution)/shard_map/ppermute | solution.py:39
  83.1 10.4 %collective-permute-start.16 = (bf16[1,2,1,2,32,1280]{5,4,3,2,1,0:T(8,128)(2,1)S(1)}, bf16[1,2,1,2,32,1280]{5,4,3,2,1,0:T(8,128)(2,1)S(1)}, u32[]{:S(2)}, u32[]{:S(2)}) collective-permute-start(bf16[1,2,1,2,32,1280]{5,4,3,2,1,0:T(8,128)(2,1)S(1)} %slice.218), channel_id=1, source_target_pairs={{0,8},{1,9},{2,10},{3,11},{4,12},{5,13},{6,14},{7,15},{8,0},{9,1},... | collective-permute-start | bytes 983048 | tf_op jit(solution)/shard_map/ppermute | solution.py:39
  85.5 5.0 %collective-permute-start.25 = (bf16[1,1,1,2,32,1024]{5,4,3,2,1,0:T(8,128)(2,1)S(1)}, bf16[1,1,1,2,32,1024]{5,4,3,2,1,0:T(8,128)(2,1)S(1)}, u32[]{:S(2)}, u32[]{:S(2)}) collective-permute-start(bf16[1,1,1,2,32,1024]{5,4,3,2,1,0:T(8,128)(2,1)S(1)} %slice.232), channel_id=1, source_target_pairs={{0,2},{1,5},{2,0},{3,7},{4,6},{5,1},{6,4},{7,3},{8,10},{9,13},{10,... | collective-permute-start | bytes 393224 | tf_op jit(solution)/shard_map/ppermute | solution.py:39
  87.4 7.6 %collective-permute-start.20 = (bf16[1,1,2,2,32,1280]{5,4,3,2,1,0:T(8,128)(2,1)S(1)}, bf16[1,1,2,2,32,1280]{5,4,3,2,1,0:T(8,128)(2,1)S(1)}, u32[]{:S(2)}, u32[]{:S(2)}) collective-permute-start(bf16[1,1,2,2,32,1280]{5,4,3,2,1,0:T(8,128)(2,1)S(1)} %slice.224), channel_id=1, source_target_pairs={{0,2},{1,5},{2,0},{3,7},{4,6},{5,1},{6,4},{7,3},{8,10},{9,13},{10,... | collective-permute-start | bytes 983048 | tf_op jit(solution)/shard_map/ppermute | solution.py:39
  90.5 6.2 %collective-permute-start.26 = (bf16[1,1,1,1,32,1024]{5,4,3,2,1,0:T(8,128)(2,1)S(1)}, bf16[1,1,1,1,32,1024]{5,4,3,2,1,0:T(8,128)(2,1)S(1)}, u32[]{:S(2)}, u32[]{:S(2)}) collective-permute-start(bf16[1,1,1,1,32,1024]{5,4,3,2,1,0:T(8,128)(2,1)S(1)} %slice.234), channel_id=1, source_target_pairs={{0,16},{1,17},{2,18},{3,19},{4,20},{5,21},{6,22},{7,23},{8,24},{9,... | collective-permute-start | bytes 196616 | tf_op jit(solution)/shard_map/ppermute | solution.py:39
  93.6 5.4 %collective-permute-start.17 = (bf16[1,1,1,2,32,1280]{5,4,3,2,1,0:T(8,128)(2,1)S(1)}, bf16[1,1,1,2,32,1280]{5,4,3,2,1,0:T(8,128)(2,1)S(1)}, u32[]{:S(2)}, u32[]{:S(2)}) collective-permute-start(bf16[1,1,1,2,32,1280]{5,4,3,2,1,0:T(8,128)(2,1)S(1)} %slice.220), channel_id=1, source_target_pairs={{0,4},{1,3},{2,6},{3,1},{4,0},{5,7},{6,2},{7,5},{8,12},{9,11},{10,... | collective-permute-start | bytes 491528 | tf_op jit(solution)/shard_map/ppermute | solution.py:39
  95.1 5.5 %collective-permute-start.21 = (bf16[1,1,1,2,32,1280]{5,4,3,2,1,0:T(8,128)(2,1)S(1)}, bf16[1,1,1,2,32,1280]{5,4,3,2,1,0:T(8,128)(2,1)S(1)}, u32[]{:S(2)}, u32[]{:S(2)}) collective-permute-start(bf16[1,1,1,2,32,1280]{5,4,3,2,1,0:T(8,128)(2,1)S(1)} %slice.226), channel_id=1, source_target_pairs={{0,8},{1,9},{2,10},{3,11},{4,12},{5,13},{6,14},{7,15},{8,0},{9,1},... | collective-permute-start | bytes 491528 | tf_op jit(solution)/shard_map/ppermute | solution.py:39
  99.0 7.3 %collective-permute-start.18 = (bf16[1,1,1,1,32,1280]{5,4,3,2,1,0:T(8,128)(2,1)S(1)}, bf16[1,1,1,1,32,1280]{5,4,3,2,1,0:T(8,128)(2,1)S(1)}, u32[]{:S(2)}, u32[]{:S(2)}) collective-permute-start(bf16[1,1,1,1,32,1280]{5,4,3,2,1,0:T(8,128)(2,1)S(1)} %slice.222), channel_id=1, source_target_pairs={{0,16},{1,17},{2,18},{3,19},{4,20},{5,21},{6,22},{7,23},{8,24},{9,... | collective-permute-start | bytes 245768 | tf_op jit(solution)/shard_map/ppermute | solution.py:39
  100.6 6.8 %collective-permute-start.22 = (bf16[1,1,1,1,32,1280]{5,4,3,2,1,0:T(8,128)(2,1)S(1)}, bf16[1,1,1,1,32,1280]{5,4,3,2,1,0:T(8,128)(2,1)S(1)}, u32[]{:S(2)}, u32[]{:S(2)}) collective-permute-start(bf16[1,1,1,1,32,1280]{5,4,3,2,1,0:T(8,128)(2,1)S(1)} %slice.228), channel_id=1, source_target_pairs={{0,16},{1,17},{2,18},{3,19},{4,20},{5,21},{6,22},{7,23},{8,24},{9,... | collective-permute-start | bytes 245768 | tf_op jit(solution)/shard_map/ppermute | solution.py:39
